TPU v7x, 128 devices: a whole 4x4x4 slice. The times are simulated.
128 devices in a mesh: dp: 32 (over z, x, y_lo), mp: 4 (over y_hi, core).
Axes of the slice: x: 4, y: 4 (y_hi: 2, y_lo: 2; y = y_hi * 2 + y_lo), z: 4, core: 2. Of those that a mesh axis runs over, the one named last changes fastest.
Arguments:
- vision_layer_entry: bfloat16 [16384, 1024], P('dp'), may hold values from -6 to 6
- latent_preact_values: bfloat16 [16384, 4096], P('dp', 'mp'), may hold values from -6 to 6
- final_layer_result: bfloat16 [16384, 1024], P('dp'), may hold values from -6 to 6
- caption_vectors_raw: bfloat16 [16384, 1024], P(('dp', 'mp')), may hold values from -0.19921875 to 0.19921875
- sharpness_factor: float32 [1], replicated, may hold values from 8 to 20
- offset_term: float32 [1], replicated, may hold values from -10 to -4
- first_feedforward_matrix: bfloat16 [1024, 4096], P(None, 'mp'), may hold values from -0.1875 to 0.1875
- second_feedforward_matrix: bfloat16 [4096, 1024], P('mp'), may hold values from -0.09375 to 0.09375
- mapper_matrix: bfloat16 [1024, 1024], P(None, 'mp'), may hold values from -0.1875 to 0.1875
- first_matrix_velocity: bfloat16 [1024, 4096], P(None, 'mp'), may hold values from -6 to 6
- second_matrix_velocity: bfloat16 [4096, 1024], P('mp'), may hold values from -6 to 6
- mapper_velocity: bfloat16 [1024, 1024], P(None, 'mp'), may hold values from -6 to 6
Outputs:
- update_up: bfloat16 [1024, 4096], P(None, 'mp')
- update_down: bfloat16 [4096, 1024], P('mp')
- update_proj: bfloat16 [1024, 1024], P(None, 'mp')
- renewed_up: bfloat16 [1024, 4096], P(None, 'mp')
- renewed_down: bfloat16 [4096, 1024], P('mp')
- renewed_proj: bfloat16 [1024, 1024], P(None, 'mp')
- text_grad: float32 [16384, 1024], P(('dp', 'mp'))
All inputs are finite; a program needn't handle non-finite values.
Results may differ from a plain program's by a relative error of at most 0.02.
Values may be sent and summed in bfloat16 or wider, within the bound.
A program may use at most 128 MiB of HBM per device.

v0:
```python
import jax
import jax.numpy as jnp
from jax import lax
from jax.sharding import PartitionSpec as P


def passed_along(block, axis, distance):
    devices = range(lax.axis_size(axis))
    route = [((i - distance) % len(devices), i) for i in devices]
    return lax.ppermute(block, axis, route)


def unit_rows(values):
    factor = lax.rsqrt(jnp.sum(values * values, axis=1, keepdims=True) + 1e-06)
    return (values * factor, factor)


def couple_derivs(vision_members, caption_members, matched_flag, similarity_scaling, offset_amount):
    similarity_grade = lax.dot_general(
        vision_members,
        caption_members,
        (((1,), (1,)), ((), ())),
        preferred_element_type=jnp.float32,
    )
    raw_similarity = similarity_scaling * similarity_grade + offset_amount
    label = jnp.where(matched_flag, 1.0, -1.0).astype(jnp.float32)
    gradient_ratio = -label * jax.nn.sigmoid(-label * raw_similarity)
    return (similarity_scaling * gradient_ratio).astype(jnp.bfloat16)


def lion_step(weight, moment, grad, axis):
    moment_wide = moment.astype(jnp.float32)
    blend = 0.9 * moment_wide + 0.1 * grad
    spread = jnp.sqrt(jnp.mean(blend * blend, axis=axis, keepdims=True) + 1e-06)
    soft = blend / jnp.sqrt(blend * blend + 0.25 * spread * (0.25 * spread))
    update = (soft + 1.0 * weight.astype(jnp.float32)).astype(jnp.bfloat16)
    renewed = (0.99 * moment_wide + 0.01 * grad).astype(jnp.bfloat16)
    return (update, renewed)


def contract_rows(left, right):
    return lax.dot_general(
        left, right, (((0,), (0,)), ((), ())), preferred_element_type=jnp.float32
    )


def contract_cols(left, right):
    return lax.dot_general(
        left, right, (((1,), (1,)), ((), ())), preferred_element_type=jnp.float32
    )


def per_device(
    vision_layer_entry,
    latent_preact_values,
    final_layer_result,
    caption_vectors_raw,
    sharpness_factor,
    offset_term,
    first_feedforward_matrix,
    second_feedforward_matrix,
    mapper_matrix,
    first_matrix_velocity,
    second_matrix_velocity,
    mapper_velocity,
):
    similarity_scaling = sharpness_factor[0]
    offset_amount = offset_term[0]
    group_rows = final_layer_result.shape[0]
    text_rows = caption_vectors_raw.shape[0]
    column_width = mapper_matrix.shape[1]
    column = lax.axis_index("mp")
    cycle_size = lax.axis_size("dp")
    embedded = jnp.dot(
        final_layer_result, mapper_matrix, preferred_element_type=jnp.float32
    ).astype(jnp.bfloat16)
    gathered = lax.all_gather(embedded, "mp", axis=1, tiled=True)
    full_width = gathered.shape[1]
    vision_members, image_scale = unit_rows(gathered.astype(jnp.float32))
    vision_reduced = vision_members.astype(jnp.bfloat16)
    caption_members, text_scale = unit_rows(caption_vectors_raw.astype(jnp.float32))
    caption_reduced = caption_members.astype(jnp.bfloat16)
    row_index = jnp.arange(group_rows, dtype=jnp.int32)
    own_slots = column * text_rows + jnp.arange(text_rows, dtype=jnp.int32)

    def advance(turn, carry):
        traversal_agent, text_acc, image_dz = carry
        matched_flag = (turn == 0) & (row_index[:, None] == own_slots[None, :])
        parameter_tensors = couple_derivs(
            vision_reduced, traversal_agent, matched_flag, similarity_scaling, offset_amount
        )
        image_dz = image_dz + jnp.dot(
            parameter_tensors, traversal_agent, preferred_element_type=jnp.float32
        )
        text_acc = text_acc + contract_rows(parameter_tensors, vision_reduced)
        traversal_agent, text_acc = (
            passed_along(traversal_agent.astype(jnp.float32), "dp", 1).astype(
                traversal_agent.dtype
            ),
            passed_along(text_acc, "dp", 1),
        )
        return (traversal_agent, text_acc, image_dz)

    start_state = (
        caption_reduced,
        jnp.zeros((text_rows, full_width), jnp.float32),
        jnp.zeros((group_rows, full_width), jnp.float32),
    )
    traversal_agent, text_acc, image_dz = lax.fori_loop(0, cycle_size, advance, start_state)
    text_grad = text_scale * (
        text_acc - caption_members * jnp.sum(caption_members * text_acc, axis=1, keepdims=True)
    )
    column_start = column * column_width
    summed = lax.psum(image_dz, "mp")
    full_grad = image_scale * (
        summed - vision_members * jnp.sum(vision_members * summed, axis=1, keepdims=True)
    )
    image_grad = lax.dynamic_slice_in_dim(full_grad, column_start, column_width, 1)
    image_grad = image_grad.astype(jnp.bfloat16)
    grad_proj = contract_rows(final_layer_result, image_grad)
    back = lax.psum(contract_cols(image_grad, mapper_matrix).astype(jnp.bfloat16), "mp")
    active, gelu_back = jax.vjp(jax.nn.gelu, latent_preact_values.astype(jnp.float32))
    grad_down = contract_rows(active.astype(jnp.bfloat16), back)
    inner = contract_cols(back, second_feedforward_matrix)
    pre_grad = gelu_back(inner)[0].astype(jnp.bfloat16)
    grad_up = contract_rows(vision_layer_entry, pre_grad)
    grad_up, grad_down, grad_proj = (
        lax.psum(grad_up.astype(jnp.bfloat16), "dp").astype(jnp.float32),
        lax.psum(grad_down.astype(jnp.bfloat16), "dp").astype(jnp.float32),
        lax.psum(grad_proj.astype(jnp.bfloat16), "dp").astype(jnp.float32),
    )
    update_up, renewed_up = lion_step(first_feedforward_matrix, first_matrix_velocity, grad_up, 0)
    update_down, renewed_down = lion_step(
        second_feedforward_matrix, second_matrix_velocity, grad_down, 1
    )
    update_proj, renewed_proj = lion_step(mapper_matrix, mapper_velocity, grad_proj, 0)
    return (update_up, update_down, update_proj, renewed_up, renewed_down, renewed_proj, text_grad)


def solution(mesh):
    return jax.shard_map(
        per_device,
        mesh=mesh,
        in_specs=(
            P("dp", None),
            P("dp", "mp"),
            P("dp", None),
            P(("dp", "mp"), None),
            P(),
            P(),
            P(None, "mp"),
            P("mp", None),
            P(None, "mp"),
            P(None, "mp"),
            P("mp", None),
            P(None, "mp"),
        ),
        out_specs=(
            P(None, "mp"),
            P("mp", None),
            P(None, "mp"),
            P(None, "mp"),
            P("mp", None),
            P(None, "mp"),
            P(("dp", "mp"), None),
        ),
        check_vma=False,
    )
```

profile of v0, /device:TPU:0, one launch (start us, length us, event | category | flops | bytes accessed | tf_op | source)
XLA Modules:
  0.0 1360.6 jit_solution(13454578069865504633)
XLA Ops:
  10.9 22.8 %all-gather.2.cloned.1.call-done = bf16[512,1024]{1,0:T(8,128)(2,1)} async-done(((bf16[512,256]{1,0:T(8,128)(2,1)}), bf16[512,1024]{1,0:T(8,128)(2,1)}) %all-gather.2.cloned.1.call-update) | async-done | bytes 1048592 | tf_op jit(solution)/shard_map/all_gather | solution.py:77
  38.4 834.2 %while.18 = (s32[]{:T(128)}, bf16[128,1024]{1,0:T(8,128)(2,1)}, f32[128,1024]{1,0:T(8,128)}, f32[512,1024]{1,0:T(8,128)S(1)}, f32[]{:T(128)}, /*index=5*/bf16[51...) while((s32[]{:T(128)}, bf16[128,1024]{1,0:T(8,128)(2,1)}, ...), condition=%wide.region_3.4_spmd.clone, body=%wide.region_2.3_spmd.clone.sunk | while | flops 404684928 | bytes 16123112 | solution.py:109
  48.3 20.6 %collective-permute-done = bf16[128,1024]{1,0:T(8,128)(2,1)} collective-permute-done((bf16[128,1024]{1,0:T(8,128)(2,1)S(1)}, bf16[128,1024]{1,0:T(8,128)(2,1)}, u32[]{:S(2)}, u32[]{:S(2)}) %collective-permute-start) | collective-permute-done | bytes 262176 | tf_op jit(solution)/shard_map/while/body/eval_jaxpr/ppermute | solution.py:10
  75.8 22.7 %collective-permute-done = bf16[128,1024]{1,0:T(8,128)(2,1)} collective-permute-done((bf16[128,1024]{1,0:T(8,128)(2,1)S(1)}, bf16[128,1024]{1,0:T(8,128)(2,1)}, u32[]{:S(2)}, u32[]{:S(2)}) %collective-permute-start) | collective-permute-done | bytes 262176 | tf_op jit(solution)/shard_map/while/body/eval_jaxpr/ppermute | solution.py:10
  105.4 21.8 %collective-permute-done = bf16[128,1024]{1,0:T(8,128)(2,1)} collective-permute-done((bf16[128,1024]{1,0:T(8,128)(2,1)S(1)}, bf16[128,1024]{1,0:T(8,128)(2,1)}, u32[]{:S(2)}, u32[]{:S(2)}) %collective-permute-start) | collective-permute-done | bytes 262176 | tf_op jit(solution)/shard_map/while/body/eval_jaxpr/ppermute | solution.py:10
  134.1 20.9 %collective-permute-done = bf16[128,1024]{1,0:T(8,128)(2,1)} collective-permute-done((bf16[128,1024]{1,0:T(8,128)(2,1)S(1)}, bf16[128,1024]{1,0:T(8,128)(2,1)}, u32[]{:S(2)}, u32[]{:S(2)}) %collective-permute-start) | collective-permute-done | bytes 262176 | tf_op jit(solution)/shard_map/while/body/eval_jaxpr/ppermute | solution.py:10
  161.9 19.9 %collective-permute-done = bf16[128,1024]{1,0:T(8,128)(2,1)} collective-permute-done((bf16[128,1024]{1,0:T(8,128)(2,1)S(1)}, bf16[128,1024]{1,0:T(8,128)(2,1)}, u32[]{:S(2)}, u32[]{:S(2)}) %collective-permute-start) | collective-permute-done | bytes 262176 | tf_op jit(solution)/shard_map/while/body/eval_jaxpr/ppermute | solution.py:10
  188.8 19.0 %collective-permute-done = bf16[128,1024]{1,0:T(8,128)(2,1)} collective-permute-done((bf16[128,1024]{1,0:T(8,128)(2,1)S(1)}, bf16[128,1024]{1,0:T(8,128)(2,1)}, u32[]{:S(2)}, u32[]{:S(2)}) %collective-permute-start) | collective-permute-done | bytes 262176 | tf_op jit(solution)/shard_map/while/body/eval_jaxpr/ppermute | solution.py:10
  214.7 18.1 %collective-permute-done = bf16[128,1024]{1,0:T(8,128)(2,1)} collective-permute-done((bf16[128,1024]{1,0:T(8,128)(2,1)S(1)}, bf16[128,1024]{1,0:T(8,128)(2,1)}, u32[]{:S(2)}, u32[]{:S(2)}) %collective-permute-start) | collective-permute-done | bytes 262176 | tf_op jit(solution)/shard_map/while/body/eval_jaxpr/ppermute | solution.py:10
  239.7 17.2 %collective-permute-done = bf16[128,1024]{1,0:T(8,128)(2,1)} collective-permute-done((bf16[128,1024]{1,0:T(8,128)(2,1)S(1)}, bf16[128,1024]{1,0:T(8,128)(2,1)}, u32[]{:S(2)}, u32[]{:S(2)}) %collective-permute-start) | collective-permute-done | bytes 262176 | tf_op jit(solution)/shard_map/while/body/eval_jaxpr/ppermute | solution.py:10
  263.8 16.2 %collective-permute-done = bf16[128,1024]{1,0:T(8,128)(2,1)} collective-permute-done((bf16[128,1024]{1,0:T(8,128)(2,1)S(1)}, bf16[128,1024]{1,0:T(8,128)(2,1)}, u32[]{:S(2)}, u32[]{:S(2)}) %collective-permute-start) | collective-permute-done | bytes 262176 | tf_op jit(solution)/shard_map/while/body/eval_jaxpr/ppermute | solution.py:10
  287.0 15.8 %collective-permute-done = bf16[128,1024]{1,0:T(8,128)(2,1)} collective-permute-done((bf16[128,1024]{1,0:T(8,128)(2,1)S(1)}, bf16[128,1024]{1,0:T(8,128)(2,1)}, u32[]{:S(2)}, u32[]{:S(2)}) %collective-permute-start) | collective-permute-done | bytes 262176 | tf_op jit(solution)/shard_map/while/body/eval_jaxpr/ppermute | solution.py:10
  309.7 15.8 %collective-permute-done = bf16[128,1024]{1,0:T(8,128)(2,1)} collective-permute-done((bf16[128,1024]{1,0:T(8,128)(2,1)S(1)}, bf16[128,1024]{1,0:T(8,128)(2,1)}, u32[]{:S(2)}, u32[]{:S(2)}) %collective-permute-start) | collective-permute-done | bytes 262176 | tf_op jit(solution)/shard_map/while/body/eval_jaxpr/ppermute | solution.py:10
  332.5 15.8 %collective-permute-done = bf16[128,1024]{1,0:T(8,128)(2,1)} collective-permute-done((bf16[128,1024]{1,0:T(8,128)(2,1)S(1)}, bf16[128,1024]{1,0:T(8,128)(2,1)}, u32[]{:S(2)}, u32[]{:S(2)}) %collective-permute-start) | collective-permute-done | bytes 262176 | tf_op jit(solution)/shard_map/while/body/eval_jaxpr/ppermute | solution.py:10
  355.2 15.8 %collective-permute-done = bf16[128,1024]{1,0:T(8,128)(2,1)} collective-permute-done((bf16[128,1024]{1,0:T(8,128)(2,1)S(1)}, bf16[128,1024]{1,0:T(8,128)(2,1)}, u32[]{:S(2)}, u32[]{:S(2)}) %collective-permute-start) | collective-permute-done | bytes 262176 | tf_op jit(solution)/shard_map/while/body/eval_jaxpr/ppermute | solution.py:10
  377.9 16.1 %collective-permute-done = bf16[128,1024]{1,0:T(8,128)(2,1)} collective-permute-done((bf16[128,1024]{1,0:T(8,128)(2,1)S(1)}, bf16[128,1024]{1,0:T(8,128)(2,1)}, u32[]{:S(2)}, u32[]{:S(2)}) %collective-permute-start) | collective-permute-done | bytes 262176 | tf_op jit(solution)/shard_map/while/body/eval_jaxpr/ppermute | solution.py:10
  401.0 17.2 %collective-permute-done = bf16[128,1024]{1,0:T(8,128)(2,1)} collective-permute-done((bf16[128,1024]{1,0:T(8,128)(2,1)S(1)}, bf16[128,1024]{1,0:T(8,128)(2,1)}, u32[]{:S(2)}, u32[]{:S(2)}) %collective-permute-start) | collective-permute-done | bytes 262176 | tf_op jit(solution)/shard_map/while/body/eval_jaxpr/ppermute | solution.py:10
  425.1 18.3 %collective-permute-done = bf16[128,1024]{1,0:T(8,128)(2,1)} collective-permute-done((bf16[128,1024]{1,0:T(8,128)(2,1)S(1)}, bf16[128,1024]{1,0:T(8,128)(2,1)}, u32[]{:S(2)}, u32[]{:S(2)}) %collective-permute-start) | collective-permute-done | bytes 262176 | tf_op jit(solution)/shard_map/while/body/eval_jaxpr/ppermute | solution.py:10
  450.3 19.4 %collective-permute-done = bf16[128,1024]{1,0:T(8,128)(2,1)} collective-permute-done((bf16[128,1024]{1,0:T(8,128)(2,1)S(1)}, bf16[128,1024]{1,0:T(8,128)(2,1)}, u32[]{:S(2)}, u32[]{:S(2)}) %collective-permute-start) | collective-permute-done | bytes 262176 | tf_op jit(solution)/shard_map/while/body/eval_jaxpr/ppermute | solution.py:10
  476.6 20.4 %collective-permute-done = bf16[128,1024]{1,0:T(8,128)(2,1)} collective-permute-done((bf16[128,1024]{1,0:T(8,128)(2,1)S(1)}, bf16[128,1024]{1,0:T(8,128)(2,1)}, u32[]{:S(2)}, u32[]{:S(2)}) %collective-permute-start) | collective-permute-done | bytes 262176 | tf_op jit(solution)/shard_map/while/body/eval_jaxpr/ppermute | solution.py:10
  503.9 21.5 %collective-permute-done = bf16[128,1024]{1,0:T(8,128)(2,1)} collective-permute-done((bf16[128,1024]{1,0:T(8,128)(2,1)S(1)}, bf16[128,1024]{1,0:T(8,128)(2,1)}, u32[]{:S(2)}, u32[]{:S(2)}) %collective-permute-start) | collective-permute-done | bytes 262176 | tf_op jit(solution)/shard_map/while/body/eval_jaxpr/ppermute | solution.py:10
  532.4 22.6 %collective-permute-done = bf16[128,1024]{1,0:T(8,128)(2,1)} collective-permute-done((bf16[128,1024]{1,0:T(8,128)(2,1)S(1)}, bf16[128,1024]{1,0:T(8,128)(2,1)}, u32[]{:S(2)}, u32[]{:S(2)}) %collective-permute-start) | collective-permute-done | bytes 262176 | tf_op jit(solution)/shard_map/while/body/eval_jaxpr/ppermute | solution.py:10
  561.9 23.8 %collective-permute-done = bf16[128,1024]{1,0:T(8,128)(2,1)} collective-permute-done((bf16[128,1024]{1,0:T(8,128)(2,1)S(1)}, bf16[128,1024]{1,0:T(8,128)(2,1)}, u32[]{:S(2)}, u32[]{:S(2)}) %collective-permute-start) | collective-permute-done | bytes 262176 | tf_op jit(solution)/shard_map/while/body/eval_jaxpr/ppermute | solution.py:10
  592.7 23.5 %collective-permute-done = bf16[128,1024]{1,0:T(8,128)(2,1)} collective-permute-done((bf16[128,1024]{1,0:T(8,128)(2,1)S(1)}, bf16[128,1024]{1,0:T(8,128)(2,1)}, u32[]{:S(2)}, u32[]{:S(2)}) %collective-permute-start) | collective-permute-done | bytes 262176 | tf_op jit(solution)/shard_map/while/body/eval_jaxpr/ppermute | solution.py:10
  623.1 22.7 %collective-permute-done = bf16[128,1024]{1,0:T(8,128)(2,1)} collective-permute-done((bf16[128,1024]{1,0:T(8,128)(2,1)S(1)}, bf16[128,1024]{1,0:T(8,128)(2,1)}, u32[]{:S(2)}, u32[]{:S(2)}) %collective-permute-start) | collective-permute-done | bytes 262176 | tf_op jit(solution)/shard_map/while/body/eval_jaxpr/ppermute | solution.py:10
  652.7 21.7 %collective-permute-done = bf16[128,1024]{1,0:T(8,128)(2,1)} collective-permute-done((bf16[128,1024]{1,0:T(8,128)(2,1)S(1)}, bf16[128,1024]{1,0:T(8,128)(2,1)}, u32[]{:S(2)}, u32[]{:S(2)}) %collective-permute-start) | collective-permute-done | bytes 262176 | tf_op jit(solution)/shard_map/while/body/eval_jaxpr/ppermute | solution.py:10
  681.4 20.8 %collective-permute-done = bf16[128,1024]{1,0:T(8,128)(2,1)} collective-permute-done((bf16[128,1024]{1,0:T(8,128)(2,1)S(1)}, bf16[128,1024]{1,0:T(8,128)(2,1)}, u32[]{:S(2)}, u32[]{:S(2)}) %collective-permute-start) | collective-permute-done | bytes 262176 | tf_op jit(solution)/shard_map/while/body/eval_jaxpr/ppermute | solution.py:10
  709.1 19.9 %collective-permute-done = bf16[128,1024]{1,0:T(8,128)(2,1)} collective-permute-done((bf16[128,1024]{1,0:T(8,128)(2,1)S(1)}, bf16[128,1024]{1,0:T(8,128)(2,1)}, u32[]{:S(2)}, u32[]{:S(2)}) %collective-permute-start) | collective-permute-done | bytes 262176 | tf_op jit(solution)/shard_map/while/body/eval_jaxpr/ppermute | solution.py:10
  736.0 19.0 %collective-permute-done = bf16[128,1024]{1,0:T(8,128)(2,1)} collective-permute-done((bf16[128,1024]{1,0:T(8,128)(2,1)S(1)}, bf16[128,1024]{1,0:T(8,128)(2,1)}, u32[]{:S(2)}, u32[]{:S(2)}) %collective-permute-start) | collective-permute-done | bytes 262176 | tf_op jit(solution)/shard_map/while/body/eval_jaxpr/ppermute | solution.py:10
  761.9 18.1 %collective-permute-done = bf16[128,1024]{1,0:T(8,128)(2,1)} collective-permute-done((bf16[128,1024]{1,0:T(8,128)(2,1)S(1)}, bf16[128,1024]{1,0:T(8,128)(2,1)}, u32[]{:S(2)}, u32[]{:S(2)}) %collective-permute-start) | collective-permute-done | bytes 262176 | tf_op jit(solution)/shard_map/while/body/eval_jaxpr/ppermute | solution.py:10
  786.9 17.1 %collective-permute-done = bf16[128,1024]{1,0:T(8,128)(2,1)} collective-permute-done((bf16[128,1024]{1,0:T(8,128)(2,1)S(1)}, bf16[128,1024]{1,0:T(8,128)(2,1)}, u32[]{:S(2)}, u32[]{:S(2)}) %collective-permute-start) | collective-permute-done | bytes 262176 | tf_op jit(solution)/shard_map/while/body/eval_jaxpr/ppermute | solution.py:10
  810.9 16.2 %collective-permute-done = bf16[128,1024]{1,0:T(8,128)(2,1)} collective-permute-done((bf16[128,1024]{1,0:T(8,128)(2,1)S(1)}, bf16[128,1024]{1,0:T(8,128)(2,1)}, u32[]{:S(2)}, u32[]{:S(2)}) %collective-permute-start) | collective-permute-done | bytes 262176 | tf_op jit(solution)/shard_map/while/body/eval_jaxpr/ppermute | solution.py:10
  834.1 15.8 %collective-permute-done = bf16[128,1024]{1,0:T(8,128)(2,1)} collective-permute-done((bf16[128,1024]{1,0:T(8,128)(2,1)S(1)}, bf16[128,1024]{1,0:T(8,128)(2,1)}, u32[]{:S(2)}, u32[]{:S(2)}) %collective-permute-start) | collective-permute-done | bytes 262176 | tf_op jit(solution)/shard_map/while/body/eval_jaxpr/ppermute | solution.py:10
  850.8 3.1 fusion.98
  856.8 15.8 %collective-permute-done = bf16[128,1024]{1,0:T(8,128)(2,1)} collective-permute-done((bf16[128,1024]{1,0:T(8,128)(2,1)S(1)}, bf16[128,1024]{1,0:T(8,128)(2,1)}, u32[]{:S(2)}, u32[]{:S(2)}) %collective-permute-start) | collective-permute-done | bytes 262176 | tf_op jit(solution)/shard_map/while/body/eval_jaxpr/ppermute | solution.py:10
  874.0 58.1 %all-reduce.5.cloned.1.call-done = f32[512,1024]{1,0:T(8,128)} async-done(((f32[512,1024]{1,0:T(8,128)}), f32[512,1024]{1,0:T(8,128)}) %all-reduce.5.cloned.1.call-update) | async-done | bytes 2097168 | tf_op jit(solution)/shard_map/psum | solution.py:114
  938.5 43.4 %all-reduce.7.cloned.1.call-done = bf16[512,1024]{1,0:T(8,128)(2,1)} async-done(((bf16[512,1024]{1,0:T(8,128)(2,1)}), bf16[512,1024]{1,0:T(8,128)(2,1)}) %all-reduce.7.cloned.1.call-update) | async-done | bytes 1048592 | tf_op jit(solution)/shard_map/psum | solution.py:121
  981.9 4.3 convolution_convert_fusion
  986.2 6.5 convert_bitcast_fusion
  992.7 4.1 copy.23
  997.8 4.1 copy.19
  1012.7 306.5 %all-reduce.9.cloned.1.call-done = (bf16[1024,1024]{0,1:T(8,128)(2,1)}, bf16[1024,1024]{0,1:T(8,128)(2,1)}, bf16[1024,256]{0,1:T(8,128)(2,1)}) async-done(((bf16[1024,1024]{0,1:T(8,128)(2,1)}, bf16[1024,1024]{0,1:T(8,128)(2,1)}, bf16[1024,256]{0,1:T(8,128)(2,1)}), (bf16[1024,1024]{0,1:T(8,128)(2,1)}, bf16[1024,1024]{0,1:T(8,128)(2,1)}, bf16[1024,256]{0,1:T(8,128)(2,1)})) %all-reduce.9.cloned.1.call-update) | async-done | bytes 4718608 | tf_op jit(solution)/shard_map/psum | solution.py:128
  1319.2 5.0 multiply_reduce_fusion
  1324.2 4.0 fusion.16
  1328.2 3.9 copy.26
  1332.2 4.9 fusion.19
  1337.1 4.0 copy.27
  1349.1 4.0 copy.30
  (384 shorter events, 257.6 us)
Async XLA Ops:
  7.2 26.5 %all-gather.2.cloned.1.call-start = ((), (), s32[]{:S(2)}) async-start(), calls=%async_computation | async-start | bytes 1310720 | tf_op jit(solution)/shard_map/all_gather | solution.py:77
  9.9 922.2 %all-reduce.5.cloned.1.call-start = ((), (), s32[]{:S(2)}) async-start(), calls=%async_computation.1 | async-start | bytes 4194304 | tf_op jit(solution)/shard_map/psum | solution.py:114
  44.7 24.2 %collective-permute-start.1 = (f32[128,1024]{1,0:T(8,128)}, f32[128,1024]{1,0:T(8,128)}, u32[]{:S(2)}, u32[]{:S(2)}) collective-permute-start(f32[128,1024]{1,0:T(8,128)} %convolution_add_fusion.2), channel_id=1, source_target_pairs={{124,0},{0,4},{4,8},{8,12},{12,16},{16,20},{20,24},{24,28},{28,32}... | collective-permute-start | bytes 1572872 | tf_op jit(solution)/shard_map/while/body/eval_jaxpr/ppermute | solution.py:10
  45.2 23.6 %collective-permute-start = (bf16[128,1024]{1,0:T(8,128)(2,1)S(1)}, bf16[128,1024]{1,0:T(8,128)(2,1)}, u32[]{:S(2)}, u32[]{:S(2)}) collective-permute-start(bf16[128,1024]{1,0:T(8,128)(2,1)S(1)} %copy.38), channel_id=1, source_target_pairs={{124,0},{0,4},{4,8},{8,12},{12,16},{16,20},{20,24},{24,28},{28,32}... | collective-permute-start | bytes 786440 | tf_op jit(solution)/shard_map/while/body/eval_jaxpr/ppermute | solution.py:10
  75.1 23.4 %collective-permute-start.1 = (f32[128,1024]{1,0:T(8,128)}, f32[128,1024]{1,0:T(8,128)}, u32[]{:S(2)}, u32[]{:S(2)}) collective-permute-start(f32[128,1024]{1,0:T(8,128)} %convolution_add_fusion.2), channel_id=1, source_target_pairs={{124,0},{0,4},{4,8},{8,12},{12,16},{16,20},{20,24},{24,28},{28,32}... | collective-permute-start | bytes 1572872 | tf_op jit(solution)/shard_map/while/body/eval_jaxpr/ppermute | solution.py:10
  75.1 23.4 %collective-permute-start = (bf16[128,1024]{1,0:T(8,128)(2,1)S(1)}, bf16[128,1024]{1,0:T(8,128)(2,1)}, u32[]{:S(2)}, u32[]{:S(2)}) collective-permute-start(bf16[128,1024]{1,0:T(8,128)(2,1)S(1)} %copy.38), channel_id=1, source_target_pairs={{124,0},{0,4},{4,8},{8,12},{12,16},{16,20},{20,24},{24,28},{28,32}... | collective-permute-start | bytes 786440 | tf_op jit(solution)/shard_map/while/body/eval_jaxpr/ppermute | solution.py:10
  104.7 22.5 %collective-permute-start.1 = (f32[128,1024]{1,0:T(8,128)}, f32[128,1024]{1,0:T(8,128)}, u32[]{:S(2)}, u32[]{:S(2)}) collective-permute-start(f32[128,1024]{1,0:T(8,128)} %convolution_add_fusion.2), channel_id=1, source_target_pairs={{124,0},{0,4},{4,8},{8,12},{12,16},{16,20},{20,24},{24,28},{28,32}... | collective-permute-start | bytes 1572872 | tf_op jit(solution)/shard_map/while/body/eval_jaxpr/ppermute | solution.py:10
  104.7 22.5 %collective-permute-start = (bf16[128,1024]{1,0:T(8,128)(2,1)S(1)}, bf16[128,1024]{1,0:T(8,128)(2,1)}, u32[]{:S(2)}, u32[]{:S(2)}) collective-permute-start(bf16[128,1024]{1,0:T(8,128)(2,1)S(1)} %copy.38), channel_id=1, source_target_pairs={{124,0},{0,4},{4,8},{8,12},{12,16},{16,20},{20,24},{24,28},{28,32}... | collective-permute-start | bytes 786440 | tf_op jit(solution)/shard_map/while/body/eval_jaxpr/ppermute | solution.py:10
  133.4 21.6 %collective-permute-start.1 = (f32[128,1024]{1,0:T(8,128)}, f32[128,1024]{1,0:T(8,128)}, u32[]{:S(2)}, u32[]{:S(2)}) collective-permute-start(f32[128,1024]{1,0:T(8,128)} %convolution_add_fusion.2), channel_id=1, source_target_pairs={{124,0},{0,4},{4,8},{8,12},{12,16},{16,20},{20,24},{24,28},{28,32}... | collective-permute-start | bytes 1572872 | tf_op jit(solution)/shard_map/while/body/eval_jaxpr/ppermute | solution.py:10
  133.4 21.6 %collective-permute-start = (bf16[128,1024]{1,0:T(8,128)(2,1)S(1)}, bf16[128,1024]{1,0:T(8,128)(2,1)}, u32[]{:S(2)}, u32[]{:S(2)}) collective-permute-start(bf16[128,1024]{1,0:T(8,128)(2,1)S(1)} %copy.38), channel_id=1, source_target_pairs={{124,0},{0,4},{4,8},{8,12},{12,16},{16,20},{20,24},{24,28},{28,32}... | collective-permute-start | bytes 786440 | tf_op jit(solution)/shard_map/while/body/eval_jaxpr/ppermute | solution.py:10
  161.2 20.6 %collective-permute-start.1 = (f32[128,1024]{1,0:T(8,128)}, f32[128,1024]{1,0:T(8,128)}, u32[]{:S(2)}, u32[]{:S(2)}) collective-permute-start(f32[128,1024]{1,0:T(8,128)} %convolution_add_fusion.2), channel_id=1, source_target_pairs={{124,0},{0,4},{4,8},{8,12},{12,16},{16,20},{20,24},{24,28},{28,32}... | collective-permute-start | bytes 1572872 | tf_op jit(solution)/shard_map/while/body/eval_jaxpr/ppermute | solution.py:10
  161.2 20.6 %collective-permute-start = (bf16[128,1024]{1,0:T(8,128)(2,1)S(1)}, bf16[128,1024]{1,0:T(8,128)(2,1)}, u32[]{:S(2)}, u32[]{:S(2)}) collective-permute-start(bf16[128,1024]{1,0:T(8,128)(2,1)S(1)} %copy.38), channel_id=1, source_target_pairs={{124,0},{0,4},{4,8},{8,12},{12,16},{16,20},{20,24},{24,28},{28,32}... | collective-permute-start | bytes 786440 | tf_op jit(solution)/shard_map/while/body/eval_jaxpr/ppermute | solution.py:10
  188.1 19.7 %collective-permute-start.1 = (f32[128,1024]{1,0:T(8,128)}, f32[128,1024]{1,0:T(8,128)}, u32[]{:S(2)}, u32[]{:S(2)}) collective-permute-start(f32[128,1024]{1,0:T(8,128)} %convolution_add_fusion.2), channel_id=1, source_target_pairs={{124,0},{0,4},{4,8},{8,12},{12,16},{16,20},{20,24},{24,28},{28,32}... | collective-permute-start | bytes 1572872 | tf_op jit(solution)/shard_map/while/body/eval_jaxpr/ppermute | solution.py:10
  188.1 19.7 %collective-permute-start = (bf16[128,1024]{1,0:T(8,128)(2,1)S(1)}, bf16[128,1024]{1,0:T(8,128)(2,1)}, u32[]{:S(2)}, u32[]{:S(2)}) collective-permute-start(bf16[128,1024]{1,0:T(8,128)(2,1)S(1)} %copy.38), channel_id=1, source_target_pairs={{124,0},{0,4},{4,8},{8,12},{12,16},{16,20},{20,24},{24,28},{28,32}... | collective-permute-start | bytes 786440 | tf_op jit(solution)/shard_map/while/body/eval_jaxpr/ppermute | solution.py:10
  214.0 18.8 %collective-permute-start.1 = (f32[128,1024]{1,0:T(8,128)}, f32[128,1024]{1,0:T(8,128)}, u32[]{:S(2)}, u32[]{:S(2)}) collective-permute-start(f32[128,1024]{1,0:T(8,128)} %convolution_add_fusion.2), channel_id=1, source_target_pairs={{124,0},{0,4},{4,8},{8,12},{12,16},{16,20},{20,24},{24,28},{28,32}... | collective-permute-start | bytes 1572872 | tf_op jit(solution)/shard_map/while/body/eval_jaxpr/ppermute | solution.py:10
  214.0 18.8 %collective-permute-start = (bf16[128,1024]{1,0:T(8,128)(2,1)S(1)}, bf16[128,1024]{1,0:T(8,128)(2,1)}, u32[]{:S(2)}, u32[]{:S(2)}) collective-permute-start(bf16[128,1024]{1,0:T(8,128)(2,1)S(1)} %copy.38), channel_id=1, source_target_pairs={{124,0},{0,4},{4,8},{8,12},{12,16},{16,20},{20,24},{24,28},{28,32}... | collective-permute-start | bytes 786440 | tf_op jit(solution)/shard_map/while/body/eval_jaxpr/ppermute | solution.py:10
  239.0 17.9 %collective-permute-start.1 = (f32[128,1024]{1,0:T(8,128)}, f32[128,1024]{1,0:T(8,128)}, u32[]{:S(2)}, u32[]{:S(2)}) collective-permute-start(f32[128,1024]{1,0:T(8,128)} %convolution_add_fusion.2), channel_id=1, source_target_pairs={{124,0},{0,4},{4,8},{8,12},{12,16},{16,20},{20,24},{24,28},{28,32}... | collective-permute-start | bytes 1572872 | tf_op jit(solution)/shard_map/while/body/eval_jaxpr/ppermute | solution.py:10
  239.0 17.9 %collective-permute-start = (bf16[128,1024]{1,0:T(8,128)(2,1)S(1)}, bf16[128,1024]{1,0:T(8,128)(2,1)}, u32[]{:S(2)}, u32[]{:S(2)}) collective-permute-start(bf16[128,1024]{1,0:T(8,128)(2,1)S(1)} %copy.38), channel_id=1, source_target_pairs={{124,0},{0,4},{4,8},{8,12},{12,16},{16,20},{20,24},{24,28},{28,32}... | collective-permute-start | bytes 786440 | tf_op jit(solution)/shard_map/while/body/eval_jaxpr/ppermute | solution.py:10
  400.3 17.9 %collective-permute-start.1 = (f32[128,1024]{1,0:T(8,128)}, f32[128,1024]{1,0:T(8,128)}, u32[]{:S(2)}, u32[]{:S(2)}) collective-permute-start(f32[128,1024]{1,0:T(8,128)} %convolution_add_fusion.2), channel_id=1, source_target_pairs={{124,0},{0,4},{4,8},{8,12},{12,16},{16,20},{20,24},{24,28},{28,32}... | collective-permute-start | bytes 1572872 | tf_op jit(solution)/shard_map/while/body/eval_jaxpr/ppermute | solution.py:10
  400.3 17.9 %collective-permute-start = (bf16[128,1024]{1,0:T(8,128)(2,1)S(1)}, bf16[128,1024]{1,0:T(8,128)(2,1)}, u32[]{:S(2)}, u32[]{:S(2)}) collective-permute-start(bf16[128,1024]{1,0:T(8,128)(2,1)S(1)} %copy.38), channel_id=1, source_target_pairs={{124,0},{0,4},{4,8},{8,12},{12,16},{16,20},{20,24},{24,28},{28,32}... | collective-permute-start | bytes 786440 | tf_op jit(solution)/shard_map/while/body/eval_jaxpr/ppermute | solution.py:10
  424.4 19.0 %collective-permute-start.1 = (f32[128,1024]{1,0:T(8,128)}, f32[128,1024]{1,0:T(8,128)}, u32[]{:S(2)}, u32[]{:S(2)}) collective-permute-start(f32[128,1024]{1,0:T(8,128)} %convolution_add_fusion.2), channel_id=1, source_target_pairs={{124,0},{0,4},{4,8},{8,12},{12,16},{16,20},{20,24},{24,28},{28,32}... | collective-permute-start | bytes 1572872 | tf_op jit(solution)/shard_map/while/body/eval_jaxpr/ppermute | solution.py:10
  424.4 19.0 %collective-permute-start = (bf16[128,1024]{1,0:T(8,128)(2,1)S(1)}, bf16[128,1024]{1,0:T(8,128)(2,1)}, u32[]{:S(2)}, u32[]{:S(2)}) collective-permute-start(bf16[128,1024]{1,0:T(8,128)(2,1)S(1)} %copy.38), channel_id=1, source_target_pairs={{124,0},{0,4},{4,8},{8,12},{12,16},{16,20},{20,24},{24,28},{28,32}... | collective-permute-start | bytes 786440 | tf_op jit(solution)/shard_map/while/body/eval_jaxpr/ppermute | solution.py:10
  449.6 20.1 %collective-permute-start.1 = (f32[128,1024]{1,0:T(8,128)}, f32[128,1024]{1,0:T(8,128)}, u32[]{:S(2)}, u32[]{:S(2)}) collective-permute-start(f32[128,1024]{1,0:T(8,128)} %convolution_add_fusion.2), channel_id=1, source_target_pairs={{124,0},{0,4},{4,8},{8,12},{12,16},{16,20},{20,24},{24,28},{28,32}... | collective-permute-start | bytes 1572872 | tf_op jit(solution)/shard_map/while/body/eval_jaxpr/ppermute | solution.py:10
  449.6 20.1 %collective-permute-start = (bf16[128,1024]{1,0:T(8,128)(2,1)S(1)}, bf16[128,1024]{1,0:T(8,128)(2,1)}, u32[]{:S(2)}, u32[]{:S(2)}) collective-permute-start(bf16[128,1024]{1,0:T(8,128)(2,1)S(1)} %copy.38), channel_id=1, source_target_pairs={{124,0},{0,4},{4,8},{8,12},{12,16},{16,20},{20,24},{24,28},{28,32}... | collective-permute-start | bytes 786440 | tf_op jit(solution)/shard_map/while/body/eval_jaxpr/ppermute | solution.py:10
  475.8 21.2 %collective-permute-start.1 = (f32[128,1024]{1,0:T(8,128)}, f32[128,1024]{1,0:T(8,128)}, u32[]{:S(2)}, u32[]{:S(2)}) collective-permute-start(f32[128,1024]{1,0:T(8,128)} %convolution_add_fusion.2), channel_id=1, source_target_pairs={{124,0},{0,4},{4,8},{8,12},{12,16},{16,20},{20,24},{24,28},{28,32}... | collective-permute-start | bytes 1572872 | tf_op jit(solution)/shard_map/while/body/eval_jaxpr/ppermute | solution.py:10
  475.9 21.1 %collective-permute-start = (bf16[128,1024]{1,0:T(8,128)(2,1)S(1)}, bf16[128,1024]{1,0:T(8,128)(2,1)}, u32[]{:S(2)}, u32[]{:S(2)}) collective-permute-start(bf16[128,1024]{1,0:T(8,128)(2,1)S(1)} %copy.38), channel_id=1, source_target_pairs={{124,0},{0,4},{4,8},{8,12},{12,16},{16,20},{20,24},{24,28},{28,32}... | collective-permute-start | bytes 786440 | tf_op jit(solution)/shard_map/while/body/eval_jaxpr/ppermute | solution.py:10
  503.2 22.2 %collective-permute-start.1 = (f32[128,1024]{1,0:T(8,128)}, f32[128,1024]{1,0:T(8,128)}, u32[]{:S(2)}, u32[]{:S(2)}) collective-permute-start(f32[128,1024]{1,0:T(8,128)} %convolution_add_fusion.2), channel_id=1, source_target_pairs={{124,0},{0,4},{4,8},{8,12},{12,16},{16,20},{20,24},{24,28},{28,32}... | collective-permute-start | bytes 1572872 | tf_op jit(solution)/shard_map/while/body/eval_jaxpr/ppermute | solution.py:10
  503.2 22.2 %collective-permute-start = (bf16[128,1024]{1,0:T(8,128)(2,1)S(1)}, bf16[128,1024]{1,0:T(8,128)(2,1)}, u32[]{:S(2)}, u32[]{:S(2)}) collective-permute-start(bf16[128,1024]{1,0:T(8,128)(2,1)S(1)} %copy.38), channel_id=1, source_target_pairs={{124,0},{0,4},{4,8},{8,12},{12,16},{16,20},{20,24},{24,28},{28,32}... | collective-permute-start | bytes 786440 | tf_op jit(solution)/shard_map/while/body/eval_jaxpr/ppermute | solution.py:10
  531.7 23.3 %collective-permute-start.1 = (f32[128,1024]{1,0:T(8,128)}, f32[128,1024]{1,0:T(8,128)}, u32[]{:S(2)}, u32[]{:S(2)}) collective-permute-start(f32[128,1024]{1,0:T(8,128)} %convolution_add_fusion.2), channel_id=1, source_target_pairs={{124,0},{0,4},{4,8},{8,12},{12,16},{16,20},{20,24},{24,28},{28,32}... | collective-permute-start | bytes 1572872 | tf_op jit(solution)/shard_map/while/body/eval_jaxpr/ppermute | solution.py:10
  531.7 23.3 %collective-permute-start = (bf16[128,1024]{1,0:T(8,128)(2,1)S(1)}, bf16[128,1024]{1,0:T(8,128)(2,1)}, u32[]{:S(2)}, u32[]{:S(2)}) collective-permute-start(bf16[128,1024]{1,0:T(8,128)(2,1)S(1)} %copy.38), channel_id=1, source_target_pairs={{124,0},{0,4},{4,8},{8,12},{12,16},{16,20},{20,24},{24,28},{28,32}... | collective-permute-start | bytes 786440 | tf_op jit(solution)/shard_map/while/body/eval_jaxpr/ppermute | solution.py:10
  561.2 24.6 %collective-permute-start.1 = (f32[128,1024]{1,0:T(8,128)}, f32[128,1024]{1,0:T(8,128)}, u32[]{:S(2)}, u32[]{:S(2)}) collective-permute-start(f32[128,1024]{1,0:T(8,128)} %convolution_add_fusion.2), channel_id=1, source_target_pairs={{124,0},{0,4},{4,8},{8,12},{12,16},{16,20},{20,24},{24,28},{28,32}... | collective-permute-start | bytes 1572872 | tf_op jit(solution)/shard_map/while/body/eval_jaxpr/ppermute | solution.py:10
  561.2 24.5 %collective-permute-start = (bf16[128,1024]{1,0:T(8,128)(2,1)S(1)}, bf16[128,1024]{1,0:T(8,128)(2,1)}, u32[]{:S(2)}, u32[]{:S(2)}) collective-permute-start(bf16[128,1024]{1,0:T(8,128)(2,1)S(1)} %copy.38), channel_id=1, source_target_pairs={{124,0},{0,4},{4,8},{8,12},{12,16},{16,20},{20,24},{24,28},{28,32}... | collective-permute-start | bytes 786440 | tf_op jit(solution)/shard_map/while/body/eval_jaxpr/ppermute | solution.py:10
  592.0 24.2 %collective-permute-start.1 = (f32[128,1024]{1,0:T(8,128)}, f32[128,1024]{1,0:T(8,128)}, u32[]{:S(2)}, u32[]{:S(2)}) collective-permute-start(f32[128,1024]{1,0:T(8,128)} %convolution_add_fusion.2), channel_id=1, source_target_pairs={{124,0},{0,4},{4,8},{8,12},{12,16},{16,20},{20,24},{24,28},{28,32}... | collective-permute-start | bytes 1572872 | tf_op jit(solution)/shard_map/while/body/eval_jaxpr/ppermute | solution.py:10
  592.0 24.2 %collective-permute-start = (bf16[128,1024]{1,0:T(8,128)(2,1)S(1)}, bf16[128,1024]{1,0:T(8,128)(2,1)}, u32[]{:S(2)}, u32[]{:S(2)}) collective-permute-start(bf16[128,1024]{1,0:T(8,128)(2,1)S(1)} %copy.38), channel_id=1, source_target_pairs={{124,0},{0,4},{4,8},{8,12},{12,16},{16,20},{20,24},{24,28},{28,32}... | collective-permute-start | bytes 786440 | tf_op jit(solution)/shard_map/while/body/eval_jaxpr/ppermute | solution.py:10
  622.4 23.4 %collective-permute-start.1 = (f32[128,1024]{1,0:T(8,128)}, f32[128,1024]{1,0:T(8,128)}, u32[]{:S(2)}, u32[]{:S(2)}) collective-permute-start(f32[128,1024]{1,0:T(8,128)} %convolution_add_fusion.2), channel_id=1, source_target_pairs={{124,0},{0,4},{4,8},{8,12},{12,16},{16,20},{20,24},{24,28},{28,32}... | collective-permute-start | bytes 1572872 | tf_op jit(solution)/shard_map/while/body/eval_jaxpr/ppermute | solution.py:10
  622.4 23.4 %collective-permute-start = (bf16[128,1024]{1,0:T(8,128)(2,1)S(1)}, bf16[128,1024]{1,0:T(8,128)(2,1)}, u32[]{:S(2)}, u32[]{:S(2)}) collective-permute-start(bf16[128,1024]{1,0:T(8,128)(2,1)S(1)} %copy.38), channel_id=1, source_target_pairs={{124,0},{0,4},{4,8},{8,12},{12,16},{16,20},{20,24},{24,28},{28,32}... | collective-permute-start | bytes 786440 | tf_op jit(solution)/shard_map/while/body/eval_jaxpr/ppermute | solution.py:10
  652.0 22.5 %collective-permute-start.1 = (f32[128,1024]{1,0:T(8,128)}, f32[128,1024]{1,0:T(8,128)}, u32[]{:S(2)}, u32[]{:S(2)}) collective-permute-start(f32[128,1024]{1,0:T(8,128)} %convolution_add_fusion.2), channel_id=1, source_target_pairs={{124,0},{0,4},{4,8},{8,12},{12,16},{16,20},{20,24},{24,28},{28,32}... | collective-permute-start | bytes 1572872 | tf_op jit(solution)/shard_map/while/body/eval_jaxpr/ppermute | solution.py:10
  652.0 22.5 %collective-permute-start = (bf16[128,1024]{1,0:T(8,128)(2,1)S(1)}, bf16[128,1024]{1,0:T(8,128)(2,1)}, u32[]{:S(2)}, u32[]{:S(2)}) collective-permute-start(bf16[128,1024]{1,0:T(8,128)(2,1)S(1)} %copy.38), channel_id=1, source_target_pairs={{124,0},{0,4},{4,8},{8,12},{12,16},{16,20},{20,24},{24,28},{28,32}... | collective-permute-start | bytes 786440 | tf_op jit(solution)/shard_map/while/body/eval_jaxpr/ppermute | solution.py:10
  680.7 21.5 %collective-permute-start.1 = (f32[128,1024]{1,0:T(8,128)}, f32[128,1024]{1,0:T(8,128)}, u32[]{:S(2)}, u32[]{:S(2)}) collective-permute-start(f32[128,1024]{1,0:T(8,128)} %convolution_add_fusion.2), channel_id=1, source_target_pairs={{124,0},{0,4},{4,8},{8,12},{12,16},{16,20},{20,24},{24,28},{28,32}... | collective-permute-start | bytes 1572872 | tf_op jit(solution)/shard_map/while/body/eval_jaxpr/ppermute | solution.py:10
  680.7 21.5 %collective-permute-start = (bf16[128,1024]{1,0:T(8,128)(2,1)S(1)}, bf16[128,1024]{1,0:T(8,128)(2,1)}, u32[]{:S(2)}, u32[]{:S(2)}) collective-permute-start(bf16[128,1024]{1,0:T(8,128)(2,1)S(1)} %copy.38), channel_id=1, source_target_pairs={{124,0},{0,4},{4,8},{8,12},{12,16},{16,20},{20,24},{24,28},{28,32}... | collective-permute-start | bytes 786440 | tf_op jit(solution)/shard_map/while/body/eval_jaxpr/ppermute | solution.py:10
  708.4 20.6 %collective-permute-start.1 = (f32[128,1024]{1,0:T(8,128)}, f32[128,1024]{1,0:T(8,128)}, u32[]{:S(2)}, u32[]{:S(2)}) collective-permute-start(f32[128,1024]{1,0:T(8,128)} %convolution_add_fusion.2), channel_id=1, source_target_pairs={{124,0},{0,4},{4,8},{8,12},{12,16},{16,20},{20,24},{24,28},{28,32}... | collective-permute-start | bytes 1572872 | tf_op jit(solution)/shard_map/while/body/eval_jaxpr/ppermute | solution.py:10
  708.4 20.6 %collective-permute-start = (bf16[128,1024]{1,0:T(8,128)(2,1)S(1)}, bf16[128,1024]{1,0:T(8,128)(2,1)}, u32[]{:S(2)}, u32[]{:S(2)}) collective-permute-start(bf16[128,1024]{1,0:T(8,128)(2,1)S(1)} %copy.38), channel_id=1, source_target_pairs={{124,0},{0,4},{4,8},{8,12},{12,16},{16,20},{20,24},{24,28},{28,32}... | collective-permute-start | bytes 786440 | tf_op jit(solution)/shard_map/while/body/eval_jaxpr/ppermute | solution.py:10
  735.3 19.7 %collective-permute-start.1 = (f32[128,1024]{1,0:T(8,128)}, f32[128,1024]{1,0:T(8,128)}, u32[]{:S(2)}, u32[]{:S(2)}) collective-permute-start(f32[128,1024]{1,0:T(8,128)} %convolution_add_fusion.2), channel_id=1, source_target_pairs={{124,0},{0,4},{4,8},{8,12},{12,16},{16,20},{20,24},{24,28},{28,32}... | collective-permute-start | bytes 1572872 | tf_op jit(solution)/shard_map/while/body/eval_jaxpr/ppermute | solution.py:10
  735.3 19.7 %collective-permute-start = (bf16[128,1024]{1,0:T(8,128)(2,1)S(1)}, bf16[128,1024]{1,0:T(8,128)(2,1)}, u32[]{:S(2)}, u32[]{:S(2)}) collective-permute-start(bf16[128,1024]{1,0:T(8,128)(2,1)S(1)} %copy.38), channel_id=1, source_target_pairs={{124,0},{0,4},{4,8},{8,12},{12,16},{16,20},{20,24},{24,28},{28,32}... | collective-permute-start | bytes 786440 | tf_op jit(solution)/shard_map/while/body/eval_jaxpr/ppermute | solution.py:10
  761.2 18.8 %collective-permute-start.1 = (f32[128,1024]{1,0:T(8,128)}, f32[128,1024]{1,0:T(8,128)}, u32[]{:S(2)}, u32[]{:S(2)}) collective-permute-start(f32[128,1024]{1,0:T(8,128)} %convolution_add_fusion.2), channel_id=1, source_target_pairs={{124,0},{0,4},{4,8},{8,12},{12,16},{16,20},{20,24},{24,28},{28,32}... | collective-permute-start | bytes 1572872 | tf_op jit(solution)/shard_map/while/body/eval_jaxpr/ppermute | solution.py:10
  761.2 18.8 %collective-permute-start = (bf16[128,1024]{1,0:T(8,128)(2,1)S(1)}, bf16[128,1024]{1,0:T(8,128)(2,1)}, u32[]{:S(2)}, u32[]{:S(2)}) collective-permute-start(bf16[128,1024]{1,0:T(8,128)(2,1)S(1)} %copy.38), channel_id=1, source_target_pairs={{124,0},{0,4},{4,8},{8,12},{12,16},{16,20},{20,24},{24,28},{28,32}... | collective-permute-start | bytes 786440 | tf_op jit(solution)/shard_map/while/body/eval_jaxpr/ppermute | solution.py:10
  874.0 107.9 %all-reduce.7.cloned.1.call-start = ((), (), s32[]{:S(2)}) async-start(), calls=%async_computation.2 | async-start | bytes 2097152 | tf_op jit(solution)/shard_map/psum | solution.py:121
  937.2 382.0 %all-reduce.9.cloned.1.call-start = ((), (), s32[]{:S(2)}) async-start(), calls=%async_computation.3 | async-start | bytes 9437184 | tf_op jit(solution)/shard_map/psum | solution.py:128
  (67 other events, 1570.3 us)
Sparse Core Ops, SparseCore 0:
  10.3 23.3 all-gather.1
  874.1 57.9 all-reduce.4
  937.3 44.5 all-reduce.6
  992.8 326.3 all-reduce.8
where the time goes:
time: 1370 us; the launch traced here: 1360 us
  waiting for transfers between devices  1040 us (76%)
  matrix products  206 us (15%)
  local copies, waits for them, and re-layouts  67 us (5%)
  other arithmetic  29.2 us (2%)
  between operations  13.9 us (1%)
    ppermute x64, waiting for transfers between devices, passed_along(): return lax.ppermute(block, axis, route)  610 us
    psum x1, waiting for transfers between devices, per_device(): lax.psum(grad_up.astype(jnp.bfloat16), 'dp').astype(jnp.float32)  306 us
    dot_general x32, matrix products, couple_derivs(): lax.dot_general(vision_members, caption_members, (((1,), (1,)), ((), ()))...  98.1 us
    dot_general x35, matrix products, contract_rows(): lax.dot_general(left, right, (((0,), (0,)), ((), ())), preferred_element_...  81.6 us
    psum x1, waiting for transfers between devices, per_device(): summed = lax.psum(image_dz, 'mp')  58.1 us
    psum x1, waiting for transfers between devices, per_device(): lax.psum(contract_cols(image_grad, mapper_matrix).astype(jnp.bfloat16), '...  43.4 us
    unnamed x42, local copies, waits for them, and re-layouts  35.6 us
    while x96, local copies, waits for them, and re-layouts  30.6 us
  transfers between devices with their start and end apart: 68, of which 36 were waited for; matrix products, arithmetic and copies ran while one was open for 3% of the time, Pallas kernels for 0%

commit v1 on v0

v1 whole, which is shorter than its diff:
```python
import functools

import jax
import jax.numpy as jnp
from jax import lax
from jax.experimental import pallas as pl
from jax.experimental.pallas import tpu as pltpu
from jax.sharding import PartitionSpec as P

MESH = pl.DeviceIdType.MESH
F32 = jnp.float32
BF16 = jnp.bfloat16
VMEM = pl.BlockSpec(memory_space=pltpu.VMEM)
SMEM = pl.BlockSpec(memory_space=pltpu.SMEM)

TEXT_STEPS = ((0, 1), (1, 0), (3, 0), (1, 1), (3, 1), (2, 0), (2, 1))
IMAGE_STEPS = (1, 3, 2)


def place():
    d = lax.axis_index("dp")
    m = lax.axis_index("mp")
    return d // 8, (d // 2) % 4, d % 2, m // 2, m % 2


def device(z, x, lo, hi, core):
    return ((z % 4) * 4 + x % 4) * 2 + lo % 2, (hi % 2) * 2 + core % 2


def remote(src, dst, send, recv, to):
    return pltpu.make_async_remote_copy(
        src_ref=src, dst_ref=dst, send_sem=send, recv_sem=recv, device_id=to, device_id_type=MESH
    )


def nn(a, b):
    return jnp.dot(a, b, preferred_element_type=F32)


def nt(a, b):
    return lax.dot_general(a, b, (((1,), (1,)), ((), ())), preferred_element_type=F32)


def tn(a, b):
    return lax.dot_general(a, b, (((0,), (0,)), ((), ())), preferred_element_type=F32)


def pair_kernel(
    sharp,
    offset,
    caption,
    final,
    mapper,
    grad_out,
    mapper_out,
    text_out,
    texts,
    images,
    weights,
    maps,
    embed,
    units,
    scale,
    text_unit,
    text_scale,
    image_own,
    image_send,
    image_recv,
    text_own,
    text_send,
    text_recv,
    text_part,
    cross_send,
    cross_recv,
    grads,
    t_s,
    t_r,
    f_s,
    f_r,
    m_s,
    m_r,
    a_s,
    a_r,
    i_s,
    i_r,
    x_s,
    x_r,
    r_s,
    r_r,
    c_s,
    c_r,
    g_s,
    g_r,
):
    z, x, lo, hi, core = place()
    sibling = device(z, x, lo, hi, core + 1)
    across = device(z, x, lo, hi + 1, core)
    beside = device(z, x, lo + 1, hi + 1, core)
    text_to = [device(z + a, x, lo + b, hi, core) for a, b in TEXT_STEPS]
    text_from = [device(z + 4 - a, x, lo + b, hi, core) for a, b in TEXT_STEPS]
    image_to = [device(z, x + a, lo, hi, core) for a in IMAGE_STEPS]
    image_from = [device(z, x + 4 - a, lo, hi, core) for a in IMAGE_STEPS]

    barrier = pltpu.get_barrier_semaphore()
    partners = text_to + image_to + [sibling, across, beside]
    for one in partners:
        pl.semaphore_signal(barrier, inc=1, device_id=one, device_id_type=MESH)

    raw = caption[...].astype(F32)
    ts = lax.rsqrt(jnp.sum(raw * raw, axis=1, keepdims=True) + 1e-06)
    tu = raw * ts
    text_unit[...] = tu
    text_scale[...] = ts
    texts[0:128, :] = tu.astype(BF16)
    maps[0] = mapper[...]

    pl.semaphore_wait(barrier, len(partners))

    map_copies = [
        remote(maps.at[0], maps.at[2], m_s.at[1], m_r.at[1], beside),
        remote(maps.at[0], maps.at[1], m_s.at[0], m_r.at[0], sibling),
    ]
    for one in map_copies:
        one.start()
    text_copies = [
        remote(texts.at[pl.ds(0, 128)], texts.at[pl.ds(128 * (k + 1), 128)], t_s.at[k], t_r.at[k], to)
        for k, to in enumerate(text_to)
    ]
    for one in text_copies:
        one.start()
    forward = [
        remote(
            texts.at[pl.ds(128 * k, 128)],
            texts.at[pl.ds(1024 + 128 * k, 128)],
            f_s.at[k],
            f_r.at[k],
            sibling,
        )
        for k in range(8)
    ]
    forward[0].start()

    half = pl.ds(core * 256, 256)

    def embed_with(k, h, c):
        column = pl.multiple_of((h % 2) * 512 + (c % 2) * 256, 256)
        embed[:, pl.ds(column, 256)] = nn(final[half, :], maps[k]).astype(BF16)

    embed_with(0, hi, core)
    map_copies[1].wait_recv()
    embed_with(1, hi, core + 1)
    map_copies[0].wait_recv()
    pass_map = remote(maps.at[2], maps.at[3], m_s.at[2], m_r.at[2], sibling)
    pass_map.start()
    embed_with(2, hi + 1, core)
    pass_map.wait_recv()
    embed_with(3, hi + 1, core + 1)

    wide = embed[...].astype(F32)
    s = lax.rsqrt(jnp.sum(wide * wide, axis=1, keepdims=True) + 1e-06)
    u = wide * s
    units[...] = u
    scale[...] = s
    images[0:256, :] = u.astype(BF16)

    image_copies = [
        remote(images.at[pl.ds(0, 256)], images.at[pl.ds(256 * (k + 1), 256)], a_s.at[k], a_r.at[k], to)
        for k, to in enumerate(image_to)
    ]
    for one in image_copies:
        one.start()

    mapper_out[hi * 2 + core] = maps[0]
    mapper_out[hi * 2 + (1 - core)] = maps[1]
    mapper_out[(1 - hi) * 2 + core] = maps[2]
    mapper_out[(1 - hi) * 2 + (1 - core)] = maps[3]

    for k in range(7):
        text_copies[k].wait_recv()
        forward[k + 1].start()
    for k in range(8):
        forward[k].wait_recv()

    factor = sharp[0]
    shift = offset[0]

    def pair_weights(b):
        rows = pl.ds(256 * b, 256)

        def chunk(j, _):
            cols = pl.ds(pl.multiple_of(j * 512, 512), 512)
            logits = factor * nt(images[rows, :], texts[cols, :]) + shift
            w = factor / (1.0 + jnp.exp(-logits))
            if b == 0:
                row = lax.broadcasted_iota(jnp.int32, (256, 512), 0)
                col = lax.broadcasted_iota(jnp.int32, (256, 512), 1)
                cls = jnp.where(j == 0, core, 1 - core)
                on = jnp.logical_and(core == hi, j % 2 == 0).astype(jnp.int32)
                hit = (row == cls * 128 + col) & (col < 128 * on)
                w = jnp.where(hit, -factor / (1.0 + jnp.exp(logits)), w)
            weights[rows, cols] = w.astype(BF16)
            return 0

        lax.fori_loop(0, 4, chunk, 0)

    def image_part(b, out):
        rows = pl.ds(256 * b, 256)

        def chunk(j, _):
            cols = pl.ds(pl.multiple_of(j * 256, 256), 256)
            out[:, cols] = nn(weights[rows, :], texts[:, cols]).astype(out.dtype)
            return 0

        lax.fori_loop(0, 4, chunk, 0)

    pair_weights(0)
    image_part(0, image_own)
    image_back = [
        remote(image_send.at[k], image_recv.at[k], i_s.at[k], i_r.at[k], image_from[k]) for k in range(3)
    ]
    for k in range(3):
        image_copies[k].wait_recv()
        pair_weights(k + 1)
        image_part(k + 1, image_send.at[k])
        image_back[k].start()

    def text_chunk(base, out):
        def chunk(j, _):
            rows = pl.ds(pl.multiple_of(j * 256, 256), 256)
            cols = pl.ds(pl.multiple_of(base + j * 256, 256), 256)
            out[rows, :] = tn(weights[:, cols], images[...]).astype(out.dtype)
            return 0

        lax.fori_loop(0, 4, chunk, 0)

    text_chunk(1024, cross_send)
    cross = remote(cross_send, cross_recv, x_s, x_r, sibling)
    cross.start()
    text_chunk(0, text_own)
    cross.wait_recv()

    def add_cross(j, _):
        rows = pl.ds(pl.multiple_of(j * 128, 128), 128)
        total = text_own[rows, :] + cross_recv[rows, :].astype(F32)
        text_own[rows, :] = total
        text_send[rows, :] = total.astype(BF16)
        return 0

    lax.fori_loop(0, 8, add_cross, 0)
    text_back = [
        remote(text_send.at[pl.ds(128 * (k + 1), 128)], text_recv.at[k], r_s.at[k], r_r.at[k], text_from[k])
        for k in range(7)
    ]
    for one in text_back:
        one.start()

    for k in range(3):
        image_back[k].wait_recv()

    mine = pl.ds(pl.multiple_of(hi * 128, 128), 128)
    theirs = pl.ds(pl.multiple_of((1 - hi) * 128, 128), 128)

    def image_sum(rows):
        total = image_own[rows, :]
        for k in range(3):
            total = total + image_recv[k, rows, :].astype(F32)
        return total

    text_part[...] = image_sum(theirs).astype(BF16)
    swap = remote(text_part, grads.at[0], c_s, c_r, across)
    swap.start()
    image_own[mine, :] = image_sum(mine)
    swap.wait_recv()
    dz = image_own[mine, :] + grads[0].astype(F32)
    u = units[mine, :]
    grad = scale[mine, :] * (dz - u * jnp.sum(u * dz, axis=1, keepdims=True))
    grads[1] = grad.astype(BF16)
    spread = [
        remote(grads.at[1], grads.at[2], g_s.at[0], g_r.at[0], across),
        remote(grads.at[1], grads.at[3], g_s.at[1], g_r.at[1], sibling),
    ]
    for one in spread:
        one.start()

    for k in range(7):
        text_back[k].wait_recv()
    dz = text_own[0:128, :]
    for k in range(7):
        dz = dz + text_recv[k].astype(F32)
    tu = text_unit[...]
    text_out[...] = text_scale[...] * (dz - tu * jnp.sum(tu * dz, axis=1, keepdims=True))

    spread[0].wait_recv()
    last = remote(grads.at[2], grads.at[4], g_s.at[2], g_r.at[2], sibling)
    last.start()
    spread[1].wait_recv()
    last.wait_recv()

    def put(k, h, c):
        grad_out[pl.ds(pl.multiple_of(c * 256 + h * 128, 128), 128), :] = grads[k]

    put(1, hi, core)
    put(2, 1 - hi, core)
    put(3, hi, 1 - core)
    put(4, 1 - hi, 1 - core)

    for one in (
        map_copies + [pass_map] + text_copies + forward + image_copies + image_back
        + [cross] + text_back + [swap] + spread + [last]
    ):
        one.wait_send()


def pairs(sharp, offset, caption, final, mapper):
    dma = pltpu.SemaphoreType.DMA
    return pl.pallas_call(
        pair_kernel,
        name="pairs",
        out_shape=(
            jax.ShapeDtypeStruct((512, 1024), BF16),
            jax.ShapeDtypeStruct((4, 1024, 256), BF16),
            jax.ShapeDtypeStruct((128, 1024), F32),
        ),
        in_specs=[SMEM, SMEM, VMEM, VMEM, VMEM],
        out_specs=(VMEM, VMEM, VMEM),
        scratch_shapes=[
            pltpu.VMEM((2048, 1024), BF16),
            pltpu.VMEM((1024, 1024), BF16),
            pltpu.VMEM((1024, 2048), BF16),
            pltpu.VMEM((4, 1024, 256), BF16),
            pltpu.VMEM((256, 1024), BF16),
            pltpu.VMEM((256, 1024), F32),
            pltpu.VMEM((256, 1), F32),
            pltpu.VMEM((128, 1024), F32),
            pltpu.VMEM((128, 1), F32),
            pltpu.VMEM((256, 1024), F32),
            pltpu.VMEM((3, 256, 1024), BF16),
            pltpu.VMEM((3, 256, 1024), BF16),
            pltpu.VMEM((1024, 1024), F32),
            pltpu.VMEM((1024, 1024), BF16),
            pltpu.VMEM((7, 128, 1024), BF16),
            pltpu.VMEM((128, 1024), BF16),
            pltpu.VMEM((1024, 1024), BF16),
            pltpu.VMEM((1024, 1024), BF16),
            pltpu.VMEM((5, 128, 1024), BF16),
            dma((7,)), dma((7,)),
            dma((8,)), dma((8,)),
            dma((3,)), dma((3,)),
            dma((3,)), dma((3,)),
            dma((3,)), dma((3,)),
            dma, dma,
            dma((7,)), dma((7,)),
            dma, dma,
            dma((3,)), dma((3,)),
        ],
        compiler_params=pltpu.CompilerParams(
            collective_id=0, has_side_effects=True, vmem_limit_bytes=56 * 2**20
        ),
    )(sharp, offset, caption, final, mapper)


def lion_step(weight, moment, grad, axis):
    moment_wide = moment.astype(F32)
    blend = 0.9 * moment_wide + 0.1 * grad
    spread = jnp.sqrt(jnp.mean(blend * blend, axis=axis, keepdims=True) + 1e-06)
    soft = blend / jnp.sqrt(blend * blend + 0.25 * spread * (0.25 * spread))
    update = (soft + 1.0 * weight.astype(F32)).astype(BF16)
    renewed = (0.99 * moment_wide + 0.01 * grad).astype(BF16)
    return (update, renewed)


def per_device(
    vision_layer_entry,
    latent_preact_values,
    final_layer_result,
    caption_vectors_raw,
    sharpness_factor,
    offset_term,
    first_feedforward_matrix,
    second_feedforward_matrix,
    mapper_matrix,
    first_matrix_velocity,
    second_matrix_velocity,
    mapper_velocity,
):
    image_grad, maps, text_grad = pairs(
        sharpness_factor, offset_term, caption_vectors_raw, final_layer_result, mapper_matrix
    )
    column = lax.axis_index("mp")
    own_columns = lax.dynamic_slice_in_dim(image_grad, column * 256, 256, 1)
    grad_proj = tn(final_layer_result, own_columns)
    mapper_full = jnp.concatenate([maps[k] for k in range(4)], axis=1)
    back = nt(image_grad, mapper_full).astype(BF16)
    active, gelu_back = jax.vjp(jax.nn.gelu, latent_preact_values.astype(F32))
    grad_down = tn(active.astype(BF16), back)
    inner = nt(back, second_feedforward_matrix)
    pre_grad = gelu_back(inner)[0].astype(BF16)
    grad_up = tn(vision_layer_entry, pre_grad)
    grad_up, grad_down, grad_proj = (
        lax.psum(grad_up.astype(BF16), "dp").astype(F32),
        lax.psum(grad_down.astype(BF16), "dp").astype(F32),
        lax.psum(grad_proj.astype(BF16), "dp").astype(F32),
    )
    update_up, renewed_up = lion_step(first_feedforward_matrix, first_matrix_velocity, grad_up, 0)
    update_down, renewed_down = lion_step(
        second_feedforward_matrix, second_matrix_velocity, grad_down, 1
    )
    update_proj, renewed_proj = lion_step(mapper_matrix, mapper_velocity, grad_proj, 0)
    return (update_up, update_down, update_proj, renewed_up, renewed_down, renewed_proj, text_grad)


def solution(mesh):
    return jax.shard_map(
        per_device,
        mesh=mesh,
        in_specs=(
            P("dp", None),
            P("dp", "mp"),
            P("dp", None),
            P(("dp", "mp"), None),
            P(),
            P(),
            P(None, "mp"),
            P("mp", None),
            P(None, "mp"),
            P(None, "mp"),
            P("mp", None),
            P(None, "mp"),
        ),
        out_specs=(
            P(None, "mp"),
            P("mp", None),
            P(None, "mp"),
            P(None, "mp"),
            P("mp", None),
            P(None, "mp"),
            P(("dp", "mp"), None),
        ),
        check_vma=False,
    )
```

time: 1370 us -> 495 us (0.36)
  waiting for transfers between devices: 1040 us -> 306 us
  matrix products: 206 us -> 14 us
  Pallas kernels: 0 us -> 102 us
  local copies, waits for them, and re-layouts: 67 us -> 38.6 us
    ppermute x64 -> x0, waiting for transfers between devices: 610 us -> none  [passed_along(): return lax.ppermute(block, axis, route)]
    dot_general x101 -> x4, matrix products: 206 us -> 14 us  [the longest x3 11.1 us: tn(): lax.dot_general(a, b, (((0,), (0,)), ((), ())), preferred_element_type=F32)]
    pallas_call x0 -> x1, Pallas kernels: none -> 102 us  [pairs(): pl.pallas_call(pair_kernel, name='pairs', out_shape=(jax.ShapeDtypeStruct...]
    psum x3 -> x1, waiting for transfers between devices: 408 us -> 306 us  [per_device(): lax.psum(grad_up.astype(BF16), 'dp').astype(F32)]
    while x96 -> x0, local copies, waits for them, and re-layouts: 30.6 us -> none
    all_gather x1 -> x0, waiting for transfers between devices: 22.8 us -> none  [per_device(): gathered = lax.all_gather(embedded, 'mp', axis=1, tiled=True)]
    unnamed x42 -> x43, local copies, waits for them, and re-layouts: 35.6 us -> 35.9 us
  transfers between devices with their start and end apart: 68 -> 1, of which waited for: 36 -> 1; matrix products, arithmetic and copies ran while one was open for 3% -> 3% of each run, Pallas kernels for 0% -> 0%
where the time goes in v1:
time: 495 us; the launch traced here: 494 us
  waiting for transfers between devices  306 us (62%)
  Pallas kernels  102 us (21%)
  local copies, waits for them, and re-layouts  38.6 us (8%)
  other arithmetic  17.3 us (3%)
  between operations  15.5 us (3%)
  matrix products  14 us (3%)
    psum x1, waiting for transfers between devices, per_device(): lax.psum(grad_up.astype(BF16), 'dp').astype(F32)  306 us
    pallas_call x1, Pallas kernels, pairs(): pl.pallas_call(pair_kernel, name='pairs', out_shape=(jax.ShapeDtypeStruct...  102 us
    unnamed x43, local copies, waits for them, and re-layouts  35.9 us
    convert_element_type x3, other arithmetic, lion_step(): renewed = (0.99 * moment_wide + 0.01 * grad).astype(BF16)  11.9 us
    dot_general x3, matrix products, tn(): lax.dot_general(a, b, (((0,), (0,)), ((), ())), preferred_element_type=F32)  11.1 us
  transfers between devices with their start and end apart: 1, of which 1 were waited for; matrix products, arithmetic and copies ran while one was open for 3% of the time, Pallas kernels for 0%

profile of v1, /device:TPU:0, one launch (start us, length us, event | category | flops | bytes accessed | tf_op | source)
XLA Modules:
  0.0 493.7 jit_solution(15865064911878455746)
XLA Ops:
  7.2 0.0 copy-start
  7.2 0.0 all-reduce.3.cloned.1.call-start
  8.6 102.0 %pairs.1 = (bf16[512,1024]{1,0:T(8,128)(2,1)}, bf16[4,1024,256]{2,1,0:T(8,128)(2,1)}, f32[128,1024]{1,0:T(8,128)}) custom-call(f32[1]{0:T(128)S(6)} %copy.37.sharp, f32[1]{0:T(128)S(6)} %copy.38.offset, bf16[128,1024]{1,0:T(8,128)(2,1)} %caption.1, bf16[512,1024]{1,0:T(8,128)(2,1)} %final.1, bf16[1024,256]{1,0:T(8,128)(2,1)} %mapper.1), custom_call_target="tpu_custom_call" | custom-call | tf_op jit(solution)/shard_map/pairs/pallas_call | solution.py:316
  110.6 0.0 copy-start.6
  110.6 2.7 slice_bitcast_fusion.3
  113.3 0.0 copy-done.6
  113.3 2.2 fusion.27
  115.5 0.0 copy-start.13
  115.5 2.9 fusion.24
  118.4 0.0 copy-start.14
  118.4 1.0 copy-done.14
  119.4 0.0 copy-done.13
  119.4 0.0 copy-start.10
  119.4 2.8 convolution_convert_fusion
  122.1 0.0 copy-done
  122.2 0.0 copy-done.10
  122.2 6.1 %convert_bitcast_fusion = bf16[1024,1024]{0,1:T(8,128)(2,1)} fusion(bf16[512,1024]{1,0:T(8,128)(2,1)S(1)} %copy-done, bf16[512,1024]{1,0:T(8,128)(2,1)} %param.13, bf16[512,1024]{1,0:T(8,128)(2,1)} %copy-done.14, bf16[1024,1024]{1,0:T(8,128)(2,1)S(1)} %copy-done.10), kind=kOutput, calls=%fused_computation.41 | convolution fusion | flops 2159542272 | bytes 7340032 | tf_op jit(solution)/shard_map/dot_general | solution.py:45
  128.3 0.0 all-reduce.3.cloned.1.call-update
  128.3 0.0 copy-start.8
  128.3 4.0 copy.23
  132.3 0.0 copy-done.8
  132.3 1.0 copy.25
  133.3 4.1 copy.19
  137.4 0.0 copy-done.11
  137.4 2.5 copy.20
  140.0 2.9 copy.21
  142.8 2.0 copy.24
  144.9 306.3 %all-reduce.3.cloned.1.call-done = (bf16[1024,1024]{0,1:T(8,128)(2,1)}, bf16[1024,1024]{0,1:T(8,128)(2,1)}, bf16[1024,256]{0,1:T(8,128)(2,1)}) async-done(((bf16[1024,1024]{0,1:T(8,128)(2,1)}, bf16[1024,1024]{0,1:T(8,128)(2,1)}, bf16[1024,256]{0,1:T(8,128)(2,1)}), (bf16[1024,1024]{0,1:T(8,128)(2,1)}, bf16[1024,1024]{0,1:T(8,128)(2,1)}, bf16[1024,256]{0,1:T(8,128)(2,1)})) %all-reduce.3.cloned.1.call-update) | async-done | bytes 4718608 | tf_op jit(solution)/shard_map/psum | solution.py:400
  451.1 5.0 %multiply_reduce_fusion = (f32[1024]{0:T(1024)S(1)}, f32[1024]{0:T(1024)S(1)}) fusion(bf16[1024,1024]{0,1:T(8,128)(2,1)} %get-tuple-element.21, bf16[1024,1024]{0,1:T(8,128)(2,1)S(1)} %copy.21, bf16[1024,1024]{0,1:T(8,128)(2,1)} %get-tuple-element.20, bf16[1024,1024]{0,1:T(8,128)(2,1)} %copy.19), kind=kLoop, calls=%fused_computation.21 | loop fusion | flops 14678016 | bytes 8396800 | tf_op jit(solution)/shard_map/reduce_sum | solution.py:365
  456.1 0.0 copy-done.1
  456.1 0.0 copy-done.2
  456.1 0.0 copy-done.4
  456.2 4.0 fusion.2
  460.1 3.9 copy.26
  464.1 4.9 fusion.5
  469.0 4.0 copy.27
  473.0 0.0 copy-done.5
  473.0 0.0 copy-done.7
  473.1 0.3 multiply_reduce_fusion.2
  473.4 3.0 fusion.31
  476.4 2.0 copy.28
  478.5 0.0 copy-done.3
  478.5 2.5 copy.29
  481.0 4.0 copy.30
  485.0 0.0 copy-done.9
  485.0 1.0 copy.31
  486.0 0.0 copy-done.12
  486.0 0.8 copy.39
  (12 shorter events, 0.0 us)
Async XLA Ops:
  7.2 115.0 %copy-start = (bf16[512,1024]{1,0:T(8,128)(2,1)S(1)}, bf16[512,1024]{1,0:T(8,128)(2,1)}, u32[]{:S(2)}) copy-start(bf16[512,1024]{1,0:T(8,128)(2,1)} %param.12) | copy-start | bytes 3145732
  7.2 444.0 %all-reduce.3.cloned.1.call-start = ((), (), s32[]{:S(2)}) async-start(), calls=%async_computation | async-start | bytes 9437184 | tf_op jit(solution)/shard_map/psum | solution.py:400
  110.6 2.7 copy-start.6
  115.5 3.9 copy-start.13
  118.4 1.0 copy-start.14
  119.4 2.8 copy-start.10
  128.3 4.0 copy-start.8
  133.3 4.1 copy-start.11
  451.1 5.0 %copy-start.1 = (bf16[1024,1024]{0,1:T(8,128)(2,1)S(1)}, bf16[1024,1024]{0,1:T(8,128)(2,1)}, u32[]{:S(2)}) copy-start(bf16[1024,1024]{0,1:T(8,128)(2,1)} %copy.19) | copy-start | bytes 6291460
  451.1 5.0 %copy-start.2 = (bf16[1024,1024]{0,1:T(8,128)(2,1)S(1)}, bf16[1024,1024]{0,1:T(8,128)(2,1)}, u32[]{:S(2)}) copy-start(bf16[1024,1024]{0,1:T(8,128)(2,1)} %get-tuple-element.20) | copy-start | bytes 6291460
  451.1 5.0 %copy-start.4 = (bf16[1024,1024]{0,1:T(8,128)(2,1)S(1)}, bf16[1024,1024]{0,1:T(8,128)(2,1)}, u32[]{:S(2)}) copy-start(bf16[1024,1024]{0,1:T(8,128)(2,1)} %copy.20) | copy-start | bytes 6291460
  469.0 4.0 copy-start.5
  469.0 4.0 copy-start.7
  473.4 5.1 %copy-start.3 = (bf16[1024,1024]{0,1:T(8,128)(2,1)S(1)}, bf16[1024,1024]{0,1:T(8,128)(2,1)}, u32[]{:S(2)}) copy-start(bf16[1024,1024]{0,1:T(8,128)(2,1)} %get-tuple-element.25) | copy-start | bytes 6291460
  481.0 4.0 copy-start.9
  481.0 5.0 %copy-start.12 = (f32[128,1024]{1,0:T(8,128)S(1)}, f32[128,1024]{1,0:T(8,128)}, u32[]{:S(2)}) copy-start(f32[128,1024]{1,0:T(8,128)} %get-tuple-element.48) | copy-start | bytes 1572868
Sparse Core Ops, SparseCore 0:
  128.4 322.6 all-reduce.2

commit v2 on v1

--- a/solution.py
+++ b/solution.py
@@ -43,6 +43,10 @@
 
 def tn(a, b):
     return lax.dot_general(a, b, (((0,), (0,)), ((), ())), preferred_element_type=F32)
+
+
+def map_columns(hi, core):
+    return pl.ds(pl.multiple_of((hi % 2) * 512 + (core % 2) * 256, 256), 256)
 
 
 def pair_kernel(
@@ -143,8 +147,7 @@
     half = pl.ds(core * 256, 256)
 
     def embed_with(k, h, c):
-        column = pl.multiple_of((h % 2) * 512 + (c % 2) * 256, 256)
-        embed[:, pl.ds(column, 256)] = nn(final[half, :], maps[k]).astype(BF16)
+        embed[:, map_columns(h, c)] = nn(final[half, :], maps[k]).astype(BF16)
 
     embed_with(0, hi, core)
     map_copies[1].wait_recv()
@@ -170,10 +173,10 @@
     for one in image_copies:
         one.start()
 
-    mapper_out[hi * 2 + core] = maps[0]
-    mapper_out[hi * 2 + (1 - core)] = maps[1]
-    mapper_out[(1 - hi) * 2 + core] = maps[2]
-    mapper_out[(1 - hi) * 2 + (1 - core)] = maps[3]
+    mapper_out[:, map_columns(hi, core)] = maps[0]
+    mapper_out[:, map_columns(hi, core + 1)] = maps[1]
+    mapper_out[:, map_columns(hi + 1, core)] = maps[2]
+    mapper_out[:, map_columns(hi + 1, core + 1)] = maps[3]
 
     for k in range(7):
         text_copies[k].wait_recv()
@@ -318,7 +321,7 @@
         name="pairs",
         out_shape=(
             jax.ShapeDtypeStruct((512, 1024), BF16),
-            jax.ShapeDtypeStruct((4, 1024, 256), BF16),
+            jax.ShapeDtypeStruct((1024, 1024), BF16),
             jax.ShapeDtypeStruct((128, 1024), F32),
         ),
         in_specs=[SMEM, SMEM, VMEM, VMEM, VMEM],
@@ -359,14 +362,348 @@
     )(sharp, offset, caption, final, mapper)
 
 
-def lion_step(weight, moment, grad, axis):
-    moment_wide = moment.astype(F32)
-    blend = 0.9 * moment_wide + 0.1 * grad
-    spread = jnp.sqrt(jnp.mean(blend * blend, axis=axis, keepdims=True) + 1e-06)
-    soft = blend / jnp.sqrt(blend * blend + 0.25 * spread * (0.25 * spread))
-    update = (soft + 1.0 * weight.astype(F32)).astype(BF16)
-    renewed = (0.99 * moment_wide + 0.01 * grad).astype(BF16)
-    return (update, renewed)
+def gelu_parts(value):
+    slope = 0.7978845608028654
+    square = value * value
+    t = jnp.tanh(slope * (value + 0.044715 * (square * value)))
+    cdf = 0.5 * (1.0 + t)
+    derivative = cdf + 0.5 * value * (1.0 - t * t) * (slope * (1.0 + 3 * 0.044715 * square))
+    return value * cdf, derivative
+
+
+PART = 1152
+STRIP = 288
+TILE = 144
+
+
+def grad_kernel(
+    image_grad,
+    mapper,
+    latent,
+    second,
+    entry,
+    final,
+    total_out,
+    back,
+    active,
+    pre,
+    grads,
+    done,
+    far_in,
+    near_in,
+    strip,
+    side_out,
+    side_in,
+    tile,
+    tile_out,
+    tile_in,
+    far_s,
+    far_r,
+    near_s,
+    near_r,
+    side_s,
+    side_r,
+    tile_s,
+    tile_r,
+    t_s,
+    t_r,
+    q_s,
+    q_r,
+    p_s,
+    p_r,
+):
+    z, x, lo, hi, core = place()
+
+    def step(part, along_p, along_q):
+        a, b = (along_p, along_q) if part == 0 else (along_q, along_p)
+        return device(z + a, x + b, lo, hi, core)
+
+    pair_lo = device(z, x, lo + 1, hi, core)
+    barrier = pltpu.get_barrier_semaphore()
+    partners = [step(0, a, 0) for a in (1, 3, 2)] + [step(0, 0, a) for a in (1, 3, 2)] + [pair_lo]
+    for one in partners:
+        pl.semaphore_signal(barrier, inc=1, device_id=one, device_id_type=MESH)
+
+    started = []
+
+    def begin(copy):
+        copy.start()
+        started.append(copy)
+        return copy
+
+    def loop(count, body):
+        def run(j, _):
+            body(pl.ds(pl.multiple_of(j * 256, 256), 256))
+            return 0
+
+        lax.fori_loop(0, count, run, 0)
+
+    first = (z, x)
+    second_axis = (x, z)
+
+    def strip_rows(part, offset):
+        at = (first[part] + offset) % 4
+        return pl.ds(pl.multiple_of(part * PART + at * STRIP, 16), STRIP)
+
+    def side_columns(part, offset):
+        at = (second_axis[part] + offset) % 4
+        return pl.ds(pl.multiple_of(at * 256, 256), 256)
+
+    left, right = pl.ds(0, 512), pl.ds(512, 512)
+
+    def send_far(part):
+        far = strip_rows(part, 2)
+        up = begin(remote(grads.at[far, left], far_in.at[part, 0], far_s.at[part, 0], far_r.at[part, 0], step(part, 1, 0)))
+        down = begin(remote(grads.at[far, right], far_in.at[part, 1], far_s.at[part, 1], far_r.at[part, 1], step(part, 3, 0)))
+        n0 = begin(
+            remote(
+                grads.at[strip_rows(part, 1), right], near_in.at[part, 0, :, right],
+                near_s.at[part, 0], near_r.at[part, 0], step(part, 1, 0),
+            )
+        )
+        n1 = begin(
+            remote(
+                grads.at[strip_rows(part, 3), left], near_in.at[part, 1, :, left],
+                near_s.at[part, 1], near_r.at[part, 1], step(part, 3, 0),
+            )
+        )
+        return up, down, n0, n1
+
+    def send_near(part, copies):
+        out = []
+        for k, (cols, offset) in enumerate(((left, 1), (right, 3))):
+            copies[k].wait_recv()
+            rows = strip_rows(part, offset)
+            grads[rows, cols] = (grads[rows, cols].astype(F32) + far_in[part, k].astype(F32)).astype(BF16)
+            out.append(
+                begin(
+                    remote(
+                        grads.at[rows, cols], near_in.at[part, k, :, cols],
+                        near_s.at[part, 2 + k], near_r.at[part, 2 + k], step(part, offset, 0),
+                    )
+                )
+            )
+        return out
+
+    def send_side(part, copies, more):
+        for one in copies[2:] + tuple(more):
+            one.wait_recv()
+        rows = strip_rows(part, 0)
+        out = []
+        for k, offset in enumerate((2, 1, 3, 0)):
+            cols = side_columns(part, offset)
+            total = (
+                grads[rows, cols].astype(F32)
+                + near_in[part, 0, :, cols].astype(F32)
+                + near_in[part, 1, :, cols].astype(F32)
+            )
+            if offset == 0:
+                strip[part] = total
+            else:
+                side_out[part, k] = total.astype(BF16)
+                out.append(
+                    begin(
+                        remote(
+                            side_out.at[part, k], side_in.at[part, k],
+                            side_s.at[part, k], side_r.at[part, k], step(part, 0, offset),
+                        )
+                    )
+                )
+        return out
+
+    mine = pl.ds(pl.multiple_of(lo * TILE, 16), TILE)
+    theirs = pl.ds(pl.multiple_of((1 - lo) * TILE, 16), TILE)
+
+    def send_tile(part, copies):
+        for one in copies:
+            one.wait_recv()
+
+        def total(rows):
+            value = strip[part, rows, :]
+            for k in range(3):
+                value = value + side_in[part, k, rows, :].astype(F32)
+            return value
+
+        tile_out[part] = total(theirs).astype(BF16)
+        out = begin(remote(tile_out.at[part], tile_in.at[part], tile_s.at[part], tile_r.at[part], pair_lo))
+        tile[part] = total(mine)
+        return out
+
+    def spread_tile(part, copy):
+        copy.wait_recv()
+        at = (part * PART + first[part] * STRIP) + lo * TILE
+        rows = pl.ds(pl.multiple_of(at, 16), TILE)
+        cols = side_columns(part, 0)
+        done[rows, cols] = (tile[part] + tile_in[part].astype(F32)).astype(BF16)
+        return begin(remote(done.at[rows, cols], done.at[rows, cols], t_s.at[part], t_r.at[part], pair_lo))
+
+    def spread_side(part, copy):
+        copy.wait_recv()
+        block = done.at[strip_rows(part, 0), side_columns(part, 0)]
+        return [
+            begin(remote(block, block, q_s.at[part, k], q_r.at[part, k], step(part, 0, offset)))
+            for k, offset in enumerate((2, 1, 3))
+        ]
+
+    def spread_strip(part, copies):
+        for one in copies:
+            one.wait_recv()
+        out = []
+        rows = strip_rows(part, 0)
+        for k, (cols, offset) in enumerate(((left, 1), (right, 3), (right, 1), (left, 3))):
+            block = done.at[rows, cols]
+            out.append(begin(remote(block, block, p_s.at[part, k], p_r.at[part, k], step(part, offset, 0))))
+        return out
+
+    def spread_far(part, copies):
+        out = []
+        for k, (cols, offset) in enumerate(((left, 1), (right, 3))):
+            copies[k].wait_recv()
+            block = done.at[strip_rows(part, 4 - offset), cols]
+            out.append(begin(remote(block, block, p_s.at[part, 4 + k], p_r.at[part, 4 + k], step(part, offset, 0))))
+        return out
+
+    def back_part(cols):
+        back[:, cols] = nt(image_grad[...], mapper[cols, :]).astype(BF16)
+
+    loop(4, back_part)
+
+    def active_part(cols):
+        value, derivative = gelu_parts(latent[:, cols].astype(F32))
+        active[:, cols] = value.astype(BF16)
+        pre[:, cols] = (nt(back[...], second[cols, :]) * derivative).astype(BF16)
+
+    loop(4, active_part)
+
+    own = image_grad[:, map_columns(hi, core)]
+
+    def proj_part(cols):
+        value = tn(final[:, cols], own).astype(BF16)
+        grads[1024:1152, cols] = value[0:128]
+        grads[2176:2304, cols] = value[128:256]
+
+    loop(4, proj_part)
+
+    def down_part(j, _):
+        cols = pl.ds(pl.multiple_of(j * 256, 256), 256)
+        rows = pl.ds(pl.multiple_of(PART + j * 256, 128), 256)
+        grads[rows, :] = tn(active[:, cols], back[...]).astype(BF16)
+        return 0
+
+    lax.fori_loop(0, 4, down_part, 0)
+    pl.semaphore_wait(barrier, len(partners))
+    far_b = send_far(1)
+
+    def up_part(cols):
+        grads[cols, :] = tn(entry[:, cols], pre[...]).astype(BF16)
+
+    loop(4, up_part)
+    far_a = send_far(0)
+    near_b = send_near(1, far_b)
+    near_a = send_near(0, far_a)
+    side_b = send_side(1, far_b, near_b)
+    side_a = send_side(0, far_a, near_a)
+    tile_b = send_tile(1, side_b)
+    tile_a = send_tile(0, side_a)
+    t_b = spread_tile(1, tile_b)
+    t_a = spread_tile(0, tile_a)
+    q_b = spread_side(1, t_b)
+    q_a = spread_side(0, t_a)
+    p_b = spread_strip(1, q_b)
+    p_a = spread_strip(0, q_a)
+    f_b = spread_far(1, p_b)
+    f_a = spread_far(0, p_a)
+    for one in p_b[2:] + p_a[2:] + f_b + f_a:
+        one.wait_recv()
+    for one in started:
+        one.wait_send()
+    total_out[...] = done[...]
+
+
+def weight_grads(image_grad, mapper, latent, second, entry, final):
+    dma = pltpu.SemaphoreType.DMA
+    return pl.pallas_call(
+        grad_kernel,
+        name="weight_grads",
+        out_shape=jax.ShapeDtypeStruct((2 * PART, 1024), BF16),
+        in_specs=[VMEM] * 6,
+        out_specs=VMEM,
+        scratch_shapes=[
+            pltpu.VMEM((512, 1024), BF16),
+            pltpu.VMEM((512, 1024), BF16),
+            pltpu.VMEM((512, 1024), BF16),
+            pltpu.VMEM((2 * PART, 1024), BF16),
+            pltpu.VMEM((2 * PART, 1024), BF16),
+            pltpu.VMEM((2, 2, STRIP, 512), BF16),
+            pltpu.VMEM((2, 2, STRIP, 1024), BF16),
+            pltpu.VMEM((2, STRIP, 256), F32),
+            pltpu.VMEM((2, 3, STRIP, 256), BF16),
+            pltpu.VMEM((2, 3, STRIP, 256), BF16),
+            pltpu.VMEM((2, TILE, 256), F32),
+            pltpu.VMEM((2, TILE, 256), BF16),
+            pltpu.VMEM((2, TILE, 256), BF16),
+            dma((2, 2)), dma((2, 2)),
+            dma((2, 4)), dma((2, 4)),
+            dma((2, 3)), dma((2, 3)),
+            dma((2,)), dma((2,)),
+            dma((2,)), dma((2,)),
+            dma((2, 3)), dma((2, 3)),
+            dma((2, 6)), dma((2, 6)),
+        ],
+        compiler_params=pltpu.CompilerParams(
+            collective_id=1, has_side_effects=True, vmem_limit_bytes=56 * 2**20
+        ),
+    )(image_grad, mapper, latent, second, entry, final)
+
+
+def lion_block(weight, moment, grad, axis):
+    grad = grad.astype(F32)
+    moment = moment.astype(F32)
+    blend = 0.9 * moment + 0.1 * grad
+    square = blend * blend
+    floor = 0.0625 * (jnp.mean(square, axis=axis, keepdims=True) + 1e-06)
+    update = blend * lax.rsqrt(square + floor) + weight.astype(F32)
+    return update.astype(BF16), (0.99 * moment + 0.01 * grad).astype(BF16)
+
+
+def lion_kernel(
+    g_up, g_down, g_proj_a, g_proj_b, w_up, w_down, w_proj, m_up, m_down, m_proj,
+    u_up, u_down, u_proj, r_up, r_down, r_proj,
+):
+    u_up[...], r_up[...] = lion_block(w_up[...], m_up[...], g_up[...], 0)
+    u_down[...], r_down[...] = lion_block(w_down[...], m_down[...], g_down[...], 1)
+
+    @pl.when(pl.program_id(0) == 0)
+    def _():
+        grad = jnp.concatenate(
+            [g[:, 256 * i : 256 * (i + 1)] for i in range(4) for g in (g_proj_a, g_proj_b)], axis=0
+        )
+        u_proj[...], r_proj[...] = lion_block(w_proj[...], m_proj[...], grad, 0)
+
+
+def lion(total, weights, moments):
+    column = pl.BlockSpec((1024, 128), lambda i: (0, i))
+    row = pl.BlockSpec((128, 1024), lambda i: (i, 0))
+    whole = pl.BlockSpec((1024, 256), lambda i: (0, 0))
+    like = [column, row, whole]
+    square = jax.ShapeDtypeStruct((1024, 1024), BF16)
+    narrow = jax.ShapeDtypeStruct((1024, 256), BF16)
+    return pl.pallas_call(
+        lion_kernel,
+        name="lion",
+        grid=(8,),
+        out_shape=(square, square, narrow, square, square, narrow),
+        in_specs=[
+            column,
+            pl.BlockSpec((128, 1024), lambda i: (9 + i, 0)),
+            pl.BlockSpec((128, 1024), lambda i: (8, 0)),
+            pl.BlockSpec((128, 1024), lambda i: (17, 0)),
+        ]
+        + like
+        + like,
+        out_specs=tuple(like + like),
+        compiler_params=pltpu.CompilerParams(vmem_limit_bytes=32 * 2**20),
+    )(total, total, total, total, *weights, *moments)
 
 
 def per_device(
@@ -383,30 +720,23 @@
     second_matrix_velocity,
     mapper_velocity,
 ):
-    image_grad, maps, text_grad = pairs(
+    image_grad, mapper_full, text_grad = pairs(
         sharpness_factor, offset_term, caption_vectors_raw, final_layer_result, mapper_matrix
     )
-    column = lax.axis_index("mp")
-    own_columns = lax.dynamic_slice_in_dim(image_grad, column * 256, 256, 1)
-    grad_proj = tn(final_layer_result, own_columns)
-    mapper_full = jnp.concatenate([maps[k] for k in range(4)], axis=1)
-    back = nt(image_grad, mapper_full).astype(BF16)
-    active, gelu_back = jax.vjp(jax.nn.gelu, latent_preact_values.astype(F32))
-    grad_down = tn(active.astype(BF16), back)
-    inner = nt(back, second_feedforward_matrix)
-    pre_grad = gelu_back(inner)[0].astype(BF16)
-    grad_up = tn(vision_layer_entry, pre_grad)
-    grad_up, grad_down, grad_proj = (
-        lax.psum(grad_up.astype(BF16), "dp").astype(F32),
-        lax.psum(grad_down.astype(BF16), "dp").astype(F32),
-        lax.psum(grad_proj.astype(BF16), "dp").astype(F32),
+    total = weight_grads(
+        image_grad,
+        mapper_full,
+        latent_preact_values,
+        second_feedforward_matrix,
+        vision_layer_entry,
+        final_layer_result,
     )
-    update_up, renewed_up = lion_step(first_feedforward_matrix, first_matrix_velocity, grad_up, 0)
-    update_down, renewed_down = lion_step(
-        second_feedforward_matrix, second_matrix_velocity, grad_down, 1
+    results = lion(
+        total,
+        (first_feedforward_matrix, second_feedforward_matrix, mapper_matrix),
+        (first_matrix_velocity, second_matrix_velocity, mapper_velocity),
     )
-    update_proj, renewed_proj = lion_step(mapper_matrix, mapper_velocity, grad_proj, 0)
-    return (update_up, update_down, update_proj, renewed_up, renewed_down, renewed_proj, text_grad)
+    return (*results, text_grad)
 
 
 def solution(mesh):

time: 495 us -> 201 us (0.41)
  waiting for transfers between devices: 306 us -> 0 us
  Pallas kernels: 102 us -> 193 us
  local copies, waits for them, and re-layouts: 38.6 us -> 4.75 us
  other arithmetic: 17.3 us -> 0 us
  matrix products: 14 us -> 0 us
  between operations: 15.5 us -> 2.04 us
    psum x1 -> x0, waiting for transfers between devices: 306 us -> none  [per_device(): lax.psum(grad_up.astype(BF16), 'dp').astype(F32)]
    pallas_call x0 -> x2, Pallas kernels: none -> 90.9 us  [the longest x1 80 us: weight_grads(): pl.pallas_call(grad_kernel, name='weight_grads', out_shape=jax.ShapeDtype...]
    unnamed x43 -> x17, local copies, waits for them, and re-layouts: 35.9 us -> 4.75 us
    dot_general x4 -> x0, matrix products: 14 us -> none  [the longest x3 11.1 us: tn(): lax.dot_general(a, b, (((0,), (0,)), ((), ())), preferred_element_type=F32)]
    convert_element_type x3 -> x0, other arithmetic: 11.9 us -> none  [lion_step(): renewed = (0.99 * moment_wide + 0.01 * grad).astype(BF16)]
    reduce_sum x2 -> x0, other arithmetic: 5.28 us -> none  [lion_step(): spread = jnp.sqrt(jnp.mean(blend * blend, axis=axis, keepdims=True) + 1e-06)]
  transfers between devices with their start and end apart: 1 -> 0, of which waited for: 1 -> 0; matrix products, arithmetic and copies ran while one was open for 3% -> 0% of each run, Pallas kernels for 0% -> 0%
where the time goes in v2:
time: 201 us; the launch traced here: 200 us
  Pallas kernels  193 us (96%)
  local copies, waits for them, and re-layouts  4.75 us (2%)
  between operations  2.04 us (1%)
    pallas_call x1, Pallas kernels, pairs(): pl.pallas_call(pair_kernel, name='pairs', out_shape=(jax.ShapeDtypeStruct...  102 us
    pallas_call x1, Pallas kernels, weight_grads(): pl.pallas_call(grad_kernel, name='weight_grads', out_shape=jax.ShapeDtype...  80 us
    pallas_call x1, Pallas kernels, lion(): pl.pallas_call(lion_kernel, name='lion', grid=(8,), out_shape=(square, sq...  10.9 us
    unnamed x17, local copies, waits for them, and re-layouts  4.75 us

profile of v2, /device:TPU:0, one launch (start us, length us, event | category | flops | bytes accessed | tf_op | source)
XLA Modules:
  0.0 199.8 jit_solution(2057326306780216651)
XLA Ops:
  1.9 102.0 %pairs.1 = (bf16[512,1024]{1,0:T(8,128)(2,1)}, bf16[1024,1024]{1,0:T(8,128)(2,1)}, f32[128,1024]{1,0:T(8,128)}) custom-call(f32[1]{0:T(128)S(6)} %copy.20.sharp, f32[1]{0:T(128)S(6)} %copy.21.offset, bf16[128,1024]{1,0:T(8,128)(2,1)} %caption.1, bf16[512,1024]{1,0:T(8,128)(2,1)} %final.3, bf16[1024,256]{1,0:T(8,128)(2,1)} %w_proj.1), custom_call_target="tpu_custom_call" | custom-call | tf_op jit(solution)/shard_map/pairs/pallas_call | solution.py:319
  103.9 0.0 copy-start.1
  104.0 0.0 copy-start.2
  104.0 0.0 copy-start.3
  104.0 0.0 copy-start.4
  104.0 0.0 copy-start.6
  104.0 80.0 %weight_grads.1.g_up.g_down.g_proj_a.g_proj_b = bf16[2304,1024]{1,0:T(8,128)(2,1)} custom-call(bf16[512,1024]{1,0:T(8,128)(2,1)} %get-tuple-element.16.image_grad, bf16[1024,1024]{1,0:T(8,128)(2,1)} %get-tuple-element.17.mapper, bf16[512,1024]{1,0:T(8,128)(2,1)} %latent.1, bf16[1024,1024]{1,0:T(8,128)(2,1)} %w_down.1, bf16[512,1024]{1,0:T(8,128)(2,1)} %entry.1, ...), custom_call_target="tpu_custom_call" | custom-call | tf_op jit(solution)/shard_map/weight_grads/pallas_call | solution.py:625
  184.0 0.0 copy-done.1
  184.0 0.0 copy-done.2
  184.0 0.0 copy-done.3
  184.0 0.0 copy-done.4
  184.1 0.0 copy-done.6
  184.1 0.0 copy-start
  184.1 2.3 %copy-done = bf16[2304,1024]{1,0:T(8,128)(2,1)S(1)} copy-done((bf16[2304,1024]{1,0:T(8,128)(2,1)S(1)}, bf16[2304,1024]{1,0:T(8,128)(2,1)}, u32[]{:S(2)}) %copy-start) | copy-done | bytes 4718616
  186.4 0.0 copy-start.5
  186.4 1.6 copy-done.5
  188.0 0.0 copy-start.7
  188.0 10.9 %lion.1 = (bf16[1024,1024]{1,0:T(8,128)(2,1)}, bf16[1024,1024]{1,0:T(8,128)(2,1)}, bf16[1024,256]{1,0:T(8,128)(2,1)}, bf16[1024,1024]{1,0:T(8,128)(2,1)}, bf16[1...) custom-call(bf16[2304,1024]{1,0:T(8,128)(2,1)S(1)} %copy-done, bf16[2304,1024]{1,0:T(8,128)(2,1)S(1)} %copy-done, ...), custom_call_target="tpu_custom_call" | custom-call | tf_op jit(solution)/shard_map/lion/pallas_call | solution.py:691
  198.9 0.0 copy-done.7
  199.0 0.8 copy.22
Async XLA Ops:
  103.9 80.1 %copy-start.1 = (bf16[1024,1024]{1,0:T(8,128)(2,1)S(1)}, bf16[1024,1024]{1,0:T(8,128)(2,1)}, u32[]{:S(2)}) copy-start(bf16[1024,1024]{1,0:T(8,128)(2,1)} %w_down.1) | copy-start | bytes 6291460
  104.0 80.1 %copy-start.2 = (bf16[1024,256]{1,0:T(8,128)(2,1)S(1)}, bf16[1024,256]{1,0:T(8,128)(2,1)}, u32[]{:S(2)}) copy-start(bf16[1024,256]{1,0:T(8,128)(2,1)} %w_proj.1) | copy-start | bytes 1572868
  104.0 80.1 %copy-start.3 = (bf16[1024,1024]{1,0:T(8,128)(2,1)S(1)}, bf16[1024,1024]{1,0:T(8,128)(2,1)}, u32[]{:S(2)}) copy-start(bf16[1024,1024]{1,0:T(8,128)(2,1)} %w_up.1) | copy-start | bytes 6291460
  104.0 80.1 %copy-start.4 = (bf16[1024,1024]{1,0:T(8,128)(2,1)S(1)}, bf16[1024,1024]{1,0:T(8,128)(2,1)}, u32[]{:S(2)}) copy-start(bf16[1024,1024]{1,0:T(8,128)(2,1)} %m_up.1) | copy-start | bytes 6291460
  104.0 80.1 %copy-start.6 = (bf16[1024,256]{1,0:T(8,128)(2,1)S(1)}, bf16[1024,256]{1,0:T(8,128)(2,1)}, u32[]{:S(2)}) copy-start(bf16[1024,256]{1,0:T(8,128)(2,1)} %m_proj.1) | copy-start | bytes 1572868
  184.1 2.3 %copy-start = (bf16[2304,1024]{1,0:T(8,128)(2,1)S(1)}, bf16[2304,1024]{1,0:T(8,128)(2,1)}, u32[]{:S(2)}) copy-start(bf16[2304,1024]{1,0:T(8,128)(2,1)} %weight_grads.1.g_up.g_down.g_proj_a.g_proj_b) | copy-start | bytes 14155780
  186.4 1.6 copy-start.5
  188.0 11.0 %copy-start.7 = (f32[128,1024]{1,0:T(8,128)S(1)}, f32[128,1024]{1,0:T(8,128)}, u32[]{:S(2)}) copy-start(f32[128,1024]{1,0:T(8,128)} %get-tuple-element.38) | copy-start | bytes 1572868

commit v3 on v0

v3 whole, which is shorter than its diff:
```python
import types

import jax
import jax.numpy as jnp
from jax import lax
from jax.experimental import pallas as pl
from jax.experimental.pallas import tpu as pltpu
from jax.sharding import PartitionSpec as P

MESH = pl.DeviceIdType.MESH
F32 = jnp.float32
BF16 = jnp.bfloat16
VMEM = pl.BlockSpec(memory_space=pltpu.VMEM)
SMEM = pl.BlockSpec(memory_space=pltpu.SMEM)
ANY = pl.BlockSpec(memory_space=pl.ANY)

PART = 1152
STRIP = 288
TILE = 144
COPIES = 160


def nn(a, b):
    return jnp.dot(a, b, preferred_element_type=F32)


def nt(a, b):
    return lax.dot_general(a, b, (((1,), (1,)), ((), ())), preferred_element_type=F32)


def tn(a, b):
    return lax.dot_general(a, b, (((0,), (0,)), ((), ())), preferred_element_type=F32)


def cut(start, size, unit=16):
    return pl.ds(start if isinstance(start, int) else pl.multiple_of(start, unit), size)


def loop(count, body, size=256):
    def run(j, _):
        body(cut(j * size, size, size))
        return 0

    lax.fori_loop(0, count, run, 0)


def gelu_parts(value):
    slope = 0.7978845608028654
    square = value * value
    t = jnp.tanh(slope * (value + 0.044715 * (square * value)))
    cdf = 0.5 * (1.0 + t)
    derivative = cdf + 0.5 * value * (1.0 - t * t) * (slope * (1.0 + 3 * 0.044715 * square))
    return value * cdf, derivative


class Links:
    def __init__(self, send, recv):
        d = lax.axis_index("dp")
        m = lax.axis_index("mp")
        self.z, self.x, self.lo = d // 8, (d // 2) % 4, d % 2
        self.hi, self.core = m // 2, m % 2
        self.y = self.hi * 2 + self.lo
        self.send, self.recv = send, recv
        self.started = []

    def at(self, z=0, x=0, y=0, core=0):
        row = (self.y + y) % 4
        dp = (((self.z + z) % 4) * 4 + (self.x + x) % 4) * 2 + row % 2
        return dp, (row // 2) * 2 + (self.core + core) % 2

    def copy(self, src, dst, to):
        k = len(self.started)
        one = pltpu.make_async_remote_copy(
            src_ref=src,
            dst_ref=dst,
            send_sem=self.send.at[k],
            recv_sem=self.recv.at[k],
            device_id=to,
            device_id_type=MESH,
        )
        one.start()
        self.started.append(one)
        return one


class RingSum:
    def __init__(self, links, src, block, far_in, near_in, on, off):
        self.links, self.src, self.block = links, src, block
        self.far_in, self.near_in, self.on, self.off = far_in, near_in, on, off
        self.half = far_in.shape[1]

    def part(self, k, i):
        return self.near_in.at[k, pl.ds(i * self.half, self.half)]

    def start(self):
        copy, src, block = self.links.copy, self.src, self.block
        self.far = [
            copy(src.at[block(2, 0)], self.far_in.at[0], self.on),
            copy(src.at[block(2, 1)], self.far_in.at[1], self.off),
        ]
        self.near = [
            copy(src.at[block(1, 1)], self.part(0, 1), self.on),
            copy(src.at[block(3, 0)], self.part(1, 0), self.off),
        ]

    def middle(self):
        for i, k, to in ((0, 1, self.on), (1, 3, self.off)):
            self.far[i].wait_recv()
            at = self.block(k, i)
            self.src[at] = (self.src[at].astype(F32) + self.far_in[i].astype(F32)).astype(BF16)
            self.near.append(self.links.copy(self.src.at[at], self.part(i, i), to))

    def arrive(self):
        for one in self.near:
            one.wait_recv()

    def total(self, i, cols=slice(None)):
        rows = pl.ds(i * self.half, self.half)
        at = self.block(0, i)
        own = self.src[at] if cols == slice(None) else self.src[at[0], cols]
        return (
            own.astype(F32)
            + self.near_in[0, rows, cols].astype(F32)
            + self.near_in[1, rows, cols].astype(F32)
        )


def step_kernel(
    sharp, offset, caption, final, mapper, latent_in, second_in, entry_in, total_out, text_out, *scratch
):
    r = types.SimpleNamespace(**dict(zip(SCRATCH, scratch)))
    net = Links(r.send, r.recv)
    hi, core = net.hi, net.core
    copy = net.copy
    sibling = net.at(core=1)
    z_on, z_off = net.at(z=1), net.at(z=3)
    x_on, x_off = net.at(x=1), net.at(x=3)
    y_on, y_off = net.at(y=1), net.at(y=3)
    across = net.at(y=2)
    pair_lo = net.at(y=1 - 2 * net.lo + 4)
    beside = net.at(y=2 * net.lo + 3)
    quarter = hi * 2 + core

    def rows_of(h, c):
        return cut(((h % 2) * 2 + c % 2) * 128, 128, 128)

    def cols_of(h, c):
        return cut(((h % 2) * 2 + c % 2) * 256, 256, 256)

    barrier = pltpu.get_barrier_semaphore()
    partners = [sibling, z_on, z_off, net.at(z=2), x_on, x_off, net.at(x=2), y_on, y_off, across]
    partners.append(net.at(y=2, core=1))
    for one in partners:
        pl.semaphore_signal(barrier, inc=1, device_id=one, device_id_type=MESH)
    loads = [
        pltpu.make_async_copy(src, dst, r.load.at[k])
        for k, (src, dst) in enumerate(
            ((latent_in, r.latent), (second_in, r.second), (entry_in, r.entry))
        )
    ]
    for one in loads:
        one.start()

    r.columns[...] = nn(final[...], mapper[...]).astype(BF16)
    raw = caption[...].astype(F32)
    text_scale = lax.rsqrt(jnp.sum(raw * raw, axis=1, keepdims=True) + 1e-06)
    unit = raw * text_scale
    r.text_scale[...] = text_scale
    r.text_unit[...] = unit
    unit = unit.astype(BF16)
    r.texts[0:64, :] = unit[0:64]
    r.texts[256:320, :] = unit[64:128]
    r.mapper[:, cols_of(hi, core)] = mapper[...]
    r.embed[:, cols_of(hi, core)] = r.columns[rows_of(hi, core), :]
    pl.semaphore_wait(barrier, len(partners))

    def give(h, c, to):
        return copy(r.columns.at[rows_of(h, c)], r.embed.at[:, cols_of(hi, core)], to)

    embed_copies = [
        give(hi + 1, core, across),
        give(hi + 1, core + 1, net.at(y=2, core=1)),
        give(hi, core + 1, sibling),
    ]

    rings = (((y_on, y_off), (z_on, z_off)), ((z_on, z_off), (y_on, y_off)))

    def slot(half, s, p, part=None):
        start = s * 512 + half * 256 + p * 64
        return pl.ds(start, 64) if part is None else pl.ds(start + 32 * part, 32)

    got = {}

    def text_copy(half, src, dst, to, part=None):
        one = copy(r.texts.at[slot(half, *src, part)], r.texts.at[slot(half, *dst, part)], to)
        got.setdefault((half, dst), []).append(one)

    def arrived(half, s, p):
        for one in got[half, (s, p)]:
            one.wait_recv()

    def text_first(half):
        on, off = rings[half][0]
        text_copy(half, (0, 0), (0, 1), on)
        text_copy(half, (0, 0), (0, 3), off)

    def text_second(half, p):
        on, off = rings[half][1]
        text_copy(half, (0, p), (1, p), on)
        text_copy(half, (0, p), (3, p), off)

    def text_far_first(half):
        on, off = rings[half][0]
        text_copy(half, (0, 1), (0, 2), on, 0)
        text_copy(half, (0, 3), (0, 2), off, 1)

    def text_far_second(half, p):
        on, off = rings[half][1]
        text_copy(half, (1, p), (2, p), on, 0)
        text_copy(half, (3, p), (2, p), off, 1)

    halves = (0, 1)
    for half in halves:
        text_first(half)
    for half in halves:
        text_second(half, 0)

    for one in embed_copies:
        one.wait_recv()
    wide = r.embed[...].astype(F32)
    image_scale = lax.rsqrt(jnp.sum(wide * wide, axis=1, keepdims=True) + 1e-06)
    unit = wide * image_scale
    r.image_scale[...] = image_scale
    r.image_unit[...] = unit
    r.images[0:128, :] = unit.astype(BF16)

    def image_slot(s, part=None):
        return pl.ds(s * 128, 128) if part is None else pl.ds(s * 128 + 64 * part, 64)

    def image_copy(src, dst, to, part=None):
        return copy(r.images.at[image_slot(src, part)], r.images.at[image_slot(dst, part)], to)

    image_on = [image_copy(0, 1, x_on, 0), image_copy(0, 1, x_on, 1)]
    image_off = [image_copy(0, 3, x_off, 1), image_copy(0, 3, x_off, 0)]
    shared = [image_copy(0, 4, sibling)]

    for half in halves:
        arrived(half, 0, 1)
        arrived(half, 0, 3)
        text_far_first(half)
        text_second(half, 1)
        text_second(half, 3)
    for half in halves:
        arrived(half, 1, 0)
        arrived(half, 3, 0)
        text_far_second(half, 0)

    image_on[0].wait_recv()
    image_far = [image_copy(1, 2, x_on, 0)]
    image_off[0].wait_recv()
    image_far.append(image_copy(3, 2, x_off, 1))
    image_on[1].wait_recv()
    image_off[1].wait_recv()
    shared += [image_copy(1, 5, sibling), image_copy(3, 7, sibling)]

    for half in halves:
        arrived(half, 0, 2)
        text_second(half, 2)

    loads[0].wait()

    def activate(cols):
        value, derivative = gelu_parts(r.latent[:, cols].astype(F32))
        r.active[:, cols] = value.astype(BF16)
        r.slope[:, cols] = derivative

    loop(4, activate)

    for half in halves:
        for p in (1, 3):
            arrived(half, 1, p)
            arrived(half, 3, p)
            text_far_second(half, p)
    for one in image_far:
        one.wait_recv()
    shared.append(image_copy(2, 6, sibling))
    for one in shared:
        one.wait_recv()

    factor = sharp[0]
    shift = offset[0]

    def pair_weights(group):
        texts = pl.ds(group * 512, 512)

        def chunk(rows):
            logits = factor * nt(r.images[rows, :], r.texts[texts, :]) + shift
            r.weights[rows, texts] = (factor / (1.0 + jnp.exp(-logits))).astype(BF16)

        loop(4, chunk)
        if group == 0:
            for half in halves:
                rows = pl.ds(half * 64, 64)
                cols = pl.ds(half * 256, 128)
                logits = factor * nt(r.images[rows, :], r.texts[cols, :]) + shift
                hit = lax.broadcasted_iota(jnp.int32, (64, 128), 0) == lax.broadcasted_iota(
                    jnp.int32, (64, 128), 1
                )
                label = jnp.where(hit, 1.0, -1.0)
                w = -label * factor / (1.0 + jnp.exp(label * logits))
                r.weights[rows, cols] = w.astype(BF16)

    def image_part(group):
        texts = pl.ds(group * 512, 512)

        def chunk(cols):
            part = nn(r.weights[:, texts], r.texts[texts, cols])
            if group:
                part = part + r.image_dz[:, cols]
            r.image_dz[:, cols] = part

        loop(4, chunk)

    pair_weights(0)
    image_part(0)
    for half in halves:
        arrived(half, 1, 2)
        arrived(half, 3, 2)
        text_far_second(half, 2)
    own_columns = r.mapper.at[:, cols_of(hi, core)]
    map_copies = [copy(own_columns, own_columns, beside), copy(own_columns, own_columns, sibling)]
    for group in (1, 3):
        pair_weights(group)
        image_part(group)
    for half in halves:
        for p in range(4):
            arrived(half, 2, p)
    pair_weights(2)
    texts = pl.ds(1024, 512)

    def last_sibling(cols):
        part = nn(r.weights[512:1024, texts], r.texts[texts, cols])
        r.cross_out[:, cols] = (part + r.image_dz[512:1024, cols]).astype(BF16)

    def last_own(cols):
        part = nn(r.weights[0:512, texts], r.texts[texts, cols])
        r.image_dz[0:512, cols] = part + r.image_dz[0:512, cols]

    loop(4, last_sibling)
    cross = copy(r.cross_out, r.cross_in, sibling)
    loop(4, last_own)
    cross.wait_recv()

    def image_block(k, i):
        return image_slot((4 - k) % 4, i), slice(None)

    image_ring = RingSum(net, r.image_sum, image_block, r.image_far, r.image_near, x_on, x_off)

    def image_total(s):
        rows = image_slot(s)
        r.image_sum[rows, :] = (r.image_dz[rows, :] + r.cross_in[rows, :].astype(F32)).astype(BF16)

    for s in (2, 1, 3):
        image_total(s)
    image_ring.start()
    image_total(0)

    def text_grads(group):
        def chunk(j, _):
            rows = cut(group * 512 + j * 256, 256, 256)
            r.text_dz[rows, :] = tn(r.weights[:, rows], r.images[...]).astype(BF16)
            return 0

        lax.fori_loop(0, 2, chunk, 0)

    def second_ring(half):
        def block(k, i):
            return pl.ds(((4 - k) % 4) * 512 + half * 256 + 128 * i, 128), slice(None)

        on, off = rings[half][1]
        return RingSum(net, r.text_dz, block, r.text_far.at[half], r.text_near.at[half], on, off)

    def first_ring(half):
        def block(k, i):
            return pl.ds(half * 256 + ((4 - k) % 4) * 64 + 32 * i, 32), slice(None)

        on, off = rings[half][0]
        return RingSum(net, r.text_sum, block, r.last_far.at[half], r.last_near.at[half], on, off)

    seconds = [second_ring(half) for half in halves]
    firsts = [first_ring(half) for half in halves]

    text_grads(2)
    image_ring.middle()
    text_grads(1)
    text_grads(3)
    for one in seconds:
        one.start()
    image_ring.arrive()
    dz = jnp.concatenate([image_ring.total(0), image_ring.total(1)], axis=0)
    unit = r.image_unit[...]
    grad = r.image_scale[...] * (dz - unit * jnp.sum(unit * dz, axis=1, keepdims=True))
    mine = rows_of(hi, core)
    r.image_grad[mine, :] = grad.astype(BF16)
    block = r.image_grad.at[mine]
    spread = [copy(block, block, across), copy(block, block, sibling)]
    text_grads(0)

    map_copies[0].wait_recv()
    other_columns = r.mapper.at[:, cols_of(hi + 1, core)]
    map_copies.append(copy(other_columns, other_columns, sibling))
    spread[0].wait_recv()
    block = r.image_grad.at[rows_of(hi + 1, core)]
    spread.append(copy(block, block, sibling))
    for one in seconds:
        one.middle()
    spread[1].wait_recv()
    spread[2].wait_recv()
    map_copies[1].wait_recv()
    map_copies[2].wait_recv()

    def back_part(cols):
        r.back[:, cols] = nt(r.image_grad[...], r.mapper[cols, :]).astype(BF16)

    loop(4, back_part)

    def proj_part(cols):
        value = tn(final[:, cols], r.image_grad[:, cols_of(hi, core)]).astype(BF16)
        r.grads[1024:1152, cols] = value[0:128]
        r.grads[2176:2304, cols] = value[128:256]

    loop(4, proj_part)

    def down_part(j, _):
        cols = cut(j * 256, 256, 256)
        r.grads[cut(PART + j * 256, 256, 128), :] = tn(r.active[:, cols], r.back[...]).astype(BF16)
        return 0

    lax.fori_loop(0, 4, down_part, 0)

    first = (net.z, net.x)
    other = (net.x, net.z)
    along = ((z_on, z_off), (x_on, x_off))

    def strip_rows(part, k, i=None):
        start = part * PART + ((first[part] + k) % 4) * STRIP
        return cut(start, STRIP) if i is None else cut(start + i * TILE, TILE)

    def side_columns(part, k):
        return cut(((other[part] + k) % 4) * 256, 256, 256)

    def grad_ring(part):
        def block(k, i):
            return strip_rows(part, k, i), slice(None)

        return RingSum(net, r.grads, block, r.grad_far.at[part], r.grad_near.at[part], *along[part])

    grad_rings = [grad_ring(part) for part in (0, 1)]
    grad_rings[1].start()
    loads[1].wait()

    def pre_part(cols):
        r.pre[:, cols] = (nt(r.back[...], r.second[cols, :]) * r.slope[:, cols]).astype(BF16)

    loop(4, pre_part)
    loads[2].wait()

    def up_part(cols):
        r.grads[cols, :] = tn(r.entry[:, cols], r.pre[...]).astype(BF16)

    loop(4, up_part)
    grad_rings[0].start()

    for half in halves:
        seconds[half].arrive()
        for i in (0, 1):
            r.text_sum[pl.ds(half * 256 + 128 * i, 128), :] = seconds[half].total(i).astype(BF16)
        firsts[half].start()
    grad_rings[1].middle()
    grad_rings[0].middle()
    for half in halves:
        firsts[half].middle()

    def side_to(part, k):
        return net.at(x=k) if part == 0 else net.at(z=k)

    order = (1, 0)
    sides = {}
    for part in order:
        ring = grad_rings[part]
        ring.arrive()
        sides[part] = []
        for n, k in enumerate((2, 1, 3, 0)):
            cols = side_columns(part, k)
            for i in (0, 1):
                rows = pl.ds(i * TILE, TILE)
                total = ring.total(i, cols)
                if k == 0:
                    r.strip[part, rows, :] = total
                else:
                    r.side_out[part, n, rows, :] = total.astype(BF16)
            if k:
                sides[part].append(copy(r.side_out.at[part, n], r.side_in.at[part, n], side_to(part, k)))

    for half in halves:
        firsts[half].arrive()
    dz = jnp.concatenate([firsts[half].total(i) for half in halves for i in (0, 1)], axis=0)
    unit = r.text_unit[...]
    text_out[...] = r.text_scale[...] * (dz - unit * jnp.sum(unit * dz, axis=1, keepdims=True))

    kept = cut(net.lo * TILE, TILE)
    given = cut((1 - net.lo) * TILE, TILE)
    tiles = {}
    for part in order:
        for one in sides[part]:
            one.wait_recv()

        def total(rows):
            value = r.strip[part, rows, :]
            for n in range(3):
                value = value + r.side_in[part, n, rows, :].astype(F32)
            return value

        r.tile_out[part] = total(given).astype(BF16)
        tiles[part] = copy(r.tile_out.at[part], r.tile_in.at[part], pair_lo)
        r.tile[part] = total(kept)

    spread_tile = {}
    for part in order:
        tiles[part].wait_recv()
        rows = cut(part * PART + first[part] * STRIP + net.lo * TILE, TILE)
        cols = side_columns(part, 0)
        r.done[rows, cols] = (r.tile[part] + r.tile_in[part].astype(F32)).astype(BF16)
        block = r.done.at[rows, cols]
        spread_tile[part] = copy(block, block, pair_lo)
    spread_side = {}
    for part in order:
        spread_tile[part].wait_recv()
        block = r.done.at[strip_rows(part, 0), side_columns(part, 0)]
        spread_side[part] = [copy(block, block, side_to(part, k)) for k in (2, 1, 3)]
    spread_strip = {}
    for part in order:
        for one in spread_side[part]:
            one.wait_recv()
        on, off = along[part]
        spread_strip[part] = []
        for i, to in ((0, on), (1, off), (1, on), (0, off)):
            block = r.done.at[strip_rows(part, 0, i)]
            spread_strip[part].append(copy(block, block, to))
    last = []
    for part in order:
        on, off = along[part]
        for i, k, to in ((0, 3, on), (1, 1, off)):
            spread_strip[part][i].wait_recv()
            block = r.done.at[strip_rows(part, k, i)]
            last.append(copy(block, block, to))
    for part in order:
        for one in spread_strip[part][2:]:
            one.wait_recv()
    for one in last:
        one.wait_recv()
    out = pltpu.make_async_copy(r.done, total_out, r.load.at[3])
    out.start()
    for one in net.started:
        one.wait_send()
    out.wait()


SCRATCH = dict(
    columns=((512, 256), BF16),
    texts=((2048, 1024), BF16),
    text_unit=((128, 1024), F32),
    text_scale=((128, 1), F32),
    embed=((128, 1024), BF16),
    image_unit=((128, 1024), F32),
    image_scale=((128, 1), F32),
    images=((1024, 1024), BF16),
    mapper=((1024, 1024), BF16),
    latent=((512, 1024), BF16),
    second=((1024, 1024), BF16),
    entry=((512, 1024), BF16),
    active=((512, 1024), BF16),
    slope=((512, 1024), F32),
    weights=((1024, 2048), BF16),
    image_dz=((1024, 1024), F32),
    cross_out=((512, 1024), BF16),
    cross_in=((512, 1024), BF16),
    image_sum=((512, 1024), BF16),
    image_far=((2, 64, 1024), BF16),
    image_near=((2, 128, 1024), BF16),
    text_dz=((2048, 1024), BF16),
    text_far=((2, 2, 128, 1024), BF16),
    text_near=((2, 2, 256, 1024), BF16),
    text_sum=((512, 1024), BF16),
    last_far=((2, 2, 32, 1024), BF16),
    last_near=((2, 2, 64, 1024), BF16),
    image_grad=((512, 1024), BF16),
    back=((512, 1024), BF16),
    pre=((512, 1024), BF16),
    grads=((2 * PART, 1024), BF16),
    done=((2 * PART, 1024), BF16),
    grad_far=((2, 2, TILE, 1024), BF16),
    grad_near=((2, 2, STRIP, 1024), BF16),
    strip=((2, STRIP, 256), F32),
    side_out=((2, 3, STRIP, 256), BF16),
    side_in=((2, 3, STRIP, 256), BF16),
    tile=((2, TILE, 256), F32),
    tile_out=((2, TILE, 256), BF16),
    tile_in=((2, TILE, 256), BF16),
    send=((COPIES,), None),
    recv=((COPIES,), None),
    load=((4,), None),
)


def step(sharp, offset, caption, final, mapper, latent, second, entry):
    return pl.pallas_call(
        step_kernel,
        name="pairs_and_weight_grads",
        out_shape=(
            jax.ShapeDtypeStruct((2 * PART, 1024), BF16),
            jax.ShapeDtypeStruct((128, 1024), F32),
        ),
        in_specs=[SMEM, SMEM, VMEM, VMEM, VMEM, ANY, ANY, ANY],
        out_specs=(ANY, VMEM),
        scratch_shapes=[
            pltpu.SemaphoreType.DMA(shape) if kind is None else pltpu.VMEM(shape, kind)
            for shape, kind in SCRATCH.values()
        ],
        compiler_params=pltpu.CompilerParams(
            collective_id=0, has_side_effects=True, vmem_limit_bytes=60 * 2**20
        ),
    )(sharp, offset, caption, final, mapper, latent, second, entry)


def lion_block(weight, moment, grad, axis):
    grad = grad.astype(F32)
    moment = moment.astype(F32)
    blend = 0.9 * moment + 0.1 * grad
    square = blend * blend
    floor = 0.0625 * (jnp.mean(square, axis=axis, keepdims=True) + 1e-06)
    update = blend * lax.rsqrt(square + floor) + weight.astype(F32)
    return update.astype(BF16), (0.99 * moment + 0.01 * grad).astype(BF16)


def lion_kernel(
    g_up, g_down, g_proj_a, g_proj_b, w_up, w_down, w_proj, m_up, m_down, m_proj,
    u_up, u_down, u_proj, r_up, r_down, r_proj,
):
    u_up[...], r_up[...] = lion_block(w_up[...], m_up[...], g_up[...], 0)
    u_down[...], r_down[...] = lion_block(w_down[...], m_down[...], g_down[...], 1)

    @pl.when(pl.program_id(0) == 0)
    def _():
        grad = jnp.concatenate(
            [g[:, 256 * i : 256 * (i + 1)] for i in range(4) for g in (g_proj_a, g_proj_b)], axis=0
        )
        u_proj[...], r_proj[...] = lion_block(w_proj[...], m_proj[...], grad, 0)


def lion(total, weights, moments):
    column = pl.BlockSpec((1024, 128), lambda i: (0, i))
    row = pl.BlockSpec((128, 1024), lambda i: (i, 0))
    whole = pl.BlockSpec((1024, 256), lambda i: (0, 0))
    like = [column, row, whole]
    square = jax.ShapeDtypeStruct((1024, 1024), BF16)
    narrow = jax.ShapeDtypeStruct((1024, 256), BF16)
    return pl.pallas_call(
        lion_kernel,
        name="lion",
        grid=(8,),
        out_shape=(square, square, narrow, square, square, narrow),
        in_specs=[
            column,
            pl.BlockSpec((128, 1024), lambda i: (9 + i, 0)),
            pl.BlockSpec((128, 1024), lambda i: (8, 0)),
            pl.BlockSpec((128, 1024), lambda i: (17, 0)),
        ]
        + like
        + like,
        out_specs=tuple(like + like),
        compiler_params=pltpu.CompilerParams(vmem_limit_bytes=60 * 2**20),
    )(total, total, total, total, *weights, *moments)


def per_device(
    vision_layer_entry,
    latent_preact_values,
    final_layer_result,
    caption_vectors_raw,
    sharpness_factor,
    offset_term,
    first_feedforward_matrix,
    second_feedforward_matrix,
    mapper_matrix,
    first_matrix_velocity,
    second_matrix_velocity,
    mapper_velocity,
):
    total, text_grad = step(
        sharpness_factor,
        offset_term,
        caption_vectors_raw,
        final_layer_result,
        mapper_matrix,
        latent_preact_values,
        second_feedforward_matrix,
        vision_layer_entry,
    )
    results = lion(
        total,
        (first_feedforward_matrix, second_feedforward_matrix, mapper_matrix),
        (first_matrix_velocity, second_matrix_velocity, mapper_velocity),
    )
    return (*results, text_grad)


def solution(mesh):
    return jax.shard_map(
        per_device,
        mesh=mesh,
        in_specs=(
            P("dp", None),
            P("dp", "mp"),
            P("dp", None),
            P(("dp", "mp"), None),
            P(),
            P(),
            P(None, "mp"),
            P("mp", None),
            P(None, "mp"),
            P(None, "mp"),
            P("mp", None),
            P(None, "mp"),
        ),
        out_specs=(
            P(None, "mp"),
            P("mp", None),
            P(None, "mp"),
            P(None, "mp"),
            P("mp", None),
            P(None, "mp"),
            P(("dp", "mp"), None),
        ),
        check_vma=False,
    )
```

time: 1370 us -> 178 us (0.13)
  waiting for transfers between devices: 1040 us -> 0 us
  matrix products: 206 us -> 0 us
  Pallas kernels: 0 us -> 174 us
  local copies, waits for them, and re-layouts: 67 us -> 0.8 us
  other arithmetic: 29.2 us -> 0 us
    ppermute x64 -> x0, waiting for transfers between devices: 610 us -> none  [passed_along(): return lax.ppermute(block, axis, route)]
    psum x3 -> x0, waiting for transfers between devices: 408 us -> none  [the longest x1 306 us: per_device(): lax.psum(grad_up.astype(jnp.bfloat16), 'dp').astype(jnp.float32)]
    dot_general x101 -> x0, matrix products: 206 us -> none  [the longest x32 98.1 us: couple_derivs(): lax.dot_general(vision_members, caption_members, (((1,), (1,)), ((), ()))...]
    pallas_call x0 -> x2, Pallas kernels: none -> 174 us  [the longest x1 160 us: step(): pl.pallas_call(step_kernel, name='pairs_and_weight_grads', out_shape=(jax...]
    unnamed x42 -> x3, local copies, waits for them, and re-layouts: 35.6 us -> 0.8 us
    while x96 -> x0, local copies, waits for them, and re-layouts: 30.6 us -> none
    all_gather x1 -> x0, waiting for transfers between devices: 22.8 us -> none  [per_device(): gathered = lax.all_gather(embedded, 'mp', axis=1, tiled=True)]
    convert_element_type x6 -> x0, other arithmetic: 16.5 us -> none  [the longest x3 11.9 us: lion_step(): renewed = (0.99 * moment_wide + 0.01 * grad).astype(jnp.bfloat16)]
  transfers between devices with their start and end apart: 68 -> 0, of which waited for: 36 -> 0; matrix products, arithmetic and copies ran while one was open for 3% -> 0% of each run, Pallas kernels for 0% -> 0%
where the time goes in v3:
time: 178 us; the launch traced here: 177 us
  Pallas kernels  174 us (98%)
  between operations  1.96 us (1%)
    pallas_call x1, Pallas kernels, step(): pl.pallas_call(step_kernel, name='pairs_and_weight_grads', out_shape=(jax...  160 us
    pallas_call x1, Pallas kernels, lion(): pl.pallas_call(lion_kernel, name='lion', grid=(8,), out_shape=(square, sq...  14.2 us

profile of v3, /device:TPU:0, one launch (start us, length us, event | category | flops | bytes accessed | tf_op | source)
XLA Modules:
  0.0 177.1 jit_solution(3425068809875930573)
XLA Ops:
  1.9 160.2 %pairs_and_weight_grads.1 = (bf16[2304,1024]{1,0:T(8,128)(2,1)}, f32[128,1024]{1,0:T(8,128)}) custom-call(f32[1]{0:T(128)S(6)} %copy.20.sharp, f32[1]{0:T(128)S(6)} %copy.21.offset, bf16[128,1024]{1,0:T(8,128)(2,1)} %caption.1, bf16[512,1024]{1,0:T(8,128)(2,1)} %final.1, bf16[1024,256]{1,0:T(8,128)(2,1)} %w_proj.1, bf16[512,1024]{1,0:T(8,128)(2,1)} %latent_in.1, ...), custom_call_target="tpu_custom_call" | custom-call | tf_op jit(solution)/shard_map/pairs_and_weight_grads/pallas_call | solution.py:617
  162.1 0.0 copy-start
  162.1 14.2 %lion.1 = (bf16[1024,1024]{1,0:T(8,128)(2,1)}, bf16[1024,1024]{1,0:T(8,128)(2,1)}, bf16[1024,256]{1,0:T(8,128)(2,1)}, bf16[1024,1024]{1,0:T(8,128)(2,1)}, bf16[1...) custom-call(bf16[2304,1024]{1,0:T(8,128)(2,1)} %get-tuple-element.15.g_up.g_down.g_proj_a.g_proj_b, ...), custom_call_target="tpu_custom_call" | custom-call | tf_op jit(solution)/shard_map/lion/pallas_call | solution.py:668
  176.3 0.0 copy-done
  176.3 0.8 copy.22
Async XLA Ops:
  162.1 14.2 %copy-start = (f32[128,1024]{1,0:T(8,128)S(1)}, f32[128,1024]{1,0:T(8,128)}, u32[]{:S(2)}) copy-start(f32[128,1024]{1,0:T(8,128)} %get-tuple-element.36) | copy-start | bytes 1572868

commit v4 on v3

--- a/solution.py
+++ b/solution.py
@@ -17,7 +17,8 @@
 PART = 1152
 STRIP = 288
 TILE = 144
-COPIES = 160
+COPIES = 176
+PLACE = (0, 1, 3, 2)
 
 
 def nn(a, b):
@@ -93,11 +94,18 @@
         return self.near_in.at[k, pl.ds(i * self.half, self.half)]
 
     def start(self):
+        self.start_far()
+        self.start_near()
+
+    def start_far(self):
         copy, src, block = self.links.copy, self.src, self.block
         self.far = [
             copy(src.at[block(2, 0)], self.far_in.at[0], self.on),
             copy(src.at[block(2, 1)], self.far_in.at[1], self.off),
         ]
+
+    def start_near(self):
+        copy, src, block = self.links.copy, self.src, self.block
         self.near = [
             copy(src.at[block(1, 1)], self.part(0, 1), self.on),
             copy(src.at[block(3, 0)], self.part(1, 0), self.off),
@@ -114,14 +122,14 @@
         for one in self.near:
             one.wait_recv()
 
-    def total(self, i, cols=slice(None)):
+    def total(self, i, cols=None, near=slice(None)):
         rows = pl.ds(i * self.half, self.half)
         at = self.block(0, i)
-        own = self.src[at] if cols == slice(None) else self.src[at[0], cols]
+        own = self.src[at] if cols is None else self.src[at[0], cols]
         return (
             own.astype(F32)
-            + self.near_in[0, rows, cols].astype(F32)
-            + self.near_in[1, rows, cols].astype(F32)
+            + self.near_in[0, rows, near].astype(F32)
+            + self.near_in[1, rows, near].astype(F32)
         )
 
 
@@ -186,7 +194,7 @@
     rings = (((y_on, y_off), (z_on, z_off)), ((z_on, z_off), (y_on, y_off)))
 
     def slot(half, s, p, part=None):
-        start = s * 512 + half * 256 + p * 64
+        start = PLACE[s] * 512 + half * 256 + p * 64
         return pl.ds(start, 64) if part is None else pl.ds(start + 32 * part, 32)
 
     got = {}
@@ -220,53 +228,105 @@
         text_copy(half, (3, p), (2, p), off, 1)
 
     halves = (0, 1)
-    for half in halves:
-        text_first(half)
-    for half in halves:
-        text_second(half, 0)
+    text_first(1)
+    text_second(0, 0)
 
     for one in embed_copies:
         one.wait_recv()
     wide = r.embed[...].astype(F32)
     image_scale = lax.rsqrt(jnp.sum(wide * wide, axis=1, keepdims=True) + 1e-06)
     unit = wide * image_scale
+    r.images[0:128, :] = unit.astype(BF16)
+
+    def image_slot(s, part=None):
+        return pl.ds(s * 128, 128) if part is None else pl.ds(s * 128 + 64 * part, 64)
+
+    def image_copy(src, dst, to, part=None):
+        return copy(r.images.at[image_slot(src, part)], r.images.at[image_slot(dst, part)], to)
+
+    image_on = [image_copy(0, 1, x_on, 0)]
+    image_off = [image_copy(0, 3, x_off, 1)]
+    image_on.append(image_copy(0, 1, x_on, 1))
+    image_off.append(image_copy(0, 3, x_off, 0))
+    text_first(0)
+    text_second(1, 0)
+    shared = [image_copy(0, 4, sibling)]
     r.image_scale[...] = image_scale
     r.image_unit[...] = unit
-    r.images[0:128, :] = unit.astype(BF16)
-
-    def image_slot(s, part=None):
-        return pl.ds(s * 128, 128) if part is None else pl.ds(s * 128 + 64 * part, 64)
-
-    def image_copy(src, dst, to, part=None):
-        return copy(r.images.at[image_slot(src, part)], r.images.at[image_slot(dst, part)], to)
-
-    image_on = [image_copy(0, 1, x_on, 0), image_copy(0, 1, x_on, 1)]
-    image_off = [image_copy(0, 3, x_off, 1), image_copy(0, 3, x_off, 0)]
-    shared = [image_copy(0, 4, sibling)]
-
-    for half in halves:
+
+    for half in (1, 0):
         arrived(half, 0, 1)
         arrived(half, 0, 3)
         text_far_first(half)
         text_second(half, 1)
         text_second(half, 3)
-    for half in halves:
+        if half == 1:
+            image_on[0].wait_recv()
+            image_far = [image_copy(1, 2, x_on, 0)]
+            image_off[0].wait_recv()
+            image_far.append(image_copy(3, 2, x_off, 1))
+
+    for half in (0, 1):
         arrived(half, 1, 0)
         arrived(half, 3, 0)
         text_far_second(half, 0)
-
-    image_on[0].wait_recv()
-    image_far = [image_copy(1, 2, x_on, 0)]
-    image_off[0].wait_recv()
-    image_far.append(image_copy(3, 2, x_off, 1))
     image_on[1].wait_recv()
     image_off[1].wait_recv()
     shared += [image_copy(1, 5, sibling), image_copy(3, 7, sibling)]
-
-    for half in halves:
+    for half in (1, 0):
         arrived(half, 0, 2)
         text_second(half, 2)
-
+    for one in image_far:
+        one.wait_recv()
+    shared.append(image_copy(2, 6, sibling))
+
+    for one in shared:
+        one.wait_recv()
+
+    factor = sharp[0]
+    shift = offset[0]
+
+    def pair_weights(s, first=0, count=1024):
+        texts = pl.ds(PLACE[s] * 512, 512)
+
+        def chunk(rows):
+            logits = factor * nt(r.images[rows, :], r.texts[texts, :]) + shift
+            r.weights[rows, texts] = (factor / (1.0 + jnp.exp(-logits))).astype(BF16)
+
+        def run(j, _):
+            chunk(cut(first + j * 512, 512, 512))
+            return 0
+
+        if count == 512:
+            chunk(pl.ds(first, 512))
+        else:
+            lax.fori_loop(0, 2, run, 0)
+
+    def matching_pairs():
+        for half in halves:
+            rows = pl.ds(half * 64, 64)
+            cols = pl.ds(half * 256, 128)
+            logits = factor * nt(r.images[rows, :], r.texts[cols, :]) + shift
+            hit = lax.broadcasted_iota(jnp.int32, (64, 128), 0) == lax.broadcasted_iota(
+                jnp.int32, (64, 128), 1
+            )
+            label = jnp.where(hit, 1.0, -1.0)
+            w = -label * factor / (1.0 + jnp.exp(label * logits))
+            r.weights[rows, cols] = w.astype(BF16)
+
+    near_texts = pl.ds(0, 1536)
+    far_texts = pl.ds(1536, 512)
+
+    def image_part(cols):
+        r.image_dz[:, cols] = nn(r.weights[:, near_texts], r.texts[near_texts, cols])
+
+    pair_weights(0)
+    matching_pairs()
+    for p in (1, 3):
+        for half in halves:
+            arrived(half, 1, p)
+            arrived(half, 3, p)
+            text_far_second(half, p)
     loads[0].wait()
 
     def activate(cols):
@@ -275,80 +335,32 @@
         r.slope[:, cols] = derivative
 
     loop(4, activate)
-
-    for half in halves:
-        for p in (1, 3):
-            arrived(half, 1, p)
-            arrived(half, 3, p)
-            text_far_second(half, p)
-    for one in image_far:
-        one.wait_recv()
-    shared.append(image_copy(2, 6, sibling))
-    for one in shared:
-        one.wait_recv()
-
-    factor = sharp[0]
-    shift = offset[0]
-
-    def pair_weights(group):
-        texts = pl.ds(group * 512, 512)
-
-        def chunk(rows):
-            logits = factor * nt(r.images[rows, :], r.texts[texts, :]) + shift
-            r.weights[rows, texts] = (factor / (1.0 + jnp.exp(-logits))).astype(BF16)
-
-        loop(4, chunk)
-        if group == 0:
-            for half in halves:
-                rows = pl.ds(half * 64, 64)
-                cols = pl.ds(half * 256, 128)
-                logits = factor * nt(r.images[rows, :], r.texts[cols, :]) + shift
-                hit = lax.broadcasted_iota(jnp.int32, (64, 128), 0) == lax.broadcasted_iota(
-                    jnp.int32, (64, 128), 1
-                )
-                label = jnp.where(hit, 1.0, -1.0)
-                w = -label * factor / (1.0 + jnp.exp(label * logits))
-                r.weights[rows, cols] = w.astype(BF16)
-
-    def image_part(group):
-        texts = pl.ds(group * 512, 512)
-
-        def chunk(cols):
-            part = nn(r.weights[:, texts], r.texts[texts, cols])
-            if group:
-                part = part + r.image_dz[:, cols]
-            r.image_dz[:, cols] = part
-
-        loop(4, chunk)
-
-    pair_weights(0)
-    image_part(0)
     for half in halves:
         arrived(half, 1, 2)
         arrived(half, 3, 2)
         text_far_second(half, 2)
+    pair_weights(1)
+    pair_weights(3)
     own_columns = r.mapper.at[:, cols_of(hi, core)]
     map_copies = [copy(own_columns, own_columns, beside), copy(own_columns, own_columns, sibling)]
-    for group in (1, 3):
-        pair_weights(group)
-        image_part(group)
-    for half in halves:
-        for p in range(4):
+    loop(4, image_part)
+    for p in range(4):
+        for half in halves:
             arrived(half, 2, p)
-    pair_weights(2)
-    texts = pl.ds(1024, 512)
 
     def last_sibling(cols):
-        part = nn(r.weights[512:1024, texts], r.texts[texts, cols])
+        part = nn(r.weights[512:1024, far_texts], r.texts[far_texts, cols])
         r.cross_out[:, cols] = (part + r.image_dz[512:1024, cols]).astype(BF16)
 
     def last_own(cols):
-        part = nn(r.weights[0:512, texts], r.texts[texts, cols])
+        part = nn(r.weights[0:512, far_texts], r.texts[far_texts, cols])
         r.image_dz[0:512, cols] = part + r.image_dz[0:512, cols]
 
-    loop(4, last_sibling)
+    pair_weights(2, 512, 512)
+    loop(2, last_sibling, 512)
     cross = copy(r.cross_out, r.cross_in, sibling)
-    loop(4, last_own)
+    pair_weights(2, 0, 512)
+    loop(2, last_own, 512)
     cross.wait_recv()
 
     def image_block(k, i):
@@ -360,22 +372,21 @@
         rows = image_slot(s)
         r.image_sum[rows, :] = (r.image_dz[rows, :] + r.cross_in[rows, :].astype(F32)).astype(BF16)
 
-    for s in (2, 1, 3):
-        image_total(s)
-    image_ring.start()
+    image_total(2)
+    image_ring.start_far()
+    image_total(1)
+    image_total(3)
+    image_ring.start_near()
     image_total(0)
 
-    def text_grads(group):
-        def chunk(j, _):
-            rows = cut(group * 512 + j * 256, 256, 256)
+    def text_grads(half, *groups):
+        for s in groups:
+            rows = pl.ds(PLACE[s] * 512 + half * 256, 256)
             r.text_dz[rows, :] = tn(r.weights[:, rows], r.images[...]).astype(BF16)
-            return 0
-
-        lax.fori_loop(0, 2, chunk, 0)
 
     def second_ring(half):
         def block(k, i):
-            return pl.ds(((4 - k) % 4) * 512 + half * 256 + 128 * i, 128), slice(None)
+            return pl.ds(PLACE[(4 - k) % 4] * 512 + half * 256 + 128 * i, 128), slice(None)
 
         on, off = rings[half][1]
         return RingSum(net, r.text_dz, block, r.text_far.at[half], r.text_near.at[half], on, off)
@@ -390,12 +401,12 @@
     seconds = [second_ring(half) for half in halves]
     firsts = [first_ring(half) for half in halves]
 
-    text_grads(2)
+    text_grads(0, 2, 1, 3)
+    seconds[0].start()
+    text_grads(1, 2)
     image_ring.middle()
-    text_grads(1)
-    text_grads(3)
-    for one in seconds:
-        one.start()
+    text_grads(1, 1, 3)
+    text_grads(0, 0)
     image_ring.arrive()
     dz = jnp.concatenate([image_ring.total(0), image_ring.total(1)], axis=0)
     unit = r.image_unit[...]
@@ -404,103 +415,214 @@
     r.image_grad[mine, :] = grad.astype(BF16)
     block = r.image_grad.at[mine]
     spread = [copy(block, block, across), copy(block, block, sibling)]
-    text_grads(0)
+    text_grads(1, 0)
 
     map_copies[0].wait_recv()
     other_columns = r.mapper.at[:, cols_of(hi + 1, core)]
     map_copies.append(copy(other_columns, other_columns, sibling))
+    seconds[0].middle()
+    map_copies[1].wait_recv()
+    map_copies[2].wait_recv()
+    spread[1].wait_recv()
+
+    def back_rows(h):
+        rows = cut((h % 2) * 256, 256, 256)
+
+        def part(cols):
+            r.back[rows, cols] = nt(r.image_grad[rows, :], r.mapper[cols, :]).astype(BF16)
+
+        loop(2, part, 512)
+
+    back_rows(hi)
     spread[0].wait_recv()
     block = r.image_grad.at[rows_of(hi + 1, core)]
     spread.append(copy(block, block, sibling))
-    for one in seconds:
-        one.middle()
-    spread[1].wait_recv()
+    seconds[1].start()
     spread[2].wait_recv()
-    map_copies[1].wait_recv()
-    map_copies[2].wait_recv()
-
-    def back_part(cols):
-        r.back[:, cols] = nt(r.image_grad[...], r.mapper[cols, :]).astype(BF16)
-
-    loop(4, back_part)
+    back_rows(hi + 1)
+
+    first = (net.z, net.x)
+    other = (net.x, net.z)
+    along = ((z_on, z_off), (x_on, x_off))
+    wide = (pl.ds(0, 512), pl.ds(512, 512))
+
+    def strip_rows(part, k, i=None):
+        start = part * PART + ((first[part] + k) % 4) * STRIP
+        return cut(start, STRIP) if i is None else cut(start + i * TILE, TILE)
+
+    def side_columns(part, c, k):
+        return cut(c * 512 + ((other[part] + k) % 4) * 128, 128, 128)
+
+    def grad_ring(part, c):
+        def block(k, i):
+            return strip_rows(part, k, i), wide[c]
+
+        n = part * 2 + c
+        return RingSum(net, r.grads, block, r.grad_far.at[n], r.grad_near.at[n], *along[part])
+
+    chains = ((1, 0), (1, 1), (0, 0), (0, 1))
+    grad_rings = {chain: grad_ring(*chain) for chain in chains}
 
     def proj_part(cols):
         value = tn(final[:, cols], r.image_grad[:, cols_of(hi, core)]).astype(BF16)
         r.grads[1024:1152, cols] = value[0:128]
         r.grads[2176:2304, cols] = value[128:256]
 
+    def down(c):
+        def part(j, _):
+            cols = cut(j * 512, 512, 512)
+            value = tn(r.active[:, cols], r.back[:, wide[c]])
+            r.grads[cut(PART + j * 512, 512, 128), wide[c]] = value.astype(BF16)
+            return 0
+
+        lax.fori_loop(0, 2, part, 0)
+
+    def up(c):
+        value = nt(r.back[...], r.second[wide[c], :]) * r.slope[:, wide[c]]
+        r.pre[:, wide[c]] = value.astype(BF16)
+
+        def part(rows):
+            r.grads[rows, wide[c]] = tn(r.entry[:, rows], r.pre[:, wide[c]]).astype(BF16)
+
+        loop(2, part, 512)
+
     loop(4, proj_part)
-
-    def down_part(j, _):
-        cols = cut(j * 256, 256, 256)
-        r.grads[cut(PART + j * 256, 256, 128), :] = tn(r.active[:, cols], r.back[...]).astype(BF16)
-        return 0
-
-    lax.fori_loop(0, 4, down_part, 0)
-
-    first = (net.z, net.x)
-    other = (net.x, net.z)
-    along = ((z_on, z_off), (x_on, x_off))
-
-    def strip_rows(part, k, i=None):
-        start = part * PART + ((first[part] + k) % 4) * STRIP
-        return cut(start, STRIP) if i is None else cut(start + i * TILE, TILE)
-
-    def side_columns(part, k):
-        return cut(((other[part] + k) % 4) * 256, 256, 256)
-
-    def grad_ring(part):
-        def block(k, i):
-            return strip_rows(part, k, i), slice(None)
-
-        return RingSum(net, r.grads, block, r.grad_far.at[part], r.grad_near.at[part], *along[part])
-
-    grad_rings = [grad_ring(part) for part in (0, 1)]
-    grad_rings[1].start()
+    down(0)
+    grad_rings[1, 0].start()
     loads[1].wait()
-
-    def pre_part(cols):
-        r.pre[:, cols] = (nt(r.back[...], r.second[cols, :]) * r.slope[:, cols]).astype(BF16)
-
-    loop(4, pre_part)
     loads[2].wait()
-
-    def up_part(cols):
-        r.grads[cols, :] = tn(r.entry[:, cols], r.pre[...]).astype(BF16)
-
-    loop(4, up_part)
-    grad_rings[0].start()
-
-    for half in halves:
+    up(0)
+    grad_rings[0, 0].start()
+    down(1)
+    grad_rings[1, 0].middle()
+    grad_rings[1, 1].start()
+    up(1)
+    grad_rings[0, 0].middle()
+    grad_rings[0, 1].start()
+
+    def text_first_sum(half):
         seconds[half].arrive()
         for i in (0, 1):
             r.text_sum[pl.ds(half * 256 + 128 * i, 128), :] = seconds[half].total(i).astype(BF16)
         firsts[half].start()
-    grad_rings[1].middle()
-    grad_rings[0].middle()
-    for half in halves:
-        firsts[half].middle()
+
+    seconds[1].middle()
+    text_first_sum(0)
 
     def side_to(part, k):
         return net.at(x=k) if part == 0 else net.at(z=k)
 
-    order = (1, 0)
     sides = {}
-    for part in order:
-        ring = grad_rings[part]
+
+    def side(part, c):
+        ring = grad_rings[part, c]
         ring.arrive()
-        sides[part] = []
+        sides[part, c] = []
         for n, k in enumerate((2, 1, 3, 0)):
-            cols = side_columns(part, k)
+            cols = side_columns(part, c, k)
+            near = cut(((other[part] + k) % 4) * 128, 128, 128)
             for i in (0, 1):
                 rows = pl.ds(i * TILE, TILE)
-                total = ring.total(i, cols)
+                total = ring.total(i, cols, near)
                 if k == 0:
-                    r.strip[part, rows, :] = total
+                    r.strip[part, rows, wide_tile[c]] = total
                 else:
-                    r.side_out[part, n, rows, :] = total.astype(BF16)
+                    r.side_out[part, n, rows, wide_tile[c]] = total.astype(BF16)
             if k:
-                sides[part].append(copy(r.side_out.at[part, n], r.side_in.at[part, n], side_to(part, k)))
+                sides[part, c].append(
+                    copy(
+                        r.side_out.at[part, n, :, wide_tile[c]],
+                        r.side_in.at[part, n, :, wide_tile[c]],
+                        side_to(part, k),
+                    )
+                )
+
+    wide_tile = (pl.ds(0, 128), pl.ds(128, 128))
+    side(1, 0)
+    grad_rings[1, 1].middle()
+    firsts[0].middle()
+    side(0, 0)
+    grad_rings[0, 1].middle()
+
+    kept = cut(net.lo * TILE, TILE)
+    given = cut((1 - net.lo) * TILE, TILE)
+    tiles = {}
+
+    def tile(part, c):
+        for one in sides[part, c]:
+            one.wait_recv()
+        at = wide_tile[c]
+
+        def total(rows):
+            value = r.strip[part, rows, at]
+            for n in range(3):
+                value = value + r.side_in[part, n, rows, at].astype(F32)
+            return value
+
+        r.tile_out[part, :, at] = total(given).astype(BF16)
+        tiles[part, c] = copy(r.tile_out.at[part, :, at], r.tile_in.at[part, :, at], pair_lo)
+        r.tile[part, :, at] = total(kept)
+
+    spread_tile = {}
+
+    def back_tile(part, c):
+        tiles[part, c].wait_recv()
+        at = wide_tile[c]
+        rows = cut(part * PART + first[part] * STRIP + net.lo * TILE, TILE)
+        cols = side_columns(part, c, 0)
+        r.done[rows, cols] = (r.tile[part, :, at] + r.tile_in[part, :, at].astype(F32)).astype(BF16)
+        block = r.done.at[rows, cols]
+        spread_tile[part, c] = copy(block, block, pair_lo)
+
+    spread_side = {}
+
+    def back_side(part, c):
+        spread_tile[part, c].wait_recv()
+        block = r.done.at[strip_rows(part, 0), side_columns(part, c, 0)]
+        spread_side[part, c] = [copy(block, block, side_to(part, k)) for k in (2, 1, 3)]
+
+    spread_strip = {}
+
+    def back_strip(part, c):
+        for one in spread_side[part, c]:
+            one.wait_recv()
+        on, off = along[part]
+        spread_strip[part, c] = []
+        for i, to in ((0, on), (1, off), (1, on), (0, off)):
+            block = r.done.at[strip_rows(part, 0, i), wide[c]]
+            spread_strip[part, c].append(copy(block, block, to))
+
+    last = []
+
+    def back_far(part, c):
+        on, off = along[part]
+        for i, k, to in ((0, 3, on), (1, 1, off)):
+            spread_strip[part, c][i].wait_recv()
+            block = r.done.at[strip_rows(part, k, i), wide[c]]
+            last.append(copy(block, block, to))
+
+    tile(1, 0)
+    side(1, 1)
+    tile(0, 0)
+    side(0, 1)
+    back_tile(1, 0)
+    back_tile(0, 0)
+    tile(1, 1)
+    back_side(1, 0)
+    tile(0, 1)
+    back_side(0, 0)
+    back_tile(1, 1)
+    back_tile(0, 1)
+    back_strip(1, 0)
+    back_side(1, 1)
+    back_strip(0, 0)
+    back_side(0, 1)
+    text_first_sum(1)
+    back_far(1, 0)
+    back_far(0, 0)
+    back_strip(1, 1)
+    back_strip(0, 1)
+    firsts[1].middle()
 
     for half in halves:
         firsts[half].arrive()
@@ -508,54 +630,10 @@
     unit = r.text_unit[...]
     text_out[...] = r.text_scale[...] * (dz - unit * jnp.sum(unit * dz, axis=1, keepdims=True))
 
-    kept = cut(net.lo * TILE, TILE)
-    given = cut((1 - net.lo) * TILE, TILE)
-    tiles = {}
-    for part in order:
-        for one in sides[part]:
-            one.wait_recv()
-
-        def total(rows):
-            value = r.strip[part, rows, :]
-            for n in range(3):
-                value = value + r.side_in[part, n, rows, :].astype(F32)
-            return value
-
-        r.tile_out[part] = total(given).astype(BF16)
-        tiles[part] = copy(r.tile_out.at[part], r.tile_in.at[part], pair_lo)
-        r.tile[part] = total(kept)
-
-    spread_tile = {}
-    for part in order:
-        tiles[part].wait_recv()
-        rows = cut(part * PART + first[part] * STRIP + net.lo * TILE, TILE)
-        cols = side_columns(part, 0)
-        r.done[rows, cols] = (r.tile[part] + r.tile_in[part].astype(F32)).astype(BF16)
-        block = r.done.at[rows, cols]
-        spread_tile[part] = copy(block, block, pair_lo)
-    spread_side = {}
-    for part in order:
-        spread_tile[part].wait_recv()
-        block = r.done.at[strip_rows(part, 0), side_columns(part, 0)]
-        spread_side[part] = [copy(block, block, side_to(part, k)) for k in (2, 1, 3)]
-    spread_strip = {}
-    for part in order:
-        for one in spread_side[part]:
-            one.wait_recv()
-        on, off = along[part]
-        spread_strip[part] = []
-        for i, to in ((0, on), (1, off), (1, on), (0, off)):
-            block = r.done.at[strip_rows(part, 0, i)]
-            spread_strip[part].append(copy(block, block, to))
-    last = []
-    for part in order:
-        on, off = along[part]
-        for i, k, to in ((0, 3, on), (1, 1, off)):
-            spread_strip[part][i].wait_recv()
-            block = r.done.at[strip_rows(part, k, i)]
-            last.append(copy(block, block, to))
-    for part in order:
-        for one in spread_strip[part][2:]:
+    back_far(1, 1)
+    back_far(0, 1)
+    for chain in chains:
+        for one in spread_strip[chain][2:]:
             one.wait_recv()
     for one in last:
         one.wait_recv()
@@ -599,8 +677,8 @@
     pre=((512, 1024), BF16),
     grads=((2 * PART, 1024), BF16),
     done=((2 * PART, 1024), BF16),
-    grad_far=((2, 2, TILE, 1024), BF16),
-    grad_near=((2, 2, STRIP, 1024), BF16),
+    grad_far=((4, 2, TILE, 512), BF16),
+    grad_near=((4, 2, STRIP, 512), BF16),
     strip=((2, STRIP, 256), F32),
     side_out=((2, 3, STRIP, 256), BF16),
     side_in=((2, 3, STRIP, 256), BF16),

time: 178 us -> 160 us (0.90)
  Pallas kernels: 174 us -> 157 us
    pallas_call x1, Pallas kernels: 160 us -> 142 us  [step(): pl.pallas_call(step_kernel, name='pairs_and_weight_grads', out_shape=(jax...]
where the time goes in v4:
time: 160 us; the launch traced here: 159 us
  Pallas kernels  157 us (98%)
  between operations  1.96 us (1%)
    pallas_call x1, Pallas kernels, step(): pl.pallas_call(step_kernel, name='pairs_and_weight_grads', out_shape=(jax...  142 us
    pallas_call x1, Pallas kernels, lion(): pl.pallas_call(lion_kernel, name='lion', grid=(8,), out_shape=(square, sq...  14.2 us

profile of v4, /device:TPU:0, one launch (start us, length us, event | category | flops | bytes accessed | tf_op | source)
XLA Modules:
  0.0 159.4 jit_solution(10531961265519634145)
XLA Ops:
  1.9 142.4 %pairs_and_weight_grads.1 = (bf16[2304,1024]{1,0:T(8,128)(2,1)}, f32[128,1024]{1,0:T(8,128)}) custom-call(f32[1]{0:T(128)S(6)} %copy.20.sharp, f32[1]{0:T(128)S(6)} %copy.21.offset, bf16[128,1024]{1,0:T(8,128)(2,1)} %caption.1, bf16[512,1024]{1,0:T(8,128)(2,1)} %final.1, bf16[1024,256]{1,0:T(8,128)(2,1)} %w_proj.1, bf16[512,1024]{1,0:T(8,128)(2,1)} %latent_in.1, ...), custom_call_target="tpu_custom_call" | custom-call | tf_op jit(solution)/shard_map/pairs_and_weight_grads/pallas_call | solution.py:695
  144.4 0.0 copy-start
  144.4 14.2 %lion.1 = (bf16[1024,1024]{1,0:T(8,128)(2,1)}, bf16[1024,1024]{1,0:T(8,128)(2,1)}, bf16[1024,256]{1,0:T(8,128)(2,1)}, bf16[1024,1024]{1,0:T(8,128)(2,1)}, bf16[1...) custom-call(bf16[2304,1024]{1,0:T(8,128)(2,1)} %get-tuple-element.15.g_up.g_down.g_proj_a.g_proj_b, ...), custom_call_target="tpu_custom_call" | custom-call | tf_op jit(solution)/shard_map/lion/pallas_call | solution.py:746
  158.6 0.0 copy-done
  158.6 0.8 copy.22
Async XLA Ops:
  144.4 14.2 %copy-start = (f32[128,1024]{1,0:T(8,128)S(1)}, f32[128,1024]{1,0:T(8,128)}, u32[]{:S(2)}) copy-start(f32[128,1024]{1,0:T(8,128)} %get-tuple-element.36) | copy-start | bytes 1572868

commit v5 on v4

--- a/solution.py
+++ b/solution.py
@@ -134,9 +134,26 @@
 
 
 def step_kernel(
-    sharp, offset, caption, final, mapper, latent_in, second_in, entry_in, total_out, text_out, *scratch
+    sharp,
+    offset,
+    caption_in,
+    final_in,
+    mapper_in,
+    latent_in,
+    second_in,
+    entry_in,
+    total_out,
+    text_out,
+    *scratch,
 ):
     r = types.SimpleNamespace(**dict(zip(SCRATCH, scratch)))
+    caption, final, mapper = r.caption, r.final, r.own_mapper
+    early = [
+        pltpu.make_async_copy(src, dst, r.load.at[7 + k])
+        for k, (src, dst) in enumerate(((caption_in, caption), (mapper_in, mapper), (final_in, final)))
+    ]
+    for one in early:
+        one.start()
     net = Links(r.send, r.recv)
     hi, core = net.hi, net.core
     copy = net.copy
@@ -169,7 +186,7 @@
     for one in loads:
         one.start()
 
-    r.columns[...] = nn(final[...], mapper[...]).astype(BF16)
+    early[0].wait()
     raw = caption[...].astype(F32)
     text_scale = lax.rsqrt(jnp.sum(raw * raw, axis=1, keepdims=True) + 1e-06)
     unit = raw * text_scale
@@ -178,7 +195,10 @@
     unit = unit.astype(BF16)
     r.texts[0:64, :] = unit[0:64]
     r.texts[256:320, :] = unit[64:128]
+    early[1].wait()
     r.mapper[:, cols_of(hi, core)] = mapper[...]
+    early[2].wait()
+    r.columns[...] = nn(final[...], mapper[...]).astype(BF16)
     r.embed[:, cols_of(hi, core)] = r.columns[rows_of(hi, core), :]
     pl.semaphore_wait(barrier, len(partners))
 
@@ -230,6 +250,8 @@
     halves = (0, 1)
     text_first(1)
     text_second(0, 0)
+    text_first(0)
+    text_second(1, 0)
 
     for one in embed_copies:
         one.wait_recv()
@@ -248,8 +270,6 @@
     image_off = [image_copy(0, 3, x_off, 1)]
     image_on.append(image_copy(0, 1, x_on, 1))
     image_off.append(image_copy(0, 3, x_off, 0))
-    text_first(0)
-    text_second(1, 0)
     shared = [image_copy(0, 4, sibling)]
     r.image_scale[...] = image_scale
     r.image_unit[...] = unit
@@ -280,9 +300,6 @@
         one.wait_recv()
     shared.append(image_copy(2, 6, sibling))
 
-    for one in shared:
-        one.wait_recv()
-
     factor = sharp[0]
     shift = offset[0]
 
@@ -320,8 +337,11 @@
     def image_part(cols):
         r.image_dz[:, cols] = nn(r.weights[:, near_texts], r.texts[near_texts, cols])
 
-    pair_weights(0)
+    pair_weights(0, 0, 512)
     matching_pairs()
+    for one in shared:
+        one.wait_recv()
+    pair_weights(0, 512, 512)
     for p in (1, 3):
         for half in halves:
             arrived(half, 1, p)
@@ -495,10 +515,10 @@
     grad_rings[0, 0].start()
     down(1)
     grad_rings[1, 0].middle()
-    grad_rings[1, 1].start()
+    grad_rings[1, 1].start_far()
     up(1)
     grad_rings[0, 0].middle()
-    grad_rings[0, 1].start()
+    grad_rings[0, 1].start_far()
 
     def text_first_sum(half):
         seconds[half].arrive()
@@ -539,10 +559,12 @@
 
     wide_tile = (pl.ds(0, 128), pl.ds(128, 128))
     side(1, 0)
+    grad_rings[0, 1].start_near()
+    side(0, 0)
+    grad_rings[1, 1].start_near()
     grad_rings[1, 1].middle()
+    grad_rings[0, 1].middle()
     firsts[0].middle()
-    side(0, 0)
-    grad_rings[0, 1].middle()
 
     kept = cut(net.lo * TILE, TILE)
     given = cut((1 - net.lo) * TILE, TILE)
@@ -602,24 +624,24 @@
             last.append(copy(block, block, to))
 
     tile(1, 0)
+    tile(0, 0)
+    back_tile(1, 0)
     side(1, 1)
-    tile(0, 0)
+    back_tile(0, 0)
     side(0, 1)
-    back_tile(1, 0)
-    back_tile(0, 0)
+    back_side(1, 0)
+    back_side(0, 0)
     tile(1, 1)
-    back_side(1, 0)
     tile(0, 1)
-    back_side(0, 0)
+    back_strip(1, 0)
+    back_strip(0, 0)
     back_tile(1, 1)
     back_tile(0, 1)
-    back_strip(1, 0)
     back_side(1, 1)
-    back_strip(0, 0)
     back_side(0, 1)
-    text_first_sum(1)
     back_far(1, 0)
     back_far(0, 0)
+    text_first_sum(1)
     back_strip(1, 1)
     back_strip(0, 1)
     firsts[1].middle()
@@ -632,19 +654,23 @@
 
     back_far(1, 1)
     back_far(0, 1)
-    for chain in chains:
-        for one in spread_strip[chain][2:]:
+    outs = []
+    for n, (part, c) in enumerate(((1, 0), (0, 0), (1, 1), (0, 1))):
+        for one in spread_strip[part, c][2:] + last[2 * n : 2 * n + 2]:
             one.wait_recv()
-    for one in last:
-        one.wait_recv()
-    out = pltpu.make_async_copy(r.done, total_out, r.load.at[3])
-    out.start()
+        block = (pl.ds(part * PART, PART), wide[c])
+        outs.append(pltpu.make_async_copy(r.done.at[block], total_out.at[block], r.load.at[3 + n]))
+        outs[-1].start()
     for one in net.started:
         one.wait_send()
-    out.wait()
+    for one in outs:
+        one.wait()
 
 
 SCRATCH = dict(
+    caption=((128, 1024), BF16),
+    final=((512, 1024), BF16),
+    own_mapper=((1024, 256), BF16),
     columns=((512, 256), BF16),
     texts=((2048, 1024), BF16),
     text_unit=((128, 1024), F32),
@@ -687,7 +713,7 @@
     tile_in=((2, TILE, 256), BF16),
     send=((COPIES,), None),
     recv=((COPIES,), None),
-    load=((4,), None),
+    load=((10,), None),
 )
 
 
@@ -699,7 +725,7 @@
             jax.ShapeDtypeStruct((2 * PART, 1024), BF16),
             jax.ShapeDtypeStruct((128, 1024), F32),
         ),
-        in_specs=[SMEM, SMEM, VMEM, VMEM, VMEM, ANY, ANY, ANY],
+        in_specs=[SMEM, SMEM] + [ANY] * 6,
         out_specs=(ANY, VMEM),
         scratch_shapes=[
             pltpu.SemaphoreType.DMA(shape) if kind is None else pltpu.VMEM(shape, kind)
@@ -711,54 +737,146 @@
     )(sharp, offset, caption, final, mapper, latent, second, entry)
 
 
-def lion_block(weight, moment, grad, axis):
-    grad = grad.astype(F32)
-    moment = moment.astype(F32)
-    blend = 0.9 * moment + 0.1 * grad
-    square = blend * blend
-    floor = 0.0625 * (jnp.mean(square, axis=axis, keepdims=True) + 1e-06)
-    update = blend * lax.rsqrt(square + floor) + weight.astype(F32)
-    return update.astype(BF16), (0.99 * moment + 0.01 * grad).astype(BF16)
+LION = dict(
+    total=((2 * PART, 1024), BF16),
+    w_up=((1024, 1024), BF16),
+    w_down=((1024, 1024), BF16),
+    w_proj=((1024, 256), BF16),
+    m_up=((1024, 1024), BF16),
+    m_down=((1024, 1024), BF16),
+    m_proj=((1024, 256), BF16),
+)
+LION_CUTS = 1
+LION_OUT = ("u_up", "u_down", "u_proj", "r_up", "r_down", "r_proj")
+LION_JOBS = 2 * LION_CUTS + 1
 
 
 def lion_kernel(
-    g_up, g_down, g_proj_a, g_proj_b, w_up, w_down, w_proj, m_up, m_down, m_proj,
-    u_up, u_down, u_proj, r_up, r_down, r_proj,
+    total, text, w_up, w_down, w_proj, m_up, m_down, m_proj,
+    u_up, u_down, u_proj, r_up, r_down, r_proj, text_out, *scratch,
 ):
-    u_up[...], r_up[...] = lion_block(w_up[...], m_up[...], g_up[...], 0)
-    u_down[...], r_down[...] = lion_block(w_down[...], m_down[...], g_down[...], 1)
-
-    @pl.when(pl.program_id(0) == 0)
-    def _():
-        grad = jnp.concatenate(
-            [g[:, 256 * i : 256 * (i + 1)] for i in range(4) for g in (g_proj_a, g_proj_b)], axis=0
+    held = dict(zip(LION, scratch))
+    kept = dict(zip(LION_OUT, scratch[len(LION) :]))
+    arrive, leave = scratch[-2:]
+    given = dict(
+        total=total, w_up=w_up, w_down=w_down, w_proj=w_proj, m_up=m_up, m_down=m_down, m_proj=m_proj
+    )
+    results = dict(u_up=u_up, u_down=u_down, u_proj=u_proj, r_up=r_up, r_down=r_down, r_proj=r_proj)
+    size = 1024 // LION_CUTS
+    whole = slice(None)
+
+    def cuts(name, n):
+        if name == "down":
+            rows = pl.ds(n * size, size)
+            return (rows, whole), [(pl.ds(PART + n * size, size), whole)]
+        if name == "up":
+            cols = pl.ds(n * size, size)
+            return (whole, cols), [(pl.ds(0, 1024), cols)]
+        return (whole, whole), [(pl.ds(1024, 128), whole), (pl.ds(PART + 1024, 128), whole)]
+
+    jobs = [("down", n) for n in range(LION_CUTS)] + [("up", n) for n in range(LION_CUTS)]
+    jobs.insert(0, ("proj", 0))
+    loads = []
+    for k, (name, n) in enumerate(jobs):
+        at, grads = cuts(name, n)
+        mine = [("w_" + name, at), ("m_" + name, at)] + [("total", one) for one in grads]
+        loads.append(
+            [
+                pltpu.make_async_copy(given[key].at[part], held[key].at[part], arrive.at[k, i])
+                for i, (key, part) in enumerate(mine)
+            ]
         )
-        u_proj[...], r_proj[...] = lion_block(w_proj[...], m_proj[...], grad, 0)
-
-
-def lion(total, weights, moments):
-    column = pl.BlockSpec((1024, 128), lambda i: (0, i))
-    row = pl.BlockSpec((128, 1024), lambda i: (i, 0))
-    whole = pl.BlockSpec((1024, 256), lambda i: (0, 0))
-    like = [column, row, whole]
+    fetched = pltpu.make_async_copy(text, scratch[-3], leave.at[LION_JOBS, 0])
+    passed = pltpu.make_async_copy(scratch[-3], text_out, leave.at[LION_JOBS, 1])
+    for one in loads[0] + loads[1] + [fetched]:
+        one.start()
+    for job in loads[2:]:
+        for one in job:
+            one.start()
+
+    def blend(m, g):
+        return 0.9 * m + 0.1 * g
+
+    def finish(name, at, m, g, mix, floor):
+        w = held["w_" + name][at].astype(F32)
+        kept["u_" + name][at] = (mix * lax.rsqrt(mix * mix + floor) + w).astype(BF16)
+        kept["r_" + name][at] = (0.99 * m + 0.01 * g).astype(BF16)
+
+    def column_job(name, cols, width, grad, count):
+        def read(j):
+            at = (cut(j * 128, 128, 128), cols)
+            g = grad(j)
+            m = held["m_" + name][at].astype(F32)
+            return at, m, g, blend(m, g)
+
+        def add(j, acc):
+            mix = read(j)[3]
+            return acc + jnp.sum((mix * mix).reshape(16, 8, width), axis=0)
+
+        acc = lax.fori_loop(0, count, add, jnp.zeros((8, width), F32), unroll=True)
+        floor = 0.0625 * (jnp.sum(acc, axis=0, keepdims=True) * (1.0 / 1024) + 1e-06)
+
+        def write(j, _):
+            at, m, g, mix = read(j)
+            finish(name, at, m, g, mix, floor)
+            return 0
+
+        lax.fori_loop(0, count, write, 0, unroll=True)
+
+    stores = []
+    for k, (name, n) in enumerate(jobs):
+        for one in loads[k]:
+            one.wait()
+        at = cuts(name, n)[0]
+        if name == "down":
+
+            def rows(j, _):
+                here = cut(n * size + j * 32, 32, 32)
+                there = cut(PART + n * size + j * 32, 32, 32)
+                m = held["m_down"][here, :].astype(F32)
+                g = held["total"][there, :].astype(F32)
+                mix = blend(m, g)
+                floor = 0.0625 * (jnp.mean(mix * mix, axis=1, keepdims=True) + 1e-06)
+                finish("down", (here, whole), m, g, mix, floor)
+                return 0
+
+            lax.fori_loop(0, size // 32, rows, 0, unroll=True)
+        elif name == "up":
+            cols = pl.ds(n * size, size)
+            column_job("up", cols, size, lambda j: held["total"][cut(j * 128, 128, 128), cols].astype(F32), 8)
+        else:
+            def grad(j):
+                rows = cut(1024 + (j % 2) * PART, 128, 128)
+                return held["total"][rows, cut((j // 2) * 256, 256, 256)].astype(F32)
+
+            column_job("proj", pl.ds(0, 256), 256, grad, 8)
+        for i, key in enumerate(("u_" + name, "r_" + name)):
+            stores.append(pltpu.make_async_copy(kept[key].at[at], results[key].at[at], leave.at[k, i]))
+            stores[-1].start()
+        if k == 1:
+            fetched.wait()
+            passed.start()
+    for one in stores:
+        one.wait()
+    passed.wait()
+
+
+def lion(total, text, weights, moments):
     square = jax.ShapeDtypeStruct((1024, 1024), BF16)
     narrow = jax.ShapeDtypeStruct((1024, 256), BF16)
+    outs = (square, square, narrow, square, square, narrow)
     return pl.pallas_call(
         lion_kernel,
         name="lion",
-        grid=(8,),
-        out_shape=(square, square, narrow, square, square, narrow),
-        in_specs=[
-            column,
-            pl.BlockSpec((128, 1024), lambda i: (9 + i, 0)),
-            pl.BlockSpec((128, 1024), lambda i: (8, 0)),
-            pl.BlockSpec((128, 1024), lambda i: (17, 0)),
-        ]
-        + like
-        + like,
-        out_specs=tuple(like + like),
+        out_shape=(*outs, jax.ShapeDtypeStruct(text.shape, F32)),
+        in_specs=[ANY] * 8,
+        out_specs=(ANY,) * 7,
+        scratch_shapes=[pltpu.VMEM(*one) for one in LION.values()]
+        + [pltpu.VMEM(one.shape, BF16) for one in outs]
+        + [pltpu.VMEM(text.shape, F32)]
+        + [pltpu.SemaphoreType.DMA((LION_JOBS, 4)), pltpu.SemaphoreType.DMA((LION_JOBS + 1, 2))],
         compiler_params=pltpu.CompilerParams(vmem_limit_bytes=60 * 2**20),
-    )(total, total, total, total, *weights, *moments)
+    )(total, text, *weights, *moments)
 
 
 def per_device(
@@ -785,12 +903,12 @@
         second_feedforward_matrix,
         vision_layer_entry,
     )
-    results = lion(
+    return lion(
         total,
+        text_grad,
         (first_feedforward_matrix, second_feedforward_matrix, mapper_matrix),
         (first_matrix_velocity, second_matrix_velocity, mapper_velocity),
     )
-    return (*results, text_grad)
 
 
 def solution(mesh):

time: 160 us -> 151 us (0.944)
  Pallas kernels: 157 us -> 149 us
    pallas_call x1, Pallas kernels: 142 us -> 138 us  [step(): pl.pallas_call(step_kernel, name='pairs_and_weight_grads', out_shape=(jax...]
    pallas_call x1, Pallas kernels: 14.2 us -> 11.2 us  [lion(): pl.pallas_call(lion_kernel, name='lion', out_shape=(*outs, jax.ShapeDtype...]
where the time goes in v5:
time: 151 us
  Pallas kernels  149 us (99%)
  between operations  2.11 us (1%)
    pallas_call x1, Pallas kernels, step(): pl.pallas_call(step_kernel, name='pairs_and_weight_grads', out_shape=(jax...  138 us
    pallas_call x1, Pallas kernels, lion(): pl.pallas_call(lion_kernel, name='lion', out_shape=(*outs, jax.ShapeDtype...  11.2 us

profile of v5, /device:TPU:0, one launch (start us, length us, event | category | flops | bytes accessed | tf_op | source)
XLA Modules:
  0.0 151.2 jit_solution(5775910364092570594)
XLA Ops:
  1.9 137.9 %pairs_and_weight_grads.1 = (bf16[2304,1024]{1,0:T(8,128)(2,1)}, f32[128,1024]{1,0:T(8,128)}) custom-call(f32[1]{0:T(128)S(6)} %copy.19.sharp, f32[1]{0:T(128)S(6)} %copy.20.offset, bf16[128,1024]{1,0:T(8,128)(2,1)} %caption_in.1, bf16[512,1024]{1,0:T(8,128)(2,1)} %final_in.1, bf16[1024,256]{1,0:T(8,128)(2,1)} %w_proj.1, bf16[512,1024]{1,0:T(8,128)(2,1)} %latent_in.1, ...), custom_call_target="tpu_custom_call" | custom-call | tf_op jit(solution)/shard_map/pairs_and_weight_grads/pallas_call | solution.py:721
  139.8 11.2 %lion.1 = (bf16[1024,1024]{1,0:T(8,128)(2,1)}, bf16[1024,1024]{1,0:T(8,128)(2,1)}, bf16[1024,256]{1,0:T(8,128)(2,1)}, bf16[1024,1024]{1,0:T(8,128)(2,1)}, bf16[1...) custom-call(bf16[2304,1024]{1,0:T(8,128)(2,1)} %get-tuple-element.9.total, ...), custom_call_target="tpu_custom_call" | custom-call | tf_op jit(solution)/shard_map/lion/pallas_call | solution.py:868

commit v6 on v5

--- a/solution.py
+++ b/solution.py
@@ -17,7 +17,7 @@
 PART = 1152
 STRIP = 288
 TILE = 144
-COPIES = 176
+COPIES = 200
 PLACE = (0, 1, 3, 2)
 
 
@@ -71,6 +71,7 @@
 
     def copy(self, src, dst, to):
         k = len(self.started)
+        assert k < COPIES
         one = pltpu.make_async_remote_copy(
             src_ref=src,
             dst_ref=dst,
@@ -278,24 +279,34 @@
         arrived(half, 0, 1)
         arrived(half, 0, 3)
         text_far_first(half)
+    for half in (0, 1):
         text_second(half, 1)
         text_second(half, 3)
-        if half == 1:
-            image_on[0].wait_recv()
-            image_far = [image_copy(1, 2, x_on, 0)]
-            image_off[0].wait_recv()
-            image_far.append(image_copy(3, 2, x_off, 1))
-
-    for half in (0, 1):
-        arrived(half, 1, 0)
-        arrived(half, 3, 0)
-        text_far_second(half, 0)
+    arrived(0, 1, 0)
+    arrived(0, 3, 0)
+    text_far_second(0, 0)
+    image_on[0].wait_recv()
+    image_far = [image_copy(1, 2, x_on, 0)]
+    image_off[0].wait_recv()
+    image_far.append(image_copy(3, 2, x_off, 1))
+    for half in (1, 0):
+        arrived(half, 0, 2)
+        text_second(half, 2)
+    arrived(1, 1, 0)
+    arrived(1, 3, 0)
+    text_far_second(1, 0)
     image_on[1].wait_recv()
     image_off[1].wait_recv()
     shared += [image_copy(1, 5, sibling), image_copy(3, 7, sibling)]
-    for half in (1, 0):
-        arrived(half, 0, 2)
-        text_second(half, 2)
+
+    loads[0].wait()
+
+    def activate(cols):
+        value, derivative = gelu_parts(r.latent[:, cols].astype(F32))
+        r.active[:, cols] = value.astype(BF16)
+        r.slope[:, cols] = derivative
+
+    loop(4, activate)
     for one in image_far:
         one.wait_recv()
     shared.append(image_copy(2, 6, sibling))
@@ -339,22 +350,17 @@
 
     pair_weights(0, 0, 512)
     matching_pairs()
+    for p in (1, 3):
+        arrived(0, 1, p)
+        arrived(0, 3, p)
+        text_far_second(0, p)
     for one in shared:
         one.wait_recv()
     pair_weights(0, 512, 512)
     for p in (1, 3):
-        for half in halves:
-            arrived(half, 1, p)
-            arrived(half, 3, p)
-            text_far_second(half, p)
-    loads[0].wait()
-
-    def activate(cols):
-        value, derivative = gelu_parts(r.latent[:, cols].astype(F32))
-        r.active[:, cols] = value.astype(BF16)
-        r.slope[:, cols] = derivative
-
-    loop(4, activate)
+        arrived(1, 1, p)
+        arrived(1, 3, p)
+        text_far_second(1, p)
     for half in halves:
         arrived(half, 1, 2)
         arrived(half, 3, 2)
@@ -383,20 +389,24 @@
     loop(2, last_own, 512)
     cross.wait_recv()
 
-    def image_block(k, i):
-        return image_slot((4 - k) % 4, i), slice(None)
-
-    image_ring = RingSum(net, r.image_sum, image_block, r.image_far, r.image_near, x_on, x_off)
+    def image_ring(n):
+        def block(k, i):
+            return pl.ds(((4 - k) % 4) * 128 + n * 64 + i * 32, 32), slice(None)
+
+        return RingSum(net, r.image_sum, block, r.image_far.at[n], r.image_near.at[n], x_on, x_off)
+
+    image_rings = [image_ring(n) for n in (0, 1)]
 
     def image_total(s):
         rows = image_slot(s)
         r.image_sum[rows, :] = (r.image_dz[rows, :] + r.cross_in[rows, :].astype(F32)).astype(BF16)
 
     image_total(2)
-    image_ring.start_far()
+    image_rings[0].start_far()
     image_total(1)
     image_total(3)
-    image_ring.start_near()
+    image_rings[0].start_near()
+    image_rings[1].start_far()
     image_total(0)
 
     def text_grads(half, *groups):
@@ -421,20 +431,32 @@
     seconds = [second_ring(half) for half in halves]
     firsts = [first_ring(half) for half in halves]
 
+    across_copies, beside_copies = [], []
+
+    def image_finish(n):
+        ring = image_rings[n]
+        ring.arrive()
+        rows = pl.ds(n * 64, 64)
+        dz = jnp.concatenate([ring.total(0), ring.total(1)], axis=0)
+        unit = r.image_unit[rows, :]
+        grad = r.image_scale[rows, :] * (dz - unit * jnp.sum(unit * dz, axis=1, keepdims=True))
+        mine = cut(quarter * 128 + n * 64, 64, 64)
+        r.image_grad[mine, :] = grad.astype(BF16)
+        block = r.image_grad.at[mine]
+        across_copies.append(copy(block, block, across))
+        beside_copies.append(copy(block, block, sibling))
+
     text_grads(0, 2, 1, 3)
     seconds[0].start()
     text_grads(1, 2)
-    image_ring.middle()
-    text_grads(1, 1, 3)
+    image_rings[0].middle()
+    image_rings[1].start_near()
+    text_grads(1, 1)
+    image_rings[1].middle()
+    text_grads(1, 3)
+    image_finish(0)
     text_grads(0, 0)
-    image_ring.arrive()
-    dz = jnp.concatenate([image_ring.total(0), image_ring.total(1)], axis=0)
-    unit = r.image_unit[...]
-    grad = r.image_scale[...] * (dz - unit * jnp.sum(unit * dz, axis=1, keepdims=True))
-    mine = rows_of(hi, core)
-    r.image_grad[mine, :] = grad.astype(BF16)
-    block = r.image_grad.at[mine]
-    spread = [copy(block, block, across), copy(block, block, sibling)]
+    image_finish(1)
     text_grads(1, 0)
 
     map_copies[0].wait_recv()
@@ -443,7 +465,8 @@
     seconds[0].middle()
     map_copies[1].wait_recv()
     map_copies[2].wait_recv()
-    spread[1].wait_recv()
+    for one in beside_copies:
+        one.wait_recv()
 
     def back_rows(h):
         rows = cut((h % 2) * 256, 256, 256)
@@ -454,11 +477,25 @@
         loop(2, part, 512)
 
     back_rows(hi)
-    spread[0].wait_recv()
-    block = r.image_grad.at[rows_of(hi + 1, core)]
-    spread.append(copy(block, block, sibling))
+    here, there = cut(hi * 256, 256, 256), cut((1 - hi) * 256, 256, 256)
+    own_cols = cols_of(hi, core)
+
+    def proj_here(cols):
+        r.image_dz[cols, 512:768] = tn(final[here, cols], r.image_grad[here, own_cols])
+
+    def down_here(cols):
+        r.image_dz[cols, 0:512] = tn(r.active[here, cols], r.back[here, 0:512])
+
+    loop(2, proj_here, 512)
+    loop(2, down_here, 512)
+    passed = []
+    for n in (0, 1):
+        across_copies[n].wait_recv()
+        block = r.image_grad.at[cut(((1 - hi) * 2 + core) * 128 + n * 64, 64, 64)]
+        passed.append(copy(block, block, sibling))
     seconds[1].start()
-    spread[2].wait_recv()
+    for one in passed:
+        one.wait_recv()
     back_rows(hi + 1)
 
     first = (net.z, net.x)
@@ -484,14 +521,18 @@
     grad_rings = {chain: grad_ring(*chain) for chain in chains}
 
     def proj_part(cols):
-        value = tn(final[:, cols], r.image_grad[:, cols_of(hi, core)]).astype(BF16)
+        value = tn(final[there, cols], r.image_grad[there, own_cols])
+        value = (value + r.image_dz[cols, 512:768]).astype(BF16)
         r.grads[1024:1152, cols] = value[0:128]
         r.grads[2176:2304, cols] = value[128:256]
 
     def down(c):
         def part(j, _):
             cols = cut(j * 512, 512, 512)
-            value = tn(r.active[:, cols], r.back[:, wide[c]])
+            if c == 0:
+                value = tn(r.active[there, cols], r.back[there, wide[c]]) + r.image_dz[cols, 0:512]
+            else:
+                value = tn(r.active[:, cols], r.back[:, wide[c]])
             r.grads[cut(PART + j * 512, 512, 128), wide[c]] = value.astype(BF16)
             return 0
 
@@ -626,11 +667,13 @@
     tile(1, 0)
     tile(0, 0)
     back_tile(1, 0)
+    text_first_sum(1)
     side(1, 1)
     back_tile(0, 0)
     side(0, 1)
     back_side(1, 0)
     back_side(0, 0)
+    firsts[1].middle()
     tile(1, 1)
     tile(0, 1)
     back_strip(1, 0)
@@ -641,10 +684,8 @@
     back_side(0, 1)
     back_far(1, 0)
     back_far(0, 0)
-    text_first_sum(1)
     back_strip(1, 1)
     back_strip(0, 1)
-    firsts[1].middle()
 
     for half in halves:
         firsts[half].arrive()
@@ -690,8 +731,8 @@
     cross_out=((512, 1024), BF16),
     cross_in=((512, 1024), BF16),
     image_sum=((512, 1024), BF16),
-    image_far=((2, 64, 1024), BF16),
-    image_near=((2, 128, 1024), BF16),
+    image_far=((2, 2, 32, 1024), BF16),
+    image_near=((2, 2, 64, 1024), BF16),
     text_dz=((2048, 1024), BF16),
     text_far=((2, 2, 128, 1024), BF16),
     text_near=((2, 2, 256, 1024), BF16),

time: 151 us -> 139 us (0.921)
  Pallas kernels: 149 us -> 137 us
    pallas_call x1, Pallas kernels: 138 us -> 126 us  [step(): pl.pallas_call(step_kernel, name='pairs_and_weight_grads', out_shape=(jax...]
where the time goes in v6:
time: 139 us
  Pallas kernels  137 us (99%)
  between operations  2.09 us (2%)
    pallas_call x1, Pallas kernels, step(): pl.pallas_call(step_kernel, name='pairs_and_weight_grads', out_shape=(jax...  126 us
    pallas_call x1, Pallas kernels, lion(): pl.pallas_call(lion_kernel, name='lion', out_shape=(*outs, jax.ShapeDtype...  11.2 us

profile of v6, /device:TPU:0, one launch (start us, length us, event | category | flops | bytes accessed | tf_op | source)
XLA Modules:
  0.0 139.3 jit_solution(9595720562133436224)
XLA Ops:
  1.9 126.1 %pairs_and_weight_grads.1 = (bf16[2304,1024]{1,0:T(8,128)(2,1)}, f32[128,1024]{1,0:T(8,128)}) custom-call(f32[1]{0:T(128)S(6)} %copy.19.sharp, f32[1]{0:T(128)S(6)} %copy.20.offset, bf16[128,1024]{1,0:T(8,128)(2,1)} %caption_in.1, bf16[512,1024]{1,0:T(8,128)(2,1)} %final_in.1, bf16[1024,256]{1,0:T(8,128)(2,1)} %w_proj.1, bf16[512,1024]{1,0:T(8,128)(2,1)} %latent_in.1, ...), custom_call_target="tpu_custom_call" | custom-call | tf_op jit(solution)/shard_map/pairs_and_weight_grads/pallas_call | solution.py:762
  128.0 11.2 %lion.1 = (bf16[1024,1024]{1,0:T(8,128)(2,1)}, bf16[1024,1024]{1,0:T(8,128)(2,1)}, bf16[1024,256]{1,0:T(8,128)(2,1)}, bf16[1024,1024]{1,0:T(8,128)(2,1)}, bf16[1...) custom-call(bf16[2304,1024]{1,0:T(8,128)(2,1)} %get-tuple-element.9.total, ...), custom_call_target="tpu_custom_call" | custom-call | tf_op jit(solution)/shard_map/lion/pallas_call | solution.py:909

commit v7 on v6

--- a/solution.py
+++ b/solution.py
@@ -63,6 +63,7 @@
         self.y = self.hi * 2 + self.lo
         self.send, self.recv = send, recv
         self.started = []
+        self.sent = 0
 
     def at(self, z=0, x=0, y=0, core=0):
         row = (self.y + y) % 4
@@ -83,6 +84,12 @@
         one.start()
         self.started.append(one)
         return one
+
+    def all_sent(self, until=None):
+        until = len(self.started) if until is None else until
+        for one in self.started[self.sent : until]:
+            one.wait_send()
+        self.sent = until
 
 
 class RingSum:
@@ -369,7 +376,7 @@
     pair_weights(3)
     own_columns = r.mapper.at[:, cols_of(hi, core)]
     map_copies = [copy(own_columns, own_columns, beside), copy(own_columns, own_columns, sibling)]
-    loop(4, image_part)
+    loop(2, image_part, 512)
     for p in range(4):
         for half in halves:
             arrived(half, 2, p)
@@ -498,9 +505,9 @@
         one.wait_recv()
     back_rows(hi + 1)
 
-    first = (net.z, net.x)
-    other = (net.x, net.z)
-    along = ((z_on, z_off), (x_on, x_off))
+    first = (net.x, net.z)
+    other = (net.z, net.x)
+    along = ((x_on, x_off), (z_on, z_off))
     wide = (pl.ds(0, 512), pl.ds(512, 512))
 
     def strip_rows(part, k, i=None):
@@ -571,7 +578,7 @@
     text_first_sum(0)
 
     def side_to(part, k):
-        return net.at(x=k) if part == 0 else net.at(z=k)
+        return net.at(z=k) if part == 0 else net.at(x=k)
 
     sides = {}
 
@@ -676,6 +683,7 @@
     firsts[1].middle()
     tile(1, 1)
     tile(0, 1)
+    before = len(net.started)
     back_strip(1, 0)
     back_strip(0, 0)
     back_tile(1, 1)
@@ -693,6 +701,7 @@
     unit = r.text_unit[...]
     text_out[...] = r.text_scale[...] * (dz - unit * jnp.sum(unit * dz, axis=1, keepdims=True))
 
+    net.all_sent(before)
     back_far(1, 1)
     back_far(0, 1)
     outs = []
@@ -702,8 +711,7 @@
         block = (pl.ds(part * PART, PART), wide[c])
         outs.append(pltpu.make_async_copy(r.done.at[block], total_out.at[block], r.load.at[3 + n]))
         outs[-1].start()
-    for one in net.started:
-        one.wait_send()
+    net.all_sent()
     for one in outs:
         one.wait()
 
@@ -787,9 +795,7 @@
     m_down=((1024, 1024), BF16),
     m_proj=((1024, 256), BF16),
 )
-LION_CUTS = 1
 LION_OUT = ("u_up", "u_down", "u_proj", "r_up", "r_down", "r_proj")
-LION_JOBS = 2 * LION_CUTS + 1
 
 
 def lion_kernel(
@@ -803,32 +809,26 @@
         total=total, w_up=w_up, w_down=w_down, w_proj=w_proj, m_up=m_up, m_down=m_down, m_proj=m_proj
     )
     results = dict(u_up=u_up, u_down=u_down, u_proj=u_proj, r_up=r_up, r_down=r_down, r_proj=r_proj)
-    size = 1024 // LION_CUTS
     whole = slice(None)
 
-    def cuts(name, n):
-        if name == "down":
-            rows = pl.ds(n * size, size)
-            return (rows, whole), [(pl.ds(PART + n * size, size), whole)]
-        if name == "up":
-            cols = pl.ds(n * size, size)
-            return (whole, cols), [(pl.ds(0, 1024), cols)]
-        return (whole, whole), [(pl.ds(1024, 128), whole), (pl.ds(PART + 1024, 128), whole)]
-
-    jobs = [("down", n) for n in range(LION_CUTS)] + [("up", n) for n in range(LION_CUTS)]
-    jobs.insert(0, ("proj", 0))
+    grads = dict(
+        down=[(pl.ds(PART, 1024), whole)],
+        up=[(pl.ds(0, 1024), whole)],
+        proj=[(pl.ds(1024, 128), whole), (pl.ds(PART + 1024, 128), whole)],
+    )
+    jobs = ("proj", "down", "up")
     loads = []
-    for k, (name, n) in enumerate(jobs):
-        at, grads = cuts(name, n)
-        mine = [("w_" + name, at), ("m_" + name, at)] + [("total", one) for one in grads]
+    for k, name in enumerate(jobs):
+        mine = [("w_" + name, (whole, whole)), ("m_" + name, (whole, whole))]
+        mine += [("total", one) for one in grads[name]]
         loads.append(
             [
                 pltpu.make_async_copy(given[key].at[part], held[key].at[part], arrive.at[k, i])
                 for i, (key, part) in enumerate(mine)
             ]
         )
-    fetched = pltpu.make_async_copy(text, scratch[-3], leave.at[LION_JOBS, 0])
-    passed = pltpu.make_async_copy(scratch[-3], text_out, leave.at[LION_JOBS, 1])
+    fetched = pltpu.make_async_copy(text, scratch[-3], leave.at[3, 0])
+    passed = pltpu.make_async_copy(scratch[-3], text_out, leave.at[3, 1])
     for one in loads[0] + loads[1] + [fetched]:
         one.start()
     for job in loads[2:]:
@@ -857,46 +857,55 @@
         acc = lax.fori_loop(0, count, add, jnp.zeros((8, width), F32), unroll=True)
         floor = 0.0625 * (jnp.sum(acc, axis=0, keepdims=True) * (1.0 / 1024) + 1e-06)
 
-        def write(j, _):
+        for j in range(count):
             at, m, g, mix = read(j)
             finish(name, at, m, g, mix, floor)
-            return 0
-
-        lax.fori_loop(0, count, write, 0, unroll=True)
 
     stores = []
-    for k, (name, n) in enumerate(jobs):
+
+    def send(name, quarter=None):
+        n = LION_OUT.index("u_" + name)
+        at = (whole, whole) if quarter is None else (pl.ds(quarter * 256, 256), whole)
+        if name == "up":
+            at = at[::-1]
+        for i, key in enumerate(("u_" + name, "r_" + name)):
+            sem = leave.at[n, 2 * (quarter or 0) + i]
+            stores.append(pltpu.make_async_copy(kept[key].at[at], results[key].at[at], sem))
+            stores[-1].start()
+
+    for k, name in enumerate(jobs):
         for one in loads[k]:
             one.wait()
-        at = cuts(name, n)[0]
         if name == "down":
 
             def rows(j, _):
-                here = cut(n * size + j * 32, 32, 32)
-                there = cut(PART + n * size + j * 32, 32, 32)
+                here = cut(j * 32, 32, 32)
                 m = held["m_down"][here, :].astype(F32)
-                g = held["total"][there, :].astype(F32)
+                g = held["total"][cut(PART + j * 32, 32, 32), :].astype(F32)
                 mix = blend(m, g)
                 floor = 0.0625 * (jnp.mean(mix * mix, axis=1, keepdims=True) + 1e-06)
                 finish("down", (here, whole), m, g, mix, floor)
                 return 0
 
-            lax.fori_loop(0, size // 32, rows, 0, unroll=True)
+            for quarter in range(4):
+                lax.fori_loop(quarter * 8, quarter * 8 + 8, rows, 0, unroll=True)
+                send("down", quarter)
+            fetched.wait()
+            passed.start()
         elif name == "up":
-            cols = pl.ds(n * size, size)
-            column_job("up", cols, size, lambda j: held["total"][cut(j * 128, 128, 128), cols].astype(F32), 8)
+            for quarter in range(4):
+                cols = pl.ds(quarter * 256, 256)
+                column_job(
+                    "up", cols, 256, lambda j: held["total"][cut(j * 128, 128, 128), cols].astype(F32), 8
+                )
+                send("up", quarter)
         else:
             def grad(j):
                 rows = cut(1024 + (j % 2) * PART, 128, 128)
                 return held["total"][rows, cut((j // 2) * 256, 256, 256)].astype(F32)
 
             column_job("proj", pl.ds(0, 256), 256, grad, 8)
-        for i, key in enumerate(("u_" + name, "r_" + name)):
-            stores.append(pltpu.make_async_copy(kept[key].at[at], results[key].at[at], leave.at[k, i]))
-            stores[-1].start()
-        if k == 1:
-            fetched.wait()
-            passed.start()
+            send("proj")
     for one in stores:
         one.wait()
     passed.wait()
@@ -915,7 +924,7 @@
         scratch_shapes=[pltpu.VMEM(*one) for one in LION.values()]
         + [pltpu.VMEM(one.shape, BF16) for one in outs]
         + [pltpu.VMEM(text.shape, F32)]
-        + [pltpu.SemaphoreType.DMA((LION_JOBS, 4)), pltpu.SemaphoreType.DMA((LION_JOBS + 1, 2))],
+        + [pltpu.SemaphoreType.DMA((3, 4)), pltpu.SemaphoreType.DMA((4, 8))],
         compiler_params=pltpu.CompilerParams(vmem_limit_bytes=60 * 2**20),
     )(total, text, *weights, *moments)
 

time: 139 us -> 138 us (level)
  no operation moved by 1% of the time
where the time goes in v7:
time: 138 us
  Pallas kernels  136 us (99%)
  between operations  2.09 us (2%)
    pallas_call x1, Pallas kernels, step(): pl.pallas_call(step_kernel, name='pairs_and_weight_grads', out_shape=(jax...  125 us
    pallas_call x1, Pallas kernels, lion(): pl.pallas_call(lion_kernel, name='lion', out_shape=(*outs, jax.ShapeDtype...  10.9 us

profile of v7, /device:TPU:0, one launch (start us, length us, event | category | flops | bytes accessed | tf_op | source)
XLA Modules:
  0.0 138.2 jit_solution(13862534832742961484)
XLA Ops:
  1.9 125.2 %pairs_and_weight_grads.1 = (bf16[2304,1024]{1,0:T(8,128)(2,1)}, f32[128,1024]{1,0:T(8,128)}) custom-call(f32[1]{0:T(128)S(6)} %copy.19.sharp, f32[1]{0:T(128)S(6)} %copy.20.offset, bf16[128,1024]{1,0:T(8,128)(2,1)} %caption_in.1, bf16[512,1024]{1,0:T(8,128)(2,1)} %final_in.1, bf16[1024,256]{1,0:T(8,128)(2,1)} %w_proj.1, bf16[512,1024]{1,0:T(8,128)(2,1)} %latent_in.1, ...), custom_call_target="tpu_custom_call" | custom-call | tf_op jit(solution)/shard_map/pairs_and_weight_grads/pallas_call | solution.py:770
  127.2 10.9 %lion.1 = (bf16[1024,1024]{1,0:T(8,128)(2,1)}, bf16[1024,1024]{1,0:T(8,128)(2,1)}, bf16[1024,256]{1,0:T(8,128)(2,1)}, bf16[1024,1024]{1,0:T(8,128)(2,1)}, bf16[1...) custom-call(bf16[2304,1024]{1,0:T(8,128)(2,1)} %get-tuple-element.9.total, ...), custom_call_target="tpu_custom_call" | custom-call | tf_op jit(solution)/shard_map/lion/pallas_call | solution.py:918

commit v8 on v7

--- a/solution.py
+++ b/solution.py
@@ -321,8 +321,8 @@
     factor = sharp[0]
     shift = offset[0]
 
-    def pair_weights(s, first=0, count=1024):
-        texts = pl.ds(PLACE[s] * 512, 512)
+    def pair_weights(s, first=0, count=1024, width=512):
+        texts = pl.ds(PLACE[s] * 512, width)
 
         def chunk(rows):
             logits = factor * nt(r.images[rows, :], r.texts[texts, :]) + shift
@@ -372,8 +372,7 @@
         arrived(half, 1, 2)
         arrived(half, 3, 2)
         text_far_second(half, 2)
-    pair_weights(1)
-    pair_weights(3)
+    pair_weights(1, width=1024)
     own_columns = r.mapper.at[:, cols_of(hi, core)]
     map_copies = [copy(own_columns, own_columns, beside), copy(own_columns, own_columns, sibling)]
     loop(2, image_part, 512)
@@ -705,12 +704,28 @@
     back_far(1, 1)
     back_far(0, 1)
     outs = []
-    for n, (part, c) in enumerate(((1, 0), (0, 0), (1, 1), (0, 1))):
-        for one in spread_strip[part, c][2:] + last[2 * n : 2 * n + 2]:
+
+    def leave(rows, c):
+        block = (rows, wide[c])
+        outs.append(pltpu.make_async_copy(r.done.at[block], total_out.at[block], r.load.at[10 + len(outs)]))
+        outs[-1].start()
+
+    ends = ((1, 0), (0, 0), (1, 1), (0, 1))
+    for n, (part, c) in enumerate(ends):
+        for one in spread_strip[part, c][2:]:
             one.wait_recv()
-        block = (pl.ds(part * PART, PART), wide[c])
-        outs.append(pltpu.make_async_copy(r.done.at[block], total_out.at[block], r.load.at[3 + n]))
-        outs[-1].start()
+        if c == 0:
+            for one in last[2 * n : 2 * n + 2]:
+                one.wait_recv()
+            leave(pl.ds(part * PART, PART), c)
+        else:
+            for k in (0, 1, 3):
+                leave(strip_rows(part, k), c)
+    for n, (part, c) in enumerate(ends):
+        if c:
+            for one in last[2 * n : 2 * n + 2]:
+                one.wait_recv()
+            leave(strip_rows(part, 2), c)
     net.all_sent()
     for one in outs:
         one.wait()
@@ -762,7 +777,7 @@
     tile_in=((2, TILE, 256), BF16),
     send=((COPIES,), None),
     recv=((COPIES,), None),
-    load=((10,), None),
+    load=((20,), None),
 )
 
 

time: 138 us -> 138 us (level)
  no operation moved by 1% of the time
where the time goes in v8:
time: 138 us
  Pallas kernels  136 us (99%)
  between operations  2.09 us (2%)
    pallas_call x1, Pallas kernels, step(): pl.pallas_call(step_kernel, name='pairs_and_weight_grads', out_shape=(jax...  125 us
    pallas_call x1, Pallas kernels, lion(): pl.pallas_call(lion_kernel, name='lion', out_shape=(*outs, jax.ShapeDtype...  10.9 us

profile of v8, /device:TPU:0, one launch (start us, length us, event | category | flops | bytes accessed | tf_op | source)
XLA Modules:
  0.0 137.6 jit_solution(18293581045060173331)
XLA Ops:
  1.9 124.6 %pairs_and_weight_grads.1 = (bf16[2304,1024]{1,0:T(8,128)(2,1)}, f32[128,1024]{1,0:T(8,128)}) custom-call(f32[1]{0:T(128)S(6)} %copy.19.sharp, f32[1]{0:T(128)S(6)} %copy.20.offset, bf16[128,1024]{1,0:T(8,128)(2,1)} %caption_in.1, bf16[512,1024]{1,0:T(8,128)(2,1)} %final_in.1, bf16[1024,256]{1,0:T(8,128)(2,1)} %w_proj.1, bf16[512,1024]{1,0:T(8,128)(2,1)} %latent_in.1, ...), custom_call_target="tpu_custom_call" | custom-call | tf_op jit(solution)/shard_map/pairs_and_weight_grads/pallas_call | solution.py:785
  126.6 10.9 %lion.1 = (bf16[1024,1024]{1,0:T(8,128)(2,1)}, bf16[1024,1024]{1,0:T(8,128)(2,1)}, bf16[1024,256]{1,0:T(8,128)(2,1)}, bf16[1024,1024]{1,0:T(8,128)(2,1)}, bf16[1...) custom-call(bf16[2304,1024]{1,0:T(8,128)(2,1)} %get-tuple-element.9.total, ...), custom_call_target="tpu_custom_call" | custom-call | tf_op jit(solution)/shard_map/lion/pallas_call | solution.py:933
